TPU v7x, 512 devices: a whole 4x8x8 slice. The times are simulated.
512 devices in a mesh: dp: 16 (over y, core), expert: 32 (over z, x).
Axes of the slice: x: 4, y: 8, z: 8, core: 2. Of those that a mesh axis runs over, the one named last changes fastest.
Arguments:
- tokens: bfloat16 [2048, 3584], P('expert', 'dp'), may hold values from -6 to 6
- expert_ids: int32 [2048, 8], P('expert'), may hold values from 0 to 31, as said below
- gate_weights: float32 [2048, 8], P('expert'), may hold values from 0.1 to 1
- w_gate: bfloat16 [32, 3584, 1024], P('expert', 'dp'), may hold values from -0.09375 to 0.09375
- w_up: bfloat16 [32, 3584, 1024], P('expert', 'dp'), may hold values from -0.09375 to 0.09375
- w_down: bfloat16 [32, 1024, 3584], P('expert', None, 'dp'), may hold values from -0.1875 to 0.1875
- cotangent: bfloat16 [2048, 3584], P('expert', 'dp'), may hold values from -6 to 6
Outputs:
- mixed: bfloat16 [2048, 3584], P('expert', 'dp')
- token_grad: bfloat16 [2048, 3584], P('expert', 'dp')
- grad_gate: bfloat16 [32, 3584, 1024], P('expert', 'dp')
- grad_up: bfloat16 [32, 3584, 1024], P('expert', 'dp')
- grad_down: bfloat16 [32, 1024, 3584], P('expert', None, 'dp')
Inputs may be any that keep to these rules, and one draw needn't show every extreme that they name: `expert_ids`: each row names 8 different experts. In each aligned block of 64 rows (the rows of one device) no expert is named by more than 32 rows, and one expert, the same in every block, is named by exactly 32 rows of every block.
All inputs are finite; a program needn't handle non-finite values.
Results may differ from a plain program's by a relative error of at most 0.035.
Values may be sent and summed in bfloat16 or wider, within the bound.
No kernel may reach another device: no remote copies, remote signals or barrier semaphores. Data moves between devices by JAX's collectives and lax.ppermute only.
A program may use at most 64 MiB of HBM per device.

v0:
```python
import jax
import jax.numpy as jnp
from jax import lax
from jax.sharding import PartitionSpec as P

EXPERTS = 32
CAP = 32


def slot_table(expert_ids, gate_weights, first_expert, local_count):
    flat_ids = expert_ids.reshape(-1)
    numbers = jnp.arange(EXPERTS, dtype=jnp.int32)
    onehot = (flat_ids[:, None] == numbers[None, :]).astype(jnp.int32)
    slot_rank = jnp.sum((jnp.cumsum(onehot, axis=0) - 1) * onehot, axis=1)
    slot_number = (flat_ids - first_expert) * CAP + slot_rank
    inside = (flat_ids >= first_expert) & (flat_ids < first_expert + local_count)
    slot_list = jnp.arange(local_count * CAP, dtype=jnp.int32)
    matches = (slot_number[None, :] == slot_list[:, None]) & inside[None, :]
    matches = matches.reshape(local_count * CAP, expert_ids.shape[0], expert_ids.shape[1])
    pick_table = jnp.sum(matches, axis=2).astype(jnp.float32)
    weighted = jnp.sum(jnp.where(matches, gate_weights[None, :, :], 0.0), axis=2)
    return (pick_table, weighted)


def expert_pass(rows_in, rows_dy, w_gate, w_up, w_down):
    gate_part = jnp.einsum("erd,edf->erf", rows_in, w_gate, preferred_element_type=jnp.float32)
    up_part = jnp.einsum("erd,edf->erf", rows_in, w_up, preferred_element_type=jnp.float32)
    gate_sum, up_sum = (
        lax.psum(gate_part.astype(jnp.bfloat16), "dp").astype(jnp.float32),
        lax.psum(up_part.astype(jnp.bfloat16), "dp").astype(jnp.float32),
    )
    logistic = jax.nn.sigmoid(gate_sum)
    hidden = (gate_sum * logistic * up_sum).astype(jnp.bfloat16)
    out_rows = jnp.einsum(
        "erf,efd->erd", hidden, w_down, preferred_element_type=jnp.float32
    ).astype(jnp.bfloat16)
    grad_part = jnp.einsum("erd,efd->erf", rows_dy, w_down, preferred_element_type=jnp.float32)
    hidden_grad = lax.psum(grad_part.astype(jnp.bfloat16), "dp").astype(jnp.float32)
    up_grad = (hidden_grad * gate_sum * logistic).astype(jnp.bfloat16)
    gate_grad = (hidden_grad * up_sum * logistic * (1.0 + gate_sum * (1.0 - logistic))).astype(
        jnp.bfloat16
    )
    row_grad = (
        jnp.einsum("erf,edf->erd", gate_grad, w_gate, preferred_element_type=jnp.float32)
        + jnp.einsum("erf,edf->erd", up_grad, w_up, preferred_element_type=jnp.float32)
    ).astype(jnp.bfloat16)
    grad_gate = jnp.einsum(
        "erd,erf->edf", rows_in, gate_grad, preferred_element_type=jnp.float32
    ).astype(jnp.bfloat16)
    grad_up = jnp.einsum(
        "erd,erf->edf", rows_in, up_grad, preferred_element_type=jnp.float32
    ).astype(jnp.bfloat16)
    grad_down = jnp.einsum(
        "erf,erd->efd", hidden, rows_dy, preferred_element_type=jnp.float32
    ).astype(jnp.bfloat16)
    return (out_rows, row_grad, grad_gate, grad_up, grad_down)


def body(tokens, expert_ids, gate_weights, w_gate, w_up, w_down, cotangent):
    width = tokens.shape[1]
    pick_table, weighted = slot_table(expert_ids, gate_weights, 0, EXPERTS)
    send_in = jnp.dot(pick_table.astype(jnp.bfloat16), tokens, preferred_element_type=jnp.float32)
    send_in = send_in.astype(jnp.bfloat16).reshape(EXPERTS, CAP, width)
    send_dy = jnp.dot(weighted, cotangent.astype(jnp.float32), precision=lax.Precision.HIGHEST)
    send_dy = send_dy.astype(jnp.bfloat16).reshape(EXPERTS, CAP, width)
    rows_in, rows_dy = (
        lax.all_to_all(send_in, "expert", split_axis=0, concat_axis=1, tiled=True),
        lax.all_to_all(send_dy, "expert", split_axis=0, concat_axis=1, tiled=True),
    )
    out_rows, row_grad, grad_gate, grad_up, grad_down = expert_pass(
        rows_in, rows_dy, w_gate, w_up, w_down
    )
    back_out, back_grad = (
        lax.all_to_all(out_rows, "expert", split_axis=1, concat_axis=0, tiled=True),
        lax.all_to_all(row_grad, "expert", split_axis=1, concat_axis=0, tiled=True),
    )
    mixed = jnp.dot(
        weighted.T,
        back_out.reshape(EXPERTS * CAP, width).astype(jnp.float32),
        precision=lax.Precision.HIGHEST,
    )
    token_grad = jnp.dot(
        pick_table.T,
        back_grad.reshape(EXPERTS * CAP, width).astype(jnp.float32),
        precision=lax.Precision.HIGHEST,
    )
    return (
        mixed.astype(jnp.bfloat16),
        token_grad.astype(jnp.bfloat16),
        grad_gate,
        grad_up,
        grad_down,
    )


def solution(mesh):
    placed = (
        P("expert", "dp"),
        P("expert", None),
        P("expert", None),
        P("expert", "dp", None),
        P("expert", "dp", None),
        P("expert", None, "dp"),
        P("expert", "dp"),
    )
    return jax.shard_map(
        body,
        mesh=mesh,
        in_specs=placed,
        out_specs=(
            P("expert", "dp"),
            P("expert", "dp"),
            P("expert", "dp", None),
            P("expert", "dp", None),
            P("expert", None, "dp"),
        ),
        check_vma=False,
    )
```

profile of v0, /device:TPU:1, one launch (start us, length us, event | category | flops | bytes accessed | tf_op | source)
XLA Modules:
  0.0 278.0 jit_solution(8771143864421726830)
XLA Ops:
  14.4 13.7 %all-to-all-start = ((bf16[32,32,224]{2,1,0:T(8,128)(2,1)}), bf16[32,32,224]{2,1,0:T(8,128)(2,1)S(1)}, u32[]{:S(2)}, u32[]{:S(2)}) async-start(bf16[32,32,224]{2,1,0:T(8,128)(2,1)} %bitcast.1), calls=%async_computation | async-start | bytes 1048576 | tf_op jit(solution)/shard_map/all_to_all | solution.py:67
  30.7 13.7 %all-to-all-done = bf16[32,32,224]{2,1,0:T(8,128)(2,1)S(1)} async-done(((bf16[32,32,224]{2,1,0:T(8,128)(2,1)}), bf16[32,32,224]{2,1,0:T(8,128)(2,1)S(1)}, u32[]{:S(2)}, u32[]{:S(2)}) %all-to-all-start) | async-done | bytes 458784 | tf_op jit(solution)/shard_map/all_to_all | solution.py:67
  44.4 5.2 %all-to-all-start.2 = ((bf16[32,32,224]{2,1,0:T(8,128)(2,1)}), bf16[32,32,224]{2,1,0:T(8,128)(2,1)S(1)}, u32[]{:S(2)}, u32[]{:S(2)}) async-start(bf16[32,32,224]{2,1,0:T(8,128)(2,1)} %bitcast.11), calls=%async_computation.2 | async-start | bytes 1048576 | tf_op jit(solution)/shard_map/all_to_all | solution.py:68
  49.9 2.1 convert_bitcast_fusion.1
  51.9 2.0 convert_bitcast_fusion.2
  53.9 10.7 %all-to-all-done.2 = bf16[32,32,224]{2,1,0:T(8,128)(2,1)S(1)} async-done(((bf16[32,32,224]{2,1,0:T(8,128)(2,1)}), bf16[32,32,224]{2,1,0:T(8,128)(2,1)S(1)}, u32[]{:S(2)}, u32[]{:S(2)}) %all-to-all-start.2) | async-done | bytes 458784 | tf_op jit(solution)/shard_map/all_to_all | solution.py:68
  64.7 2.0 convert_bitcast_fusion
  66.7 131.9 %all-reduce.3.cloned.1.call-done = (bf16[1,1024,1024]{2,1,0:T(8,128)(2,1)}, bf16[1,1024,1024]{2,1,0:T(8,128)(2,1)}, bf16[1,1024,1024]{2,1,0:T(8,128)(2,1)}) async-done(((bf16[1,1024,1024]{2,1,0:T(8,128)(2,1)}, bf16[1,1024,1024]{2,1,0:T(8,128)(2,1)}, bf16[1,1024,1024]{2,1,0:T(8,128)(2,1)}), (bf16[1,1024,1024]{2,1,0:T(8,128)(2,1)}, bf16[1,1024,1024]{2,1,0:T(8,128)(2,1)}, ...) | async-done | bytes 6291472 | tf_op jit(solution)/shard_map/psum | solution.py:30
  198.6 5.6 %fusion.3 = (bf16[1,1024,1024]{2,1,0:T(8,128)(2,1)S(1)}, bf16[1,1024,1024]{2,1,0:T(8,128)(2,1)S(1)}, bf16[1,1024,1024]{2,1,0:T(8,128)(2,1)}) fusion(bf16[1,1024,1024]{2,1,0:T(8,128)(2,1)} %get-tuple-element.5, bf16[1,1024,1024]{2,1,0:T(8,128)(2,1)} %get-tuple-element.7, bf16[1,1024,1024]{2,1,0:T(8,128)(2,1)} %get-tuple-element.6), kind=kLoop, calls=%fused_computation.9 | loop fusion | flops 19922944 | bytes 12582912 | tf_op jit(solution)/shard_map/convert_element_type | solution.py:40
  205.6 1.6 fusion.53
  207.2 3.5 %copy.84 = bf16[1,1024,224]{2,0,1:T(2,128)(2,1)} copy(bf16[1,1024,224]{1,2,0:T(8,128)(2,1)} %fusion.53) | data formatting | bytes 917504 | tf_op jit(solution)/shard_map/convert_element_type | solution.py:46
  211.2 5.7 %reduce.3 = bf16[1024,224]{1,0:T(8,128)(2,1)} reduce(bf16[1024,1,224]{2,1,0:T(2,128)(2,1)} %bitcast.111, bf16[]{:T(256)} %broadcast.63), dimensions={1}, to_apply=%bitcast.94.reduce_sub_computation | reduce | bytes 917506
  216.9 2.7 reshape.161
  219.6 10.2 %all-to-all-start.3 = ((bf16[32,2,3584]{2,1,0:T(2,128)(2,1)}), bf16[32,2,3584]{2,1,0:T(2,128)(2,1)}, u32[]{:S(2)}, u32[]{:S(2)}) async-start(bf16[32,2,3584]{2,1,0:T(2,128)(2,1)} %reshape.161), calls=%async_computation.3 | async-start | bytes 917504 | tf_op jit(solution)/shard_map/all_to_all | solution.py:75
  229.8 3.2 %fusion.50 = bf16[1,1024,224]{1,2,0:T(8,128)(2,1)} fusion(bf16[1,1024,1024]{2,1,0:T(8,128)(2,1)} %get-tuple-element.10, bf16[1,1024,224]{1,2,0:T(8,128)(2,1)} %param.12), kind=kOutput, calls=%fused_computation.46 | convolution fusion | flops 469991424 | bytes 3014656 | tf_op jit(solution)/shard_map/erf,efd->erd/dot_general | solution.py:34
  233.0 3.5 %copy.81 = bf16[1,1024,224]{2,0,1:T(2,128)(2,1)} copy(bf16[1,1024,224]{1,2,0:T(8,128)(2,1)} %fusion.50) | data formatting | bytes 917504 | tf_op jit(solution)/shard_map/convert_element_type | solution.py:36
  236.6 5.7 %reduce.2 = bf16[1024,224]{1,0:T(8,128)(2,1)} reduce(bf16[1024,1,224]{2,1,0:T(2,128)(2,1)} %bitcast.112, bf16[]{:T(256)} %broadcast.63), dimensions={1}, to_apply=%bitcast.92.reduce_sub_computation | reduce | bytes 917506
  242.2 2.7 reshape.159
  244.9 9.0 %all-to-all-start.1 = ((bf16[32,2,3584]{2,1,0:T(2,128)(2,1)}), bf16[32,2,3584]{2,1,0:T(2,128)(2,1)}, u32[]{:S(2)}, u32[]{:S(2)}) async-start(bf16[32,2,3584]{2,1,0:T(2,128)(2,1)} %reshape.159), calls=%async_computation.1 | async-start | bytes 917504 | tf_op jit(solution)/shard_map/all_to_all | solution.py:74
  254.0 3.0 %fusion.41 = bf16[1,224,1024]{2,1,0:T(8,128)(2,1)} fusion(bf16[1024,224]{1,0:T(8,128)(2,1)S(1)} %bitcast.109, bf16[1,1024,1024]{2,1,0:T(8,128)(2,1)} %copy-done.1), kind=kOutput, calls=%fused_computation.43 | convolution fusion | flops 469991424 | bytes 3014656 | tf_op jit(solution)/shard_map/erd,erf->edf/dot_general | solution.py:50
  259.0 1.5 fusion.47
  260.4 2.7 reshape.162
  264.9 1.8 all-to-all-done.1
  266.7 2.6 reshape.160
  (56 shorter events, 17.4 us)
Async XLA Ops:
  7.2 42.7 %copy-start = (bf16[1,224,1024]{2,1,0:T(8,128)(2,1)S(1)}, bf16[1,224,1024]{2,1,0:T(8,128)(2,1)}, u32[]{:S(2)}) copy-start(bf16[1,224,1024]{2,1,0:T(8,128)(2,1)} %param.11) | copy-start | bytes 1376260
  7.2 21.0 %copy-start.11 = (f32[64,8]{0,1:T(8,128)S(1)}, f32[64,8]{0,1:T(8,128)}, u32[]{:S(2)}) copy-start(f32[64,8]{0,1:T(8,128)} %param.9) | copy-start | bytes 6148
  7.2 22.0 %copy-start.10 = (bf16[64,224]{1,0:T(8,128)(2,1)S(1)}, bf16[64,224]{1,0:T(8,128)(2,1)}, u32[]{:S(2)}) copy-start(bf16[64,224]{1,0:T(8,128)(2,1)} %param.13) | copy-start | bytes 86020
  12.3 2.1 copy-start.2
  14.4 30.0 %all-to-all-start = ((bf16[32,32,224]{2,1,0:T(8,128)(2,1)}), bf16[32,32,224]{2,1,0:T(8,128)(2,1)S(1)}, u32[]{:S(2)}, u32[]{:S(2)}) async-start(bf16[32,32,224]{2,1,0:T(8,128)(2,1)} %bitcast.1), calls=%async_computation | async-start | bytes 1048576 | tf_op jit(solution)/shard_map/all_to_all | solution.py:67
  30.7 21.2 %copy-start.7 = (bf16[1,224,1024]{2,1,0:T(8,128)(2,1)S(1)}, bf16[1,224,1024]{2,1,0:T(8,128)(2,1)}, u32[]{:S(2)}) copy-start(bf16[1,224,1024]{2,1,0:T(8,128)(2,1)} %param.10) | copy-start | bytes 1376260
  44.4 20.3 %all-to-all-start.2 = ((bf16[32,32,224]{2,1,0:T(8,128)(2,1)}), bf16[32,32,224]{2,1,0:T(8,128)(2,1)S(1)}, u32[]{:S(2)}, u32[]{:S(2)}) async-start(bf16[32,32,224]{2,1,0:T(8,128)(2,1)} %bitcast.11), calls=%async_computation.2 | async-start | bytes 1048576 | tf_op jit(solution)/shard_map/all_to_all | solution.py:68
  49.6 149.0 %all-reduce.3.cloned.1.call-start = ((), (), s32[]{:S(2)}) async-start(), calls=%async_computation.4 | async-start | bytes 12582912 | tf_op jit(solution)/shard_map/psum | solution.py:30
  51.9 12.8 %copy-start.9 = (bf16[1,1024,224]{1,2,0:T(8,128)(2,1)S(1)}, bf16[1,1024,224]{1,2,0:T(8,128)(2,1)}, u32[]{:S(2)}) copy-start(bf16[1,1024,224]{1,2,0:T(8,128)(2,1)} %param.12) | copy-start | bytes 1376260
  64.7 2.0 copy-start.4
  204.3 1.3 copy-start.1
  204.3 1.3 copy-start.8
  219.6 25.4 %all-to-all-start.3 = ((bf16[32,2,3584]{2,1,0:T(2,128)(2,1)}), bf16[32,2,3584]{2,1,0:T(2,128)(2,1)}, u32[]{:S(2)}, u32[]{:S(2)}) async-start(bf16[32,2,3584]{2,1,0:T(2,128)(2,1)} %reshape.161), calls=%async_computation.3 | async-start | bytes 917504 | tf_op jit(solution)/shard_map/all_to_all | solution.py:75
  244.9 21.8 %all-to-all-start.1 = ((bf16[32,2,3584]{2,1,0:T(2,128)(2,1)}), bf16[32,2,3584]{2,1,0:T(2,128)(2,1)}, u32[]{:S(2)}, u32[]{:S(2)}) async-start(bf16[32,2,3584]{2,1,0:T(2,128)(2,1)} %reshape.159), calls=%async_computation.1 | async-start | bytes 917504 | tf_op jit(solution)/shard_map/all_to_all | solution.py:74
  257.0 1.4 copy-start.5
  257.0 1.9 copy-start.6
  260.4 3.3 %copy-start.3 = (s32[1024,64]{0,1:T(8,128)S(1)}, s32[1024,64]{0,1:T(8,128)}, u32[]{:S(2)}) copy-start(s32[1024,64]{0,1:T(8,128)} %copy-done.2) | copy-start | bytes 786436
Sparse Core Ops, SparseCore 0:
  66.8 131.7 all-reduce.2
where the time goes:
time: 283 us; the launch traced here: 278 us
  waiting for transfers between devices  158 us (56%)
  starting transfers between devices  38.4 us (14%)
  local copies, waits for them, and re-layouts  24.3 us (9%)
  matrix products  21.6 us (8%)
  other arithmetic  21.4 us (8%)
  between operations  14.2 us (5%)
    psum x1, waiting for transfers between devices, expert_pass(): lax.psum(up_part.astype(jnp.bfloat16), 'dp').astype(jnp.float32)  132 us
    all_to_all x1, starting transfers between devices, body(): lax.all_to_all(send_in, 'expert', split_axis=0, concat_axis=1, tiled=True)  13.7 us
    all_to_all x1, waiting for transfers between devices, body(): lax.all_to_all(send_in, 'expert', split_axis=0, concat_axis=1, tiled=True)  13.7 us
    unnamed x31, local copies, waits for them, and re-layouts  13.2 us
    unnamed x2, other arithmetic  11.3 us
    all_to_all x1, waiting for transfers between devices, body(): lax.all_to_all(send_dy, 'expert', split_axis=0, concat_axis=1, tiled=True)  10.7 us
    all_to_all x1, starting transfers between devices, body(): lax.all_to_all(row_grad, 'expert', split_axis=1, concat_axis=0, tiled=True)  10.2 us
    all_to_all x1, starting transfers between devices, body(): lax.all_to_all(out_rows, 'expert', split_axis=1, concat_axis=0, tiled=True)  9.05 us
  transfers between devices with their start and end apart: 5, of which 4 were waited for; matrix products, arithmetic and copies ran while one was open for 12% of the time, Pallas kernels for 0%

commit v1 on v0

v1 whole, which is shorter than its diff:
```python
import functools
import jax
import jax.numpy as jnp
from jax import lax
from jax.experimental import pallas as pl
from jax.experimental.pallas import tpu as pltpu
from jax.sharding import Mesh, PartitionSpec as P

EXPERTS = 32
CAP = 32
BF = jnp.bfloat16
F32 = jnp.float32
SWAP = [(0, 1), (1, 0)]


def iota(shape, dim):
    return lax.broadcasted_iota(jnp.int32, shape, dim)


def contract_first(left, right, precision=None):
    return lax.dot_general(
        left, right, (((0,), (0,)), ((), ())), preferred_element_type=F32, precision=precision
    )


def slot_table(ids, gates):
    tokens = ids.shape[0]
    numbers = iota((tokens, EXPERTS), 1)
    chosen = jnp.zeros((tokens, EXPERTS), F32)
    weight = jnp.zeros((tokens, EXPERTS), F32)
    for k in range(ids.shape[1]):
        hit = ids[:, k : k + 1] == numbers
        chosen = chosen + hit.astype(F32)
        weight = weight + jnp.where(hit, gates[:, k : k + 1], 0.0)
    row, col = iota((tokens, tokens), 0), iota((tokens, tokens), 1)
    earlier = (row < col).astype(F32)
    same = (row == col).astype(F32)
    rank_t = contract_first(chosen, earlier)
    chosen_t = contract_first(chosen, same)
    weight_t = contract_first(weight, same, lax.Precision.HIGHEST)
    code = jnp.where(chosen_t > 0.5, rank_t, -1.0).astype(jnp.int32)
    slots = iota((EXPERTS, CAP, tokens), 1)
    hit = code[:, None, :] == slots
    pick = jnp.where(hit, 1.0, 0.0).reshape(EXPERTS * CAP, tokens)
    slot_gate = jnp.sum(jnp.where(hit, weight_t[:, None, :], 0.0), axis=2, keepdims=True)
    return pick, slot_gate.reshape(EXPERTS * CAP, 1)


def send_kernel(ids_ref, gates_ref, tokens_ref, cotangent_ref, rows_ref, dy_ref):
    pick, slot_gate = slot_table(ids_ref[...], gates_ref[...])
    pick = pick.astype(BF)
    rows = jnp.dot(pick, tokens_ref[...], preferred_element_type=F32)
    rows_ref[...] = rows.astype(BF)
    dy = jnp.dot(pick, cotangent_ref[...], preferred_element_type=F32)
    dy_ref[...] = (dy * slot_gate).astype(BF)


def mix_kernel(ids_ref, gates_ref, back_ref, mixed_ref):
    pick, slot_gate = slot_table(ids_ref[...], gates_ref[...])
    pick = pick.astype(BF)
    scaled = back_ref[...].astype(F32) * slot_gate
    high = scaled.astype(BF)
    low = (scaled - high.astype(F32)).astype(BF)
    mixed_ref[...] = (contract_first(pick, high) + contract_first(pick, low)).astype(BF)


def grad_kernel(ids_ref, gates_ref, back_ref, grad_ref):
    pick, _ = slot_table(ids_ref[...], gates_ref[...])
    grad_ref[...] = contract_first(pick.astype(BF), back_ref[...]).astype(BF)


def dot(spec, left, right):
    return jnp.einsum(spec, left, right, preferred_element_type=F32)


def to_experts(rows):
    width = rows.shape[1]
    rows = rows.reshape(EXPERTS, CAP, width)
    rows = lax.all_to_all(rows, "expert", split_axis=0, concat_axis=0, tiled=True)
    return rows.reshape(EXPERTS * CAP, width)


def halves(rows, core):
    rows = rows.reshape(8, 2, 64, rows.shape[1])
    own = lax.dynamic_index_in_dim(rows, core, 1, keepdims=False)
    other = lax.dynamic_index_in_dim(rows, 1 - core, 1, keepdims=False)
    return own.reshape(512, -1), other.reshape(512, -1)


def scatter(part):
    return lax.psum_scatter(part, "y", scatter_dimension=0, tiled=True).astype(F32)


def gather(shard):
    return lax.all_gather(shard, ("y", "core"), axis=0, tiled=True)


def body(tokens, expert_ids, gate_weights, w_gate, w_up, w_down, cotangent):
    width = tokens.shape[1]
    slots = EXPERTS * CAP
    w_gate, w_up, w_down = w_gate[0], w_up[0], w_down[0]
    core = lax.axis_index("core")
    send_in, send_dy = pl.pallas_call(
        send_kernel,
        out_shape=[jax.ShapeDtypeStruct((slots, width), BF)] * 2,
        name="send_rows",
    )(expert_ids, gate_weights, tokens, cotangent)
    rows_in = to_experts(send_in)
    rows_dy = to_experts(send_dy)

    own, other = halves(rows_in, core)
    gate_other = lax.ppermute(dot("rd,df->rf", other, w_gate).astype(BF), "core", SWAP)
    up_other = lax.ppermute(dot("rd,df->rf", other, w_up).astype(BF), "core", SWAP)
    gate_part = (dot("rd,df->rf", own, w_gate) + gate_other.astype(F32)).astype(BF)
    up_part = (dot("rd,df->rf", own, w_up) + up_other.astype(F32)).astype(BF)
    gate_sum = scatter(gate_part)
    up_sum = scatter(up_part)

    own, other = halves(rows_dy, core)
    hid_other = lax.ppermute(dot("rd,fd->rf", other, w_down).astype(BF), "core", SWAP)
    hid_part = (dot("rd,fd->rf", own, w_down) + hid_other.astype(F32)).astype(BF)
    hidden_grad = scatter(hid_part)

    logistic = jax.nn.sigmoid(gate_sum)
    hidden = gather((gate_sum * logistic * up_sum).astype(BF))
    up_grad = (hidden_grad * gate_sum * logistic).astype(BF)
    gate_grad = (hidden_grad * up_sum * logistic * (1.0 + gate_sum * (1.0 - logistic))).astype(BF)
    up_grad = gather(up_grad)
    gate_grad = gather(gate_grad)

    out_rows = dot("rf,fd->rd", hidden, w_down).astype(BF)
    back_out = to_experts(out_rows)
    mixed = pl.pallas_call(
        mix_kernel, out_shape=jax.ShapeDtypeStruct(tokens.shape, BF), name="mix_rows"
    )(expert_ids, gate_weights, back_out)

    row_grad = (
        dot("rf,df->rd", gate_grad, w_gate) + dot("rf,df->rd", up_grad, w_up)
    ).astype(BF)
    back_grad = to_experts(row_grad)
    token_grad = pl.pallas_call(
        grad_kernel, out_shape=jax.ShapeDtypeStruct(tokens.shape, BF), name="sum_rows"
    )(expert_ids, gate_weights, back_grad)

    grad_down = dot("rf,rd->fd", hidden, rows_dy).astype(BF)
    grad_gate = dot("rd,rf->df", rows_in, gate_grad).astype(BF)
    grad_up = dot("rd,rf->df", rows_in, up_grad).astype(BF)
    return mixed, token_grad, grad_gate[None], grad_up[None], grad_down[None]


def solution(mesh):
    fine = Mesh(mesh.devices.reshape(8, 2, 32), ("y", "core", "expert"))
    dp = ("y", "core")
    placed = (
        P("expert", dp),
        P("expert", None),
        P("expert", None),
        P("expert", dp, None),
        P("expert", dp, None),
        P("expert", None, dp),
        P("expert", dp),
    )
    return jax.shard_map(
        body,
        mesh=fine,
        in_specs=placed,
        out_specs=(
            P("expert", dp),
            P("expert", dp),
            P("expert", dp, None),
            P("expert", dp, None),
            P("expert", None, dp),
        ),
        check_vma=False,
    )
```

time: 283 us -> 369 us (1.30)
  waiting for transfers between devices: 158 us -> 252 us
  blocking collectives: 0 us -> 30.1 us
  other arithmetic: 21.4 us -> 1.93 us
  local copies, waits for them, and re-layouts: 24.3 us -> 6.29 us
  Pallas kernels: 0 us -> 7.53 us
    psum x1 -> x0, waiting for transfers between devices: 132 us -> none  [expert_pass(): lax.psum(up_part.astype(jnp.bfloat16), 'dp').astype(jnp.float32)]
    all_gather x0 -> x3, waiting for transfers between devices: none -> 116 us  [gather(): return lax.all_gather(shard, ('y', 'core'), axis=0, tiled=True)]
    reduce_scatter x0 -> x3, waiting for transfers between devices: none -> 105 us  [scatter(): lax.psum_scatter(part, 'y', scatter_dimension=0, tiled=True).astype(F32)]
    all_to_all x0 -> x1, blocking collectives: none -> 30.1 us  [to_experts(): lax.all_to_all(rows, 'expert', split_axis=0, concat_axis=0, tiled=True)]
    all_to_all x4 -> x3, starting transfers between devices: 38.2 us -> 25.5 us  [to_experts(): lax.all_to_all(rows, 'expert', split_axis=0, concat_axis=0, tiled=True)]
    unnamed x2 -> x0, other arithmetic: 11.3 us -> none
    ppermute x0 -> x3, starting transfers between devices: none -> 10.4 us  [the longest x1 5.66 us: body(): lax.ppermute(dot('rd,df->rf', other, w_up).astype(BF), 'core', SWAP)]
    unnamed x31 -> x18, local copies, waits for them, and re-layouts: 13.2 us -> 3.32 us
  transfers between devices with their start and end apart: 5 -> 12, of which waited for: 4 -> 11; matrix products, arithmetic and copies ran while one was open for 12% -> 5% of each run, Pallas kernels for 0% -> 1%
where the time goes in v1:
time: 369 us; the launch traced here: 367 us
  waiting for transfers between devices  252 us (68%)
  starting transfers between devices  36.1 us (10%)
  blocking collectives  30.1 us (8%)
  matrix products  18.6 us (5%)
  between operations  14.3 us (4%)
  Pallas kernels  7.53 us (2%)
  local copies, waits for them, and re-layouts  6.29 us (2%)
    all_gather x3, waiting for transfers between devices, gather(): return lax.all_gather(shard, ('y', 'core'), axis=0, tiled=True)  116 us
    reduce_scatter x3, waiting for transfers between devices, scatter(): lax.psum_scatter(part, 'y', scatter_dimension=0, tiled=True).astype(F32)  105 us
    all_to_all x1, blocking collectives, to_experts(): lax.all_to_all(rows, 'expert', split_axis=0, concat_axis=0, tiled=True)  30.1 us
    all_to_all x3, starting transfers between devices, to_experts(): lax.all_to_all(rows, 'expert', split_axis=0, concat_axis=0, tiled=True)  25.5 us
    all_to_all x3, waiting for transfers between devices, to_experts(): lax.all_to_all(rows, 'expert', split_axis=0, concat_axis=0, tiled=True)  22.8 us
    dot_general x12, matrix products, dot(): return jnp.einsum(spec, left, right, preferred_element_type=F32)  18.6 us
  transfers between devices with their start and end apart: 12, of which 11 were waited for; matrix products, arithmetic and copies ran while one was open for 5% of the time, Pallas kernels for 1%

profile of v1, /device:TPU:1, one launch (start us, length us, event | category | flops | bytes accessed | tf_op | source)
XLA Modules:
  0.0 367.3 jit_solution(17043927965515512021)
XLA Ops:
  10.0 2.5 send_rows.1
  12.5 30.1 %all_to_all.20 = bf16[32,32,224]{2,1,0:T(8,128)(2,1)S(1)} all-to-all(bf16[32,32,224]{2,1,0:T(8,128)(2,1)} %bitcast.75), channel_id=1, replica_groups=mesh['y'=8,'core'=2,'expert'=32] {'expert'}, dimensions={0} | all-to-all | bytes 917504 | tf_op jit(solution)/shard_map/all_to_all | solution.py:79
  42.6 5.2 %all-to-all-start.2 = ((bf16[32,32,224]{2,1,0:T(8,128)(2,1)}), bf16[32,32,224]{2,1,0:T(8,128)(2,1)S(1)}, u32[]{:S(2)}, u32[]{:S(2)}) async-start(bf16[32,32,224]{2,1,0:T(8,128)(2,1)} %bitcast.74), calls=%async_computation.4 | async-start | bytes 1048576 | tf_op jit(solution)/shard_map/all_to_all | solution.py:79
  47.9 15.0 %all-to-all-done.2 = bf16[32,32,224]{2,1,0:T(8,128)(2,1)S(1)} async-done(((bf16[32,32,224]{2,1,0:T(8,128)(2,1)}), bf16[32,32,224]{2,1,0:T(8,128)(2,1)S(1)}, u32[]{:S(2)}, u32[]{:S(2)}) %all-to-all-start.2) | async-done | bytes 458784 | tf_op jit(solution)/shard_map/all_to_all | solution.py:79
  64.3 5.7 %collective-permute-start.1 = (bf16[512,1024]{1,0:T(8,128)(2,1)S(1)}, bf16[512,1024]{1,0:T(8,128)(2,1)S(1)}, u32[]{:S(2)}, u32[]{:S(2)}) collective-permute-start(bf16[512,1024]{1,0:T(8,128)(2,1)S(1)} %convolution_convert_fusion.1), channel_id=1, source_target_pairs={{0,32},{32,0},{1,33},{33,1},{2,34},{34,2},{3,35},{35,3},{4,36},{36... | collective-permute-start | bytes 3145736 | tf_op jit(solution)/shard_map/ppermute | solution.py:113
  69.9 2.3 collective-permute-done.1
  74.2 2.4 collective-permute-start
  76.6 2.3 collective-permute-done
  80.8 2.3 collective-permute-start.2
  86.8 19.4 %reduce-scatter.6.cloned.1.call-done = bf16[64,1024]{1,0:T(8,128)(2,1)} async-done(((bf16[512,1024]{1,0:T(8,128)(2,1)}), bf16[64,1024]{1,0:T(8,128)(2,1)}) %reduce-scatter.6.cloned.1.call-update) | async-done | bytes 131088 | tf_op jit(solution)/shard_map/reduce_scatter | solution.py:91
  106.2 43.0 %reduce-scatter.4.cloned.1.call-done = bf16[64,1024]{1,0:T(8,128)(2,1)} async-done(((bf16[512,1024]{1,0:T(8,128)(2,1)}), bf16[64,1024]{1,0:T(8,128)(2,1)}) %reduce-scatter.4.cloned.1.call-update) | async-done | bytes 131088 | tf_op jit(solution)/shard_map/reduce_scatter | solution.py:91
  149.2 43.0 %reduce-scatter.8.cloned.1.call-done = bf16[64,1024]{1,0:T(8,128)(2,1)} async-done(((bf16[512,1024]{1,0:T(8,128)(2,1)}), bf16[64,1024]{1,0:T(8,128)(2,1)}) %reduce-scatter.8.cloned.1.call-update) | async-done | bytes 131088 | tf_op jit(solution)/shard_map/reduce_scatter | solution.py:91
  195.4 45.3 %all-gather.6.cloned.1.call-done = bf16[1024,1024]{1,0:T(8,128)(2,1)} async-done(((bf16[64,1024]{1,0:T(8,128)(2,1)}), bf16[1024,1024]{1,0:T(8,128)(2,1)}) %all-gather.6.cloned.1.call-update) | async-done | bytes 2097168 | tf_op jit(solution)/shard_map/all_gather | solution.py:95
  240.7 2.4 fusion.16
  243.1 41.0 %all-gather.8.cloned.1.call-done = bf16[1024,1024]{1,0:T(8,128)(2,1)} async-done(((bf16[64,1024]{1,0:T(8,128)(2,1)}), bf16[1024,1024]{1,0:T(8,128)(2,1)}) %all-gather.8.cloned.1.call-update) | async-done | bytes 2097168 | tf_op jit(solution)/shard_map/all_gather | solution.py:95
  284.1 2.4 fusion
  287.5 10.0 %all-to-all-start.3 = ((bf16[32,32,224]{2,1,0:T(8,128)(2,1)}), bf16[32,32,224]{2,1,0:T(8,128)(2,1)}, u32[]{:S(2)}, u32[]{:S(2)}) async-start(bf16[32,32,224]{2,1,0:T(8,128)(2,1)} %bitcast.13), calls=%async_computation.6 | async-start | bytes 1048576 | tf_op jit(solution)/shard_map/all_to_all | solution.py:79
  297.5 30.0 %all-gather.4.cloned.1.call-done = bf16[1024,1024]{1,0:T(8,128)(2,1)} async-done(((bf16[64,1024]{1,0:T(8,128)(2,1)}), bf16[1024,1024]{1,0:T(8,128)(2,1)}) %all-gather.4.cloned.1.call-update) | async-done | bytes 2097168 | tf_op jit(solution)/shard_map/all_gather | solution.py:95
  327.5 2.4 convolution_convert_fusion.6
  330.9 10.3 %all-to-all-start.1 = ((bf16[32,32,224]{2,1,0:T(8,128)(2,1)}), bf16[32,32,224]{2,1,0:T(8,128)(2,1)}, u32[]{:S(2)}, u32[]{:S(2)}) async-start(bf16[32,32,224]{2,1,0:T(8,128)(2,1)} %bitcast.69), calls=%async_computation.3 | async-start | bytes 1048576 | tf_op jit(solution)/shard_map/all_to_all | solution.py:79
  341.2 3.0 fusion.1
  347.7 2.3 sum_rows.1
  350.0 7.8 %all-to-all-done.1 = bf16[32,32,224]{2,1,0:T(8,128)(2,1)} async-done(((bf16[32,32,224]{2,1,0:T(8,128)(2,1)}), bf16[32,32,224]{2,1,0:T(8,128)(2,1)}, u32[]{:S(2)}, u32[]{:S(2)}) %all-to-all-start.1) | async-done | bytes 458784 | tf_op jit(solution)/shard_map/all_to_all | solution.py:79
  357.8 2.7 mix_rows.1
  (44 shorter events, 20.3 us)
Async XLA Ops:
  7.2 66.5 %copy-start = (bf16[1,224,1024]{2,1,0:T(8,128)(2,1)S(1)}, bf16[1,224,1024]{2,1,0:T(8,128)(2,1)}, u32[]{:S(2)}) copy-start(bf16[1,224,1024]{2,1,0:T(8,128)(2,1)} %param.10) | copy-start | bytes 1376260
  12.5 51.3 %copy-start.2 = (bf16[1,224,1024]{2,1,0:T(8,128)(2,1)S(1)}, bf16[1,224,1024]{2,1,0:T(8,128)(2,1)}, u32[]{:S(2)}) copy-start(bf16[1,224,1024]{2,1,0:T(8,128)(2,1)} %param.11) | copy-start | bytes 1376260
  42.6 20.3 %all-to-all-start.2 = ((bf16[32,32,224]{2,1,0:T(8,128)(2,1)}), bf16[32,32,224]{2,1,0:T(8,128)(2,1)S(1)}, u32[]{:S(2)}, u32[]{:S(2)}) async-start(bf16[32,32,224]{2,1,0:T(8,128)(2,1)} %bitcast.74), calls=%async_computation.4 | async-start | bytes 1048576 | tf_op jit(solution)/shard_map/all_to_all | solution.py:79
  47.9 58.3 %reduce-scatter.6.cloned.1.call-start = ((), (), s32[]{:S(2)}) async-start(), calls=%async_computation.8 | async-start | bytes 1179648 | tf_op jit(solution)/shard_map/reduce_scatter | solution.py:91
  62.9 10.7 %copy-start.3 = (bf16[32,32,224]{2,1,0:T(8,128)(2,1)}, bf16[32,32,224]{2,1,0:T(8,128)(2,1)S(1)}, u32[]{:S(2)}) copy-start(bf16[32,32,224]{2,1,0:T(8,128)(2,1)S(1)} %all-to-all-done.2) | copy-start | bytes 1376260
  64.3 7.9 %collective-permute-start.1 = (bf16[512,1024]{1,0:T(8,128)(2,1)S(1)}, bf16[512,1024]{1,0:T(8,128)(2,1)S(1)}, u32[]{:S(2)}, u32[]{:S(2)}) collective-permute-start(bf16[512,1024]{1,0:T(8,128)(2,1)S(1)} %convolution_convert_fusion.1), channel_id=1, source_target_pairs={{0,32},{32,0},{1,33},{33,1},{2,34},{34,2},{3,35},{35,3},{4,36},{36... | collective-permute-start | bytes 3145736 | tf_op jit(solution)/shard_map/ppermute | solution.py:113
  73.6 75.6 %reduce-scatter.4.cloned.1.call-start = ((), (), s32[]{:S(2)}) async-start(), calls=%async_computation.7 | async-start | bytes 1179648 | tf_op jit(solution)/shard_map/reduce_scatter | solution.py:91
  74.1 6.2 %copy-start.5 = (bf16[1,1024,224]{1,2,0:T(8,128)(2,1)S(1)}, bf16[1,1024,224]{1,2,0:T(8,128)(2,1)}, u32[]{:S(2)}) copy-start(bf16[1,1024,224]{1,2,0:T(8,128)(2,1)} %param.12) | copy-start | bytes 1376260
  74.2 4.7 %collective-permute-start = (bf16[512,1024]{1,0:T(8,128)(2,1)S(1)}, bf16[512,1024]{1,0:T(8,128)(2,1)S(1)}, u32[]{:S(2)}, u32[]{:S(2)}) collective-permute-start(bf16[512,1024]{1,0:T(8,128)(2,1)S(1)} %convolution_convert_fusion.2), channel_id=1, source_target_pairs={{0,32},{32,0},{1,33},{33,1},{2,34},{34,2},{3,35},{35,3},{4,36},{36... | collective-permute-start | bytes 3145736 | tf_op jit(solution)/shard_map/ppermute | solution.py:112
  80.2 5.1 %copy-start.6 = (bf16[8,1,64,224]{3,2,1,0:T(8,128)(2,1)S(1)}, bf16[8,1,64,224]{3,2,1,0:T(8,128)(2,1)}, u32[]{:S(2)}) copy-start(bf16[8,1,64,224]{3,2,1,0:T(8,128)(2,1)} %get-tuple-element.9) | copy-start | bytes 688132
  80.3 112.0 %reduce-scatter.8.cloned.1.call-start = ((), (), s32[]{:S(2)}) async-start(), calls=%async_computation.10 | async-start | bytes 1179648 | tf_op jit(solution)/shard_map/reduce_scatter | solution.py:91
  80.8 4.6 %collective-permute-start.2 = (bf16[512,1024]{1,0:T(8,128)(2,1)S(1)}, bf16[512,1024]{1,0:T(8,128)(2,1)S(1)}, u32[]{:S(2)}, u32[]{:S(2)}) collective-permute-start(bf16[512,1024]{1,0:T(8,128)(2,1)S(1)} %convolution_convert_fusion), channel_id=1, source_target_pairs={{0,32},{32,0},{1,33},{33,1},{2,34},{34,2},{3,35},{35,3},{4,36},{36... | collective-permute-start | bytes 3145736 | tf_op jit(solution)/shard_map/ppermute | solution.py:120
  86.8 153.9 %all-gather.6.cloned.1.call-start = ((), (), s32[]{:S(2)}) async-start(), calls=%async_computation.11 | async-start | bytes 2228224 | tf_op jit(solution)/shard_map/all_gather | solution.py:95
  194.2 89.9 %all-gather.8.cloned.1.call-start = ((), (), s32[]{:S(2)}) async-start(), calls=%async_computation.12 | async-start | bytes 2228224 | tf_op jit(solution)/shard_map/all_gather | solution.py:95
  194.8 132.7 %all-gather.4.cloned.1.call-start = ((), (), s32[]{:S(2)}) async-start(), calls=%async_computation.9 | async-start | bytes 2228224 | tf_op jit(solution)/shard_map/all_gather | solution.py:95
  287.5 43.5 %all-to-all-start.3 = ((bf16[32,32,224]{2,1,0:T(8,128)(2,1)}), bf16[32,32,224]{2,1,0:T(8,128)(2,1)}, u32[]{:S(2)}, u32[]{:S(2)}) async-start(bf16[32,32,224]{2,1,0:T(8,128)(2,1)} %bitcast.13), calls=%async_computation.6 | async-start | bytes 1048576 | tf_op jit(solution)/shard_map/all_to_all | solution.py:79
  330.9 13.3 %copy-start.1 = (bf16[1024,1024]{1,0:T(8,128)(2,1)S(1)}, bf16[1024,1024]{1,0:T(8,128)(2,1)}, u32[]{:S(2)}) copy-start(bf16[1024,1024]{1,0:T(8,128)(2,1)} %all-gather.8.cloned.1.call-done) | copy-start | bytes 6291460
  330.9 26.9 %all-to-all-start.1 = ((bf16[32,32,224]{2,1,0:T(8,128)(2,1)}), bf16[32,32,224]{2,1,0:T(8,128)(2,1)}, u32[]{:S(2)}, u32[]{:S(2)}) async-start(bf16[32,32,224]{2,1,0:T(8,128)(2,1)} %bitcast.69), calls=%async_computation.3 | async-start | bytes 1048576 | tf_op jit(solution)/shard_map/all_to_all | solution.py:79
  344.3 1.4 copy-start.4
  344.3 1.9 copy-start.7
Sparse Core Ops, SparseCore 0:
  73.8 32.3 reduce-scatter.5
  109.0 40.1 reduce-scatter.3
  152.0 40.1 reduce-scatter.7
  194.8 45.8 all-gather.5
  243.2 40.8 all-gather.7
  286.6 40.7 all-gather.3

commit v2 on v1

v2 whole, which is shorter than its diff:
```python
import jax
import jax.numpy as jnp
from jax import lax
from jax.experimental import pallas as pl
from jax.experimental.pallas import tpu as pltpu
from jax.sharding import Mesh, PartitionSpec as P

EXPERTS = 32
CAP = 32
HALF = CAP // 2
ROWS = EXPERTS * HALF
WIDE = 224
FFW = 1024
OWN = slice(0, WIDE)
OTHER = slice(256, 256 + WIDE)
BOTH = 512
STEP = 128
N_Y = 8
BF = jnp.bfloat16
F32 = jnp.float32


def iota(shape, dim):
    return lax.broadcasted_iota(jnp.int32, shape, dim)


def dot(left, right):
    return jnp.dot(left, right, preferred_element_type=F32)


def dot_t(left, right):
    return lax.dot_general(left, right, (((1,), (1,)), ((), ())), preferred_element_type=F32)


def t_dot(left, right):
    return lax.dot_general(left, right, (((0,), (0,)), ((), ())), preferred_element_type=F32)


def shape(*dims, dtype=BF):
    return jax.ShapeDtypeStruct(dims, dtype)


def table_kernel(core_ref, ids_ref, gates_ref, pick_ref, gate_ref):
    tokens = ids_ref.shape[1]
    numbers = iota((EXPERTS, tokens), 0)
    chosen = jnp.zeros((EXPERTS, tokens), F32)
    weight = jnp.zeros((EXPERTS, tokens), F32)
    for k in range(ids_ref.shape[0]):
        hit = ids_ref[k : k + 1, :] == numbers
        chosen = chosen + jnp.where(hit, 1.0, 0.0)
        weight = weight + jnp.where(hit, gates_ref[k : k + 1, :], 0.0)
    earlier = jnp.where(iota((tokens, tokens), 0) < iota((tokens, tokens), 1), 1.0, 0.0)
    rank = dot(chosen.astype(BF), earlier.astype(BF))
    slot = jnp.where(chosen > 0.5, rank, -1.0).astype(jnp.int32) - core_ref[0] * HALF
    hit = slot[:, None, :] == iota((EXPERTS, HALF, tokens), 1)
    pick_ref[...] = jnp.where(hit, 1.0, 0.0).reshape(ROWS, tokens).astype(BF)
    gate = jnp.sum(jnp.where(hit, weight[:, None, :], 0.0), axis=2, keepdims=True)
    gate_ref[...] = gate.reshape(ROWS, 1)


def rows_kernel(pick_ref, own_ref, other_ref, out_ref):
    out_ref[...] = jnp.zeros_like(out_ref)
    out_ref[:, OWN] = dot(pick_ref[...], own_ref[...]).astype(BF)
    out_ref[:, OTHER] = dot(pick_ref[...], other_ref[...]).astype(BF)


def scaled_kernel(pick_ref, gate_ref, own_ref, other_ref, out_ref):
    out_ref[...] = jnp.zeros_like(out_ref)
    out_ref[:, OWN] = (dot(pick_ref[...], own_ref[...]) * gate_ref[...]).astype(BF)
    out_ref[:, OTHER] = (dot(pick_ref[...], other_ref[...]) * gate_ref[...]).astype(BF)


def gate_up_kernel(rows_ref, gate_own, gate_other, up_own, up_other, out_ref):
    own, other = rows_ref[:, OWN], rows_ref[:, OTHER]
    out_ref[:, :FFW] = (dot(own, gate_own[...]) + dot(other, gate_other[...])).astype(BF)
    out_ref[:, FFW:] = (dot(own, up_own[...]) + dot(other, up_other[...])).astype(BF)


def hidden_grad_kernel(dy_ref, down_own, down_other, out_ref):
    own, other = dy_ref[:, OWN], dy_ref[:, OTHER]
    out_ref[...] = (dot_t(own, down_own[...]) + dot_t(other, down_other[...])).astype(BF)


def out_kernel(hidden_ref, down_own, down_other, out_ref):
    out_ref[...] = jnp.zeros_like(out_ref)
    out_ref[:, OWN] = dot(hidden_ref[...], down_own[...]).astype(BF)
    out_ref[:, OTHER] = dot(hidden_ref[...], down_other[...]).astype(BF)


def row_grad_kernel(grads_ref, gate_own, gate_other, up_own, up_other, out_ref):
    gate, up = grads_ref[:, :FFW], grads_ref[:, FFW:]
    out_ref[...] = jnp.zeros_like(out_ref)
    out_ref[:, OWN] = (dot_t(gate, gate_own[...]) + dot_t(up, up_own[...])).astype(BF)
    out_ref[:, OTHER] = (dot_t(gate, gate_other[...]) + dot_t(up, up_other[...])).astype(BF)


def mix_kernel(pick_ref, gate_ref, back_ref, own_ref, other_ref):
    scaled = back_ref[...].astype(F32) * gate_ref[...]
    high = scaled.astype(BF)
    low = (scaled - high.astype(F32)).astype(BF)
    total = t_dot(pick_ref[...], high) + t_dot(pick_ref[...], low)
    own_ref[...] = total[:, OWN]
    other_ref[...] = total[:, OTHER]


def sum_kernel(pick_ref, back_ref, own_ref, other_ref):
    total = t_dot(pick_ref[...], back_ref[...])
    own_ref[...] = total[:, OWN]
    other_ref[...] = total[:, OTHER]


def per_rows(kernel, out_width, rows, *weights):
    whole = [pl.BlockSpec(w.shape, lambda i: (0, 0)) for w in weights]
    return pl.pallas_call(
        kernel,
        grid=(ROWS // STEP,),
        in_specs=[pl.BlockSpec((STEP, rows.shape[1]), lambda i: (i, 0))] + whole,
        out_specs=pl.BlockSpec((STEP, out_width), lambda i: (i, 0)),
        out_shape=shape(ROWS, out_width),
        compiler_params=pltpu.CompilerParams(vmem_limit_bytes=32 * 1024 * 1024),
        name=kernel.__name__,
    )(rows, *weights)


def at_once(kernel, out_shape, *args):
    return pl.pallas_call(
        kernel,
        out_shape=out_shape,
        compiler_params=pltpu.CompilerParams(vmem_limit_bytes=32 * 1024 * 1024),
        name=kernel.__name__,
    )(*args)


def to_experts(rows):
    rows = rows.reshape(EXPERTS, HALF, rows.shape[1])
    rows = lax.all_to_all(rows, "expert", split_axis=0, concat_axis=0, tiled=True)
    return rows.reshape(ROWS, -1)


def across(parts):
    return lax.all_to_all(parts, "y", split_axis=0, concat_axis=0, tiled=True)


def swap(array):
    return lax.ppermute(array, "core", [(0, 1), (1, 0)])


def after(array, *others):
    return lax.optimization_barrier((array,) + others)[0]


def body(tokens, expert_ids, gate_weights, w_gate, w_up, w_down, cotangent):
    gate_own, up_own, down_own = w_gate[0], w_up[0], w_down[0]
    core = lax.axis_index("core").reshape(1)
    tokens_other, cotangent_other = swap(tokens), swap(cotangent)
    pick, slot_gate = pl.pallas_call(
        table_kernel,
        in_specs=[pl.BlockSpec(memory_space=pltpu.SMEM)]
        + [pl.BlockSpec(memory_space=pltpu.VMEM)] * 2,
        out_shape=[shape(ROWS, tokens.shape[0]), shape(ROWS, 1, dtype=F32)],
        name="table_kernel",
    )(core, expert_ids.T, gate_weights.T)

    send_in = at_once(rows_kernel, shape(ROWS, BOTH), pick, tokens, tokens_other)
    gate_other = swap(after(gate_own, send_in))
    up_other = swap(after(up_own, send_in))
    down_other = swap(after(down_own, send_in))
    rows_in = to_experts(send_in)
    send_dy = at_once(
        scaled_kernel, shape(ROWS, BOTH), pick, slot_gate, cotangent, cotangent_other
    )
    rows_dy = to_experts(after(send_dy, rows_in))

    gate_up = per_rows(gate_up_kernel, 2 * FFW, rows_in, gate_own, gate_other, up_own, up_other)
    sums = lax.psum_scatter(gate_up, "y", scatter_dimension=0, tiled=True).astype(F32)
    rows_dy = after(rows_dy, gate_up)
    parts = per_rows(hidden_grad_kernel, FFW, rows_dy, down_own, down_other)
    parts = across(parts.reshape(N_Y, ROWS // N_Y, FFW))
    hidden_grad = jnp.sum(parts.astype(F32), axis=0)

    gate_sum, up_sum = sums[:, :FFW], sums[:, FFW:]
    logistic = jax.nn.sigmoid(gate_sum)
    hidden = (gate_sum * logistic * up_sum).astype(BF)
    up_grad = (hidden_grad * gate_sum * logistic).astype(BF)
    gate_grad = (hidden_grad * up_sum * logistic * (1.0 + gate_sum * (1.0 - logistic))).astype(BF)
    shard = jnp.concatenate([gate_grad, up_grad], axis=1)
    grads = lax.all_gather(shard, "y", axis=0, tiled=True)
    hidden = across(jnp.broadcast_to(after(hidden, shard), (N_Y,) + hidden.shape))
    hidden = hidden.reshape(ROWS, FFW)

    out_rows = per_rows(out_kernel, BOTH, hidden, down_own, down_other)
    back_out = to_experts(out_rows)
    part_shape = [shape(*tokens.shape, dtype=F32)] * 2
    mixed, mixed_other = at_once(mix_kernel, part_shape, pick, slot_gate, back_out)
    mixed = (mixed + swap(mixed_other)).astype(BF)

    row_grad = per_rows(row_grad_kernel, BOTH, grads, gate_own, gate_other, up_own, up_other)
    back_grad = to_experts(row_grad)

    down_part = swap(t_dot(hidden, rows_dy[:, OTHER]).astype(BF))
    grad_down = (t_dot(hidden, rows_dy[:, OWN]) + down_part.astype(F32)).astype(BF)
    gate_part = swap(t_dot(rows_in[:, OTHER], grads[:, :FFW]).astype(BF))
    up_part = swap(t_dot(rows_in[:, OTHER], grads[:, FFW:]).astype(BF))
    grad_gate = (t_dot(rows_in[:, OWN], grads[:, :FFW]) + gate_part.astype(F32)).astype(BF)
    grad_up = (t_dot(rows_in[:, OWN], grads[:, FFW:]) + up_part.astype(F32)).astype(BF)

    token_grad, grad_other = at_once(sum_kernel, part_shape, pick, back_grad)
    token_grad = (token_grad + swap(grad_other)).astype(BF)
    return mixed, token_grad, grad_gate[None], grad_up[None], grad_down[None]


def solution(mesh):
    fine = Mesh(mesh.devices.reshape(N_Y, 2, EXPERTS), ("y", "core", "expert"))
    dp = ("y", "core")
    placed = (
        P("expert", dp),
        P("expert", None),
        P("expert", None),
        P("expert", dp, None),
        P("expert", dp, None),
        P("expert", None, dp),
        P("expert", dp),
    )
    return jax.shard_map(
        body,
        mesh=fine,
        in_specs=placed,
        out_specs=(
            P("expert", dp),
            P("expert", dp),
            P("expert", dp, None),
            P("expert", dp, None),
            P("expert", None, dp),
        ),
        check_vma=False,
    )
```

time: 369 us -> 230 us (0.62)
  waiting for transfers between devices: 252 us -> 37.7 us
  blocking collectives: 30.1 us -> 70.8 us
  starting transfers between devices: 36.1 us -> 66 us
  matrix products: 18.6 us -> 10.1 us
  Pallas kernels: 7.53 us -> 15.1 us
  local copies, waits for them, and re-layouts: 6.29 us -> 11.2 us
    all_gather x3 -> x1, waiting for transfers between devices: 116 us -> 0.02 us  [body(): grads = lax.all_gather(shard, 'y', axis=0, tiled=True)]
    reduce_scatter x3 -> x1, waiting for transfers between devices: 105 us -> 0.02 us  [body(): lax.psum_scatter(gate_up, 'y', scatter_dimension=0, tiled=True).astype(F32)]
    all_to_all x1 -> x2, blocking collectives: 30.1 us -> 70.8 us  [across(): return lax.all_to_all(parts, 'y', split_axis=0, concat_axis=0, tiled=True)]
    ppermute x3 -> x10, starting transfers between devices: 10.4 us -> 42.2 us  [swap(): return lax.ppermute(array, 'core', [(0, 1), (1, 0)])]
    all_to_all x3 -> x4, waiting for transfers between devices: 22.8 us -> 34.9 us  [to_experts(): lax.all_to_all(rows, 'expert', split_axis=0, concat_axis=0, tiled=True)]
    dot_general x12 -> x6, matrix products: 18.6 us -> 10.1 us  [t_dot(): lax.dot_general(left, right, (((0,), (0,)), ((), ())), preferred_element_...]
    unnamed x18 -> x35, local copies, waits for them, and re-layouts: 3.32 us -> 11.1 us
    pallas_call x3 -> x9, Pallas kernels: 7.53 us -> 15.1 us  [the longest x4 9.85 us: per_rows(): pl.pallas_call(kernel, grid=(ROWS // STEP,), in_specs=[pl.BlockSpec((STEP...]
  transfers between devices with their start and end apart: 12 -> 16, of which waited for: 11 -> 6; matrix products, arithmetic and copies ran while one was open for 5% -> 5% of each run, Pallas kernels for 1% -> 5%
where the time goes in v2:
time: 230 us; the launch traced here: 229 us
  blocking collectives  70.8 us (31%)
  starting transfers between devices  66 us (29%)
  waiting for transfers between devices  37.7 us (16%)
  Pallas kernels  15.1 us (7%)
  between operations  14.3 us (6%)
  local copies, waits for them, and re-layouts  11.2 us (5%)
  matrix products  10.1 us (4%)
  other arithmetic  3.31 us (1%)
    all_to_all x2, blocking collectives, across(): return lax.all_to_all(parts, 'y', split_axis=0, concat_axis=0, tiled=True)  70.8 us
    ppermute x10, starting transfers between devices, swap(): return lax.ppermute(array, 'core', [(0, 1), (1, 0)])  42.2 us
    all_to_all x4, waiting for transfers between devices, to_experts(): lax.all_to_all(rows, 'expert', split_axis=0, concat_axis=0, tiled=True)  34.9 us
    all_to_all x4, starting transfers between devices, to_experts(): lax.all_to_all(rows, 'expert', split_axis=0, concat_axis=0, tiled=True)  23.8 us
    unnamed x35, local copies, waits for them, and re-layouts  11.1 us
    dot_general x6, matrix products, t_dot(): lax.dot_general(left, right, (((0,), (0,)), ((), ())), preferred_element_...  10.1 us
    pallas_call x4, Pallas kernels, per_rows(): pl.pallas_call(kernel, grid=(ROWS // STEP,), in_specs=[pl.BlockSpec((STEP...  9.85 us
  transfers between devices with their start and end apart: 16, of which 6 were waited for; matrix products, arithmetic and copies ran while one was open for 5% of the time, Pallas kernels for 5%

profile of v2, /device:TPU:1, one launch (start us, length us, event | category | flops | bytes accessed | tf_op | source)
XLA Modules:
  0.0 228.6 jit_solution(6386336654996979175)
XLA Ops:
  7.2 8.8 %collective-permute-start = (bf16[64,224]{1,0:T(8,128)(2,1)}, bf16[64,224]{1,0:T(8,128)(2,1)S(1)}, u32[]{:S(2)}, u32[]{:S(2)}) collective-permute-start(bf16[64,224]{1,0:T(8,128)(2,1)} %own_ref.2), channel_id=1, source_target_pairs={{0,32},{32,0},{1,33},{33,1},{2,34},{34,2},{3,35},{35,3},{4,36},{36... | collective-permute-start | bytes 86024 | tf_op jit(solution)/shard_map/ppermute | solution.py:145
  20.4 7.5 %all-to-all-start = ((bf16[32,16,512]{2,1,0:T(8,128)(2,1)}), bf16[32,16,512]{2,1,0:T(8,128)(2,1)S(1)}, u32[]{:S(2)}, u32[]{:S(2)}) async-start(bf16[32,16,512]{2,1,0:T(8,128)(2,1)} %bitcast.3), calls=%async_computation | async-start | bytes 1048576 | tf_op jit(solution)/shard_map/all_to_all | solution.py:136
  28.0 2.2 collective-permute-start.1
  30.2 2.1 collective-permute-start.2
  34.1 10.6 %all-to-all-done = bf16[32,16,512]{2,1,0:T(8,128)(2,1)S(1)} async-done(((bf16[32,16,512]{2,1,0:T(8,128)(2,1)}), bf16[32,16,512]{2,1,0:T(8,128)(2,1)S(1)}, u32[]{:S(2)}, u32[]{:S(2)}) %all-to-all-start) | async-done | bytes 524320 | tf_op jit(solution)/shard_map/all_to_all | solution.py:136
  46.8 3.0 %gate_up_kernel.1 = bf16[512,2048]{1,0:T(8,128)(2,1)} custom-call(bf16[512,512]{1,0:T(8,128)(2,1)S(1)} %bitcast.34, bf16[224,1024]{1,0:T(8,128)(2,1)S(1)} %bitcast.43, bf16[224,1024]{1,0:T(8,128)(2,1)S(1)} %collective-permute-done.1.gate_other, bf16[224,1024]{1,0:T(8,128)(2,1)S(1)} %bitcast.46, bf16[224,1024]{1,0:T(8,128)(2,1)S(1)} %collective-permute-done.2.up_other), custom_call_target="tpu_custom_call" | custom-call | tf_op jit(solution)/shard_map/gate_up_kernel/pallas_call | solution.py:114
  50.5 3.8 %collective-permute-start.3 = (bf16[64,224]{1,0:T(8,128)(2,1)S(1)}, bf16[64,224]{1,0:T(8,128)(2,1)S(1)}, u32[]{:S(2)}, u32[]{:S(2)}) collective-permute-start(bf16[64,224]{1,0:T(8,128)(2,1)S(1)} %copy-done.15), channel_id=1, source_target_pairs={{0,32},{32,0},{1,33},{33,1},{2,34},{34,2},{3,35},{35,3},{4,36},{36... | collective-permute-start | bytes 86024 | tf_op jit(solution)/shard_map/ppermute | solution.py:145
  56.2 4.4 %all-to-all-start.1 = ((bf16[32,16,512]{2,1,0:T(8,128)(2,1)}), bf16[32,16,512]{2,1,0:T(8,128)(2,1)S(1)}, u32[]{:S(2)}, u32[]{:S(2)}) async-start(bf16[32,16,512]{2,1,0:T(8,128)(2,1)} %bitcast.7), calls=%async_computation.2 | async-start | bytes 1048576 | tf_op jit(solution)/shard_map/all_to_all | solution.py:136
  60.9 2.5 %collective-permute-start.4 = (bf16[1024,224]{1,0:T(8,128)(2,1)S(1)}, bf16[1024,224]{1,0:T(8,128)(2,1)S(1)}, u32[]{:S(2)}, u32[]{:S(2)}) collective-permute-start(bf16[1024,224]{1,0:T(8,128)(2,1)S(1)} %bitcast.27), channel_id=1, source_target_pairs={{0,32},{32,0},{1,33},{33,1},{2,34},{34,2},{3,35},{35,3},{4,36},{36... | collective-permute-start | bytes 1376264 | tf_op jit(solution)/shard_map/ppermute | solution.py:145
  63.4 13.8 %all-to-all-done.1 = bf16[32,16,512]{2,1,0:T(8,128)(2,1)S(1)} async-done(((bf16[32,16,512]{2,1,0:T(8,128)(2,1)}), bf16[32,16,512]{2,1,0:T(8,128)(2,1)S(1)}, u32[]{:S(2)}, u32[]{:S(2)}) %all-to-all-start.1) | async-done | bytes 524320 | tf_op jit(solution)/shard_map/all_to_all | solution.py:136
  79.1 33.6 %all_to_all.30 = bf16[8,64,1024]{2,1,0:T(8,128)(2,1)S(1)} all-to-all(bf16[8,64,1024]{2,1,0:T(8,128)(2,1)S(1)} %bitcast.30), channel_id=1, replica_groups=mesh['y'=8,'core'=2,'expert'=32] {'y'}, dimensions={0} | all-to-all | bytes 2097152 | tf_op jit(solution)/shard_map/all_to_all | solution.py:141
  115.0 37.3 %all_to_all.31 = bf16[8,64,1024]{2,1,0:T(8,128)(2,1)S(1)} all-to-all(bf16[8,64,1024]{2,1,0:T(8,128)(2,1)S(1)} %broadcast_in_dim.12), channel_id=1, replica_groups=mesh['y'=8,'core'=2,'expert'=32] {'y'}, dimensions={0} | all-to-all | bytes 2097152 | tf_op jit(solution)/shard_map/all_to_all | solution.py:141
  154.3 7.9 %all-to-all-start.4 = ((bf16[32,16,512]{2,1,0:T(8,128)(2,1)}), bf16[32,16,512]{2,1,0:T(8,128)(2,1)S(1)}, u32[]{:S(2)}, u32[]{:S(2)}) async-start(bf16[32,16,512]{2,1,0:T(8,128)(2,1)} %bitcast.39), calls=%async_computation.5 | async-start | bytes 1048576 | tf_op jit(solution)/shard_map/all_to_all | solution.py:136
  163.5 6.2 %collective-permute-start.9 = (bf16[1024,224]{0,1:T(8,128)(2,1)}, bf16[1024,224]{0,1:T(8,128)(2,1)}, u32[]{:S(2)}, u32[]{:S(2)}) collective-permute-start(bf16[1024,224]{0,1:T(8,128)(2,1)} %convolution_convert_fusion), channel_id=1, source_target_pairs={{0,32},{32,0},{1,33},{33,1},{2,34},{34,2},{3,35},{35,3},{4,36},{36... | collective-permute-start | bytes 1376264 | tf_op jit(solution)/shard_map/ppermute | solution.py:145
  169.7 5.3 %all-to-all-done.4 = bf16[32,16,512]{2,1,0:T(8,128)(2,1)S(1)} async-done(((bf16[32,16,512]{2,1,0:T(8,128)(2,1)}), bf16[32,16,512]{2,1,0:T(8,128)(2,1)S(1)}, u32[]{:S(2)}, u32[]{:S(2)}) %all-to-all-start.4) | async-done | bytes 524320 | tf_op jit(solution)/shard_map/all_to_all | solution.py:136
  176.1 8.5 %collective-permute-start.5 = (f32[64,224]{1,0:T(8,128)}, f32[64,224]{1,0:T(8,128)S(1)}, u32[]{:S(2)}, u32[]{:S(2)}) collective-permute-start(f32[64,224]{1,0:T(8,128)} %get-tuple-element.26), channel_id=1, source_target_pairs={{0,32},{32,0},{1,33},{33,1},{2,34},{34,2},{3,35},{35,3},{4,36},{36... | collective-permute-start | bytes 172040 | tf_op jit(solution)/shard_map/ppermute | solution.py:145
  190.3 3.7 %row_grad_kernel.1 = bf16[512,512]{1,0:T(8,128)(2,1)} custom-call(bf16[512,2048]{1,0:T(8,128)(2,1)S(1)} %copy-done.3, bf16[224,1024]{1,0:T(8,128)(2,1)S(1)} %bitcast.44, bf16[224,1024]{1,0:T(8,128)(2,1)S(1)} %copy-done.10, bf16[224,1024]{1,0:T(8,128)(2,1)S(1)} %bitcast.47, bf16[224,1024]{1,0:T(8,128)(2,1)S(1)} %copy-done.12), custom_call_target="tpu_custom_call" | custom-call | tf_op jit(solution)/shard_map/row_grad_kernel/pallas_call | solution.py:114
  194.0 3.9 %all-to-all-start.5 = ((bf16[32,16,512]{2,1,0:T(8,128)(2,1)}), bf16[32,16,512]{2,1,0:T(8,128)(2,1)S(1)}, u32[]{:S(2)}, u32[]{:S(2)}) async-start(bf16[32,16,512]{2,1,0:T(8,128)(2,1)} %bitcast.14), calls=%async_computation.6 | async-start | bytes 1048576 | tf_op jit(solution)/shard_map/all_to_all | solution.py:136
  199.7 2.1 collective-permute-start.8
  203.0 2.2 collective-permute-start.7
  205.3 2.2 fusion.8
  209.3 5.3 %all-to-all-done.5 = bf16[32,16,512]{2,1,0:T(8,128)(2,1)S(1)} async-done(((bf16[32,16,512]{2,1,0:T(8,128)(2,1)}), bf16[32,16,512]{2,1,0:T(8,128)(2,1)S(1)}, u32[]{:S(2)}, u32[]{:S(2)}) %all-to-all-start.5) | async-done | bytes 524320 | tf_op jit(solution)/shard_map/all_to_all | solution.py:136
  214.9 3.8 %collective-permute-start.6 = (f32[64,224]{1,0:T(8,128)S(1)}, f32[64,224]{1,0:T(8,128)S(1)}, u32[]{:S(2)}, u32[]{:S(2)}) collective-permute-start(f32[64,224]{1,0:T(8,128)S(1)} %get-tuple-element.28), channel_id=1, source_target_pairs={{0,32},{32,0},{1,33},{33,1},{2,34},{34,2},{3,35},{35,3},{4,36},{36... | collective-permute-start | bytes 172040 | tf_op jit(solution)/shard_map/ppermute | solution.py:145
  218.7 2.4 %fusion.6 = bf16[1,224,1024]{2,1,0:T(8,128)(2,1)} fusion(bf16[224,1024]{1,0:T(8,128)(2,1)S(1)} %collective-permute-done.7, bf16[512,2048]{1,0:T(8,128)(2,1)} %all-gather.2.cloned.1.call-done.grads_ref, bf16[512,512]{1,0:T(8,128)(2,1)S(1)} %bitcast.38), kind=kOutput, calls=%fused_computation.13 | convolution fusion | flops 235569152 | bytes 2228224 | tf_op jit(solution)/shard_map/dot_general | solution.py:36
  (69 shorter events, 31.1 us)
Async XLA Ops:
  7.2 10.5 %collective-permute-start = (bf16[64,224]{1,0:T(8,128)(2,1)}, bf16[64,224]{1,0:T(8,128)(2,1)S(1)}, u32[]{:S(2)}, u32[]{:S(2)}) collective-permute-start(bf16[64,224]{1,0:T(8,128)(2,1)} %own_ref.2), channel_id=1, source_target_pairs={{0,32},{32,0},{1,33},{33,1},{2,34},{34,2},{3,35},{35,3},{4,36},{36... | collective-permute-start | bytes 86024 | tf_op jit(solution)/shard_map/ppermute | solution.py:145
  20.4 24.3 %all-to-all-start = ((bf16[32,16,512]{2,1,0:T(8,128)(2,1)}), bf16[32,16,512]{2,1,0:T(8,128)(2,1)S(1)}, u32[]{:S(2)}, u32[]{:S(2)}) async-start(bf16[32,16,512]{2,1,0:T(8,128)(2,1)} %bitcast.3), calls=%async_computation | async-start | bytes 1048576 | tf_op jit(solution)/shard_map/all_to_all | solution.py:136
  27.9 85.0 %reduce-scatter.2.cloned.1.call-start = ((), (), s32[]{:S(2)}) async-start(), calls=%async_computation.7 | async-start | bytes 2359296 | tf_op jit(solution)/shard_map/reduce_scatter | solution.py:175
  28.0 4.3 %collective-permute-start.1 = (bf16[224,1024]{1,0:T(8,128)(2,1)}, bf16[224,1024]{1,0:T(8,128)(2,1)S(1)}, u32[]{:S(2)}, u32[]{:S(2)}) collective-permute-start(bf16[224,1024]{1,0:T(8,128)(2,1)} %bitcast.42), channel_id=1, source_target_pairs={{0,32},{32,0},{1,33},{33,1},{2,34},{34,2},{3,35},{35,3},{4,36},{36... | collective-permute-start | bytes 1376264 | tf_op jit(solution)/shard_map/ppermute | solution.py:145
  30.2 3.9 %collective-permute-start.2 = (bf16[224,1024]{1,0:T(8,128)(2,1)}, bf16[224,1024]{1,0:T(8,128)(2,1)S(1)}, u32[]{:S(2)}, u32[]{:S(2)}) collective-permute-start(bf16[224,1024]{1,0:T(8,128)(2,1)} %bitcast.45), channel_id=1, source_target_pairs={{0,32},{32,0},{1,33},{33,1},{2,34},{34,2},{3,35},{35,3},{4,36},{36... | collective-permute-start | bytes 1376264 | tf_op jit(solution)/shard_map/ppermute | solution.py:145
  32.3 17.4 %copy-start.9 = (bf16[224,1024]{1,0:T(8,128)(2,1)}, bf16[224,1024]{1,0:T(8,128)(2,1)S(1)}, u32[]{:S(2)}) copy-start(bf16[224,1024]{1,0:T(8,128)(2,1)S(1)} %collective-permute-done.1.gate_other) | copy-start | bytes 1376260
  34.1 15.6 %copy-start.11 = (bf16[224,1024]{1,0:T(8,128)(2,1)}, bf16[224,1024]{1,0:T(8,128)(2,1)S(1)}, u32[]{:S(2)}) copy-start(bf16[224,1024]{1,0:T(8,128)(2,1)S(1)} %collective-permute-done.2.up_other) | copy-start | bytes 1376260
  44.7 1.0 copy-start.5
  49.7 5.4 %copy-start.2 = (bf16[512,64]{1,0:T(8,128)(2,1)S(1)}, bf16[512,64]{1,0:T(8,128)(2,1)}, u32[]{:S(2)}) copy-start(bf16[512,64]{1,0:T(8,128)(2,1)} %get-tuple-element.17.pick_ref) | copy-start | bytes 196612
  49.7 5.4 %copy-start.13 = (f32[512,1]{1,0:T(8,128)S(1)}, f32[512,1]{1,0:T(8,128)}, u32[]{:S(2)}) copy-start(f32[512,1]{1,0:T(8,128)} %get-tuple-element.18.gate_ref) | copy-start | bytes 6148
  49.8 10.9 %copy-start.16 = (bf16[1,1024,224]{1,2,0:T(8,128)(2,1)S(1)}, bf16[1,1024,224]{1,2,0:T(8,128)(2,1)}, u32[]{:S(2)}) copy-start(bf16[1,1024,224]{1,2,0:T(8,128)(2,1)} %param.12) | copy-start | bytes 1376260
  50.5 4.6 %collective-permute-start.3 = (bf16[64,224]{1,0:T(8,128)(2,1)S(1)}, bf16[64,224]{1,0:T(8,128)(2,1)S(1)}, u32[]{:S(2)}, u32[]{:S(2)}) collective-permute-start(bf16[64,224]{1,0:T(8,128)(2,1)S(1)} %copy-done.15), channel_id=1, source_target_pairs={{0,32},{32,0},{1,33},{33,1},{2,34},{34,2},{3,35},{35,3},{4,36},{36... | collective-permute-start | bytes 86024 | tf_op jit(solution)/shard_map/ppermute | solution.py:145
  56.2 21.0 %all-to-all-start.1 = ((bf16[32,16,512]{2,1,0:T(8,128)(2,1)}), bf16[32,16,512]{2,1,0:T(8,128)(2,1)S(1)}, u32[]{:S(2)}, u32[]{:S(2)}) async-start(bf16[32,16,512]{2,1,0:T(8,128)(2,1)} %bitcast.7), calls=%async_computation.2 | async-start | bytes 1048576 | tf_op jit(solution)/shard_map/all_to_all | solution.py:136
  60.6 124.0 %all-gather.2.cloned.1.call-start = ((), (), s32[]{:S(2)}) async-start(), calls=%async_computation.8 | async-start | bytes 2359296 | tf_op jit(solution)/shard_map/all_gather | solution.py:187
  60.9 16.3 %collective-permute-start.4 = (bf16[1024,224]{1,0:T(8,128)(2,1)S(1)}, bf16[1024,224]{1,0:T(8,128)(2,1)S(1)}, u32[]{:S(2)}, u32[]{:S(2)}) collective-permute-start(bf16[1024,224]{1,0:T(8,128)(2,1)S(1)} %bitcast.27), channel_id=1, source_target_pairs={{0,32},{32,0},{1,33},{33,1},{2,34},{34,2},{3,35},{35,3},{4,36},{36... | collective-permute-start | bytes 1376264 | tf_op jit(solution)/shard_map/ppermute | solution.py:145
  154.3 20.7 %all-to-all-start.4 = ((bf16[32,16,512]{2,1,0:T(8,128)(2,1)}), bf16[32,16,512]{2,1,0:T(8,128)(2,1)S(1)}, u32[]{:S(2)}, u32[]{:S(2)}) async-start(bf16[32,16,512]{2,1,0:T(8,128)(2,1)} %bitcast.39), calls=%async_computation.5 | async-start | bytes 1048576 | tf_op jit(solution)/shard_map/all_to_all | solution.py:136
  163.5 41.8 %collective-permute-start.9 = (bf16[1024,224]{0,1:T(8,128)(2,1)}, bf16[1024,224]{0,1:T(8,128)(2,1)}, u32[]{:S(2)}, u32[]{:S(2)}) collective-permute-start(bf16[1024,224]{0,1:T(8,128)(2,1)} %convolution_convert_fusion), channel_id=1, source_target_pairs={{0,32},{32,0},{1,33},{33,1},{2,34},{34,2},{3,35},{35,3},{4,36},{36... | collective-permute-start | bytes 1376264 | tf_op jit(solution)/shard_map/ppermute | solution.py:145
  176.1 31.4 %collective-permute-start.5 = (f32[64,224]{1,0:T(8,128)}, f32[64,224]{1,0:T(8,128)S(1)}, u32[]{:S(2)}, u32[]{:S(2)}) collective-permute-start(f32[64,224]{1,0:T(8,128)} %get-tuple-element.26), channel_id=1, source_target_pairs={{0,32},{32,0},{1,33},{33,1},{2,34},{34,2},{3,35},{35,3},{4,36},{36... | collective-permute-start | bytes 172040 | tf_op jit(solution)/shard_map/ppermute | solution.py:145
  184.6 1.6 copy-start.3
  194.0 20.6 %all-to-all-start.5 = ((bf16[32,16,512]{2,1,0:T(8,128)(2,1)}), bf16[32,16,512]{2,1,0:T(8,128)(2,1)S(1)}, u32[]{:S(2)}, u32[]{:S(2)}) async-start(bf16[32,16,512]{2,1,0:T(8,128)(2,1)} %bitcast.14), calls=%async_computation.6 | async-start | bytes 1048576 | tf_op jit(solution)/shard_map/all_to_all | solution.py:136
  197.9 3.9 %copy-start.4 = (bf16[512,2048]{1,0:T(8,128)(2,1)S(1)}, bf16[512,2048]{1,0:T(8,128)(2,1)}, u32[]{:S(2)}) copy-start(bf16[512,2048]{1,0:T(8,128)(2,1)} %all-gather.2.cloned.1.call-done.grads_ref) | copy-start | bytes 6291460
  199.7 8.4 %collective-permute-start.8 = (bf16[224,1024]{1,0:T(8,128)(2,1)S(1)}, bf16[224,1024]{1,0:T(8,128)(2,1)S(1)}, u32[]{:S(2)}, u32[]{:S(2)}) collective-permute-start(bf16[224,1024]{1,0:T(8,128)(2,1)S(1)} %convolution_convert_fusion.1), channel_id=1, source_target_pairs={{0,32},{32,0},{1,33},{33,1},{2,34},{34,2},{3,35},{35,3},{4,36},{36... | collective-permute-start | bytes 1376264 | tf_op jit(solution)/shard_map/ppermute | solution.py:145
  203.0 15.6 %collective-permute-start.7 = (bf16[224,1024]{1,0:T(8,128)(2,1)}, bf16[224,1024]{1,0:T(8,128)(2,1)S(1)}, u32[]{:S(2)}, u32[]{:S(2)}) collective-permute-start(bf16[224,1024]{1,0:T(8,128)(2,1)} %convolution_convert_fusion.2), channel_id=1, source_target_pairs={{0,32},{32,0},{1,33},{33,1},{2,34},{34,2},{3,35},{35,3},{4,36},{36... | collective-permute-start | bytes 1376264 | tf_op jit(solution)/shard_map/ppermute | solution.py:145
  214.9 6.2 %collective-permute-start.6 = (f32[64,224]{1,0:T(8,128)S(1)}, f32[64,224]{1,0:T(8,128)S(1)}, u32[]{:S(2)}, u32[]{:S(2)}) collective-permute-start(f32[64,224]{1,0:T(8,128)S(1)} %get-tuple-element.28), channel_id=1, source_target_pairs={{0,32},{32,0},{1,33},{33,1},{2,34},{34,2},{3,35},{35,3},{4,36},{36... | collective-permute-start | bytes 172040 | tf_op jit(solution)/shard_map/ppermute | solution.py:145
  (9 other events, 8.3 us)
Sparse Core Ops, SparseCore 0:
  49.9 37.9 reduce-scatter.1
  115.0 52.1 all-gather.1

commit v3 on v2

v3 whole, which is shorter than its diff:
```python
import jax
import jax.numpy as jnp
from jax import lax
from jax.experimental import pallas as pl
from jax.experimental.pallas import tpu as pltpu
from jax.sharding import Mesh, PartitionSpec as P

EXPERTS = 32
CAP = 32
HALF = CAP // 2
ROWS = EXPERTS * HALF
WIDE = 224
PAIR = 2 * WIDE
STACK = 512
JOIN = 2 * PAIR - STACK
FFW = 1024
N_Y = 8
SHARD = ROWS // N_Y
BF = jnp.bfloat16
F32 = jnp.float32
VMEM_LIMIT = 24 * 1024 * 1024


def iota(shape, dim):
    return lax.broadcasted_iota(jnp.int32, shape, dim)


def dot(left, right):
    return jnp.dot(left, right, preferred_element_type=F32)


def dot_t(left, right):
    return lax.dot_general(left, right, (((1,), (1,)), ((), ())), preferred_element_type=F32)


def t_dot(left, right):
    return lax.dot_general(left, right, (((0,), (0,)), ((), ())), preferred_element_type=F32)


def shape(*dims, dtype=BF):
    return jax.ShapeDtypeStruct(dims, dtype)


def start(copies):
    for copy in copies:
        copy.start()


def wait(copies):
    for copy in copies:
        copy.wait()


def copies_of(pairs, sems):
    return [pltpu.make_async_copy(src, dst, sems.at[i]) for i, (src, dst) in enumerate(pairs)]


def send_kernel(
    core_ref,
    ids_hbm,
    gates_hbm,
    tokens_hbm,
    cotangent_hbm,
    others_hbm,
    pick_ref,
    gate_ref,
    out_ref,
    ids_ref,
    gates_ref,
    tokens_ref,
    cotangent_ref,
    others_ref,
    sems,
):
    loads = copies_of(
        (
            (ids_hbm, ids_ref),
            (gates_hbm, gates_ref),
            (tokens_hbm, tokens_ref),
            (cotangent_hbm, cotangent_ref),
            (others_hbm, others_ref),
        ),
        sems,
    )
    start(loads)
    wait(loads[:2])
    tokens = ids_ref.shape[1]
    numbers = iota((EXPERTS, tokens), 0)
    chosen = jnp.zeros((EXPERTS, tokens), F32)
    weight = jnp.zeros((EXPERTS, tokens), F32)
    for k in range(ids_ref.shape[0]):
        hit = ids_ref[k : k + 1, :] == numbers
        chosen = chosen + jnp.where(hit, 1.0, 0.0)
        weight = weight + jnp.where(hit, gates_ref[k : k + 1, :], 0.0)
    earlier = jnp.where(iota((tokens, tokens), 0) < iota((tokens, tokens), 1), 1.0, 0.0)
    rank = dot(chosen.astype(BF), earlier.astype(BF))
    slot = jnp.where(chosen > 0.5, rank, -1.0).astype(jnp.int32) - core_ref[0] * HALF
    hit = slot[:, None, :] == iota((EXPERTS, HALF, tokens), 1)
    pick = jnp.where(hit, 1.0, 0.0).reshape(ROWS, tokens).astype(BF)
    gate = jnp.sum(jnp.where(hit, weight[:, None, :], 0.0), axis=2, keepdims=True)
    gate = gate.reshape(ROWS, 1)
    pick_ref[...] = pick
    gate_ref[...] = gate
    wait(loads[2:])
    features = jnp.concatenate(
        [tokens_ref[...], others_ref[:tokens], cotangent_ref[...], others_ref[tokens:]], axis=1
    )
    rows = dot(pick, features)
    scale = jnp.where(iota((1, 2 * PAIR), 1) < PAIR, 1.0, gate)
    out_ref[...] = (rows * scale).astype(BF)


def sums_kernel(rows, gate, up, down, out_hbm, out, sems):
    columns = [pl.ds(i * FFW, FFW) for i in range(3)]
    stores = copies_of([(out.at[:, c], out_hbm.at[:, c]) for c in columns], sems)
    for i, weights in enumerate((gate, up, down)):
        left = rows[:, :STACK] if i < 2 else rows[:, 2 * PAIR - STACK :]
        out[:, i * FFW : (i + 1) * FFW] = dot(left, weights[...]).astype(BF)
        stores[i].start()
    wait(stores)


def shard_kernel(sums_hbm, out_hbm, sums, out, in_sems, out_sems):
    columns = [pl.ds(i * FFW, FFW) for i in range(3)]
    loads = copies_of([(sums_hbm.at[:, c], sums.at[:, c]) for c in columns], in_sems)
    stores = copies_of([(out.at[:, c], out_hbm.at[:, c]) for c in columns], out_sems)
    start(loads)
    wait(loads[:2])
    gate_sum = sums[:, :FFW].astype(F32)
    up_sum = sums[:, FFW : 2 * FFW].astype(F32)
    logistic = jax.nn.sigmoid(gate_sum)
    silu = gate_sum * logistic
    out[:, :FFW] = (silu * up_sum).astype(BF)
    stores[0].start()
    loads[2].wait()
    total = sums[:, 2 * FFW :].astype(F32)
    slope = logistic * (1.0 + gate_sum * (1.0 - logistic))
    out[:, FFW : 2 * FFW] = (total * up_sum * slope).astype(BF)
    stores[1].start()
    out[:, 2 * FFW :] = (total * silu).astype(BF)
    stores[2].start()
    wait(stores)


def back_kernel(full_hbm, gate, up, down, out_hbm, full, out, in_sems, out_sems):
    half = ROWS // 2
    parts = [pl.ds(i * half, half) for i in range(2)]
    columns = [pl.ds(i * FFW, FFW) for i in range(3)]
    blocks = [(p, c) for p in parts for c in columns]
    loads = copies_of([(full_hbm.at[p, c], full.at[p, c]) for p, c in blocks], in_sems)
    stores = copies_of([(out.at[p], out_hbm.at[p]) for p in parts], out_sems)
    start(loads)
    for i in range(2):
        rows = slice(i * half, (i + 1) * half)
        loads[3 * i].wait()
        result = dot_t(full[rows, :FFW], down[...])
        loads[3 * i + 1].wait()
        grad = dot_t(full[rows, FFW : 2 * FFW], gate[...])
        loads[3 * i + 2].wait()
        grad = grad + dot_t(full[rows, 2 * FFW :], up[...])
        out[rows, :JOIN] = grad[:, :JOIN].astype(BF)
        out[rows, JOIN:STACK] = (grad[:, JOIN:] + result[:, : STACK - JOIN]).astype(BF)
        out[rows, STACK:] = result[:, STACK - JOIN :].astype(BF)
        stores[i].start()
    wait(stores)


def mix_kernel(pick_ref, gate_ref, back_ref, out_ref):
    scaled = back_ref[:, JOIN:].astype(F32) * gate_ref[...]
    high = scaled.astype(BF)
    low = (scaled - high.astype(F32)).astype(BF)
    mixed = t_dot(pick_ref[...], high) + t_dot(pick_ref[...], low)
    grad = t_dot(pick_ref[...], back_ref[:, :STACK])
    out_ref[:, :JOIN] = grad[:, :JOIN]
    first = iota((1, STACK - JOIN), 1) < PAIR - JOIN
    out_ref[:, JOIN:STACK] = jnp.where(first, grad[:, JOIN:], mixed[:, : STACK - JOIN])
    out_ref[:, STACK:] = mixed[:, STACK - JOIN :]


HBM_SPEC = pl.BlockSpec(memory_space=pltpu.HBM)
VMEM_SPEC = pl.BlockSpec(memory_space=pltpu.VMEM)
SMEM_SPEC = pl.BlockSpec(memory_space=pltpu.SMEM)


def call(kernel, out_shape, *args, **kwargs):
    return pl.pallas_call(
        kernel,
        out_shape=out_shape,
        compiler_params=pltpu.CompilerParams(vmem_limit_bytes=VMEM_LIMIT),
        name=kernel.__name__,
        **kwargs,
    )(*args)


def in_hbm(*arrays):
    return [pltpu.with_memory_space_constraint(a, pltpu.HBM) for a in arrays]


def in_vmem(*arrays):
    return [pltpu.with_memory_space_constraint(a, pltpu.VMEM) for a in arrays]


def buffers(*arrays):
    return [pltpu.VMEM(a.shape, a.dtype) for a in arrays]


def semaphores(*counts):
    return [pltpu.SemaphoreType.DMA((n,)) for n in counts]


def to_experts(rows):
    rows = rows.reshape(EXPERTS, HALF, rows.shape[1])
    rows = lax.all_to_all(rows, "expert", split_axis=0, concat_axis=0, tiled=True)
    return rows.reshape(ROWS, -1)


def swap(array):
    return lax.ppermute(array, "core", [(0, 1), (1, 0)])


def after(array, *others):
    return lax.optimization_barrier((array,) + others)[0]


def body(tokens, expert_ids, gate_weights, w_gate, w_up, w_down, cotangent):
    gate_own, up_own, down_own = w_gate[0], w_up[0], w_down[0].T
    others = swap(jnp.concatenate([tokens, cotangent], axis=0))
    inputs = (expert_ids.T, gate_weights.T, tokens, cotangent, others)
    pick, slot_gate, send = call(
        send_kernel,
        [shape(ROWS, tokens.shape[0]), shape(ROWS, 1, dtype=F32), shape(ROWS, 2 * PAIR)],
        lax.axis_index("core").reshape(1),
        *in_hbm(*inputs),
        in_specs=[SMEM_SPEC] + [HBM_SPEC] * 5,
        scratch_shapes=buffers(*inputs) + semaphores(5),
    )
    rows = to_experts(send)
    gate_own, up_own, down_own, _ = lax.optimization_barrier((gate_own, up_own, down_own, send))
    zeros = jnp.zeros((STACK - PAIR, FFW), BF)
    gate_stack = jnp.concatenate([gate_own, swap(gate_own), zeros], axis=0)
    up_stack = jnp.concatenate([up_own, swap(up_own), zeros], axis=0)
    down_stack = jnp.concatenate([zeros, down_own, swap(down_own)], axis=0)

    parts = call(
        sums_kernel,
        shape(ROWS, 3 * FFW),
        rows,
        *in_vmem(gate_stack, up_stack, down_stack),
        in_specs=[VMEM_SPEC] * 4,
        out_specs=HBM_SPEC,
        scratch_shapes=[pltpu.VMEM((ROWS, 3 * FFW), BF)] + semaphores(3),
    )
    sums = lax.psum_scatter(parts, "y", scatter_dimension=0, tiled=True)
    shard = call(
        shard_kernel,
        shape(SHARD, 3 * FFW),
        *in_hbm(sums),
        in_specs=[HBM_SPEC],
        out_specs=HBM_SPEC,
        scratch_shapes=buffers(sums, sums) + semaphores(3, 3),
    )
    full = lax.all_gather(shard, "y", axis=0, tiled=True)
    back = call(
        back_kernel,
        shape(ROWS, 2 * PAIR),
        *in_hbm(full),
        *in_vmem(gate_stack, up_stack, down_stack),
        in_specs=[HBM_SPEC] + [VMEM_SPEC] * 3,
        out_specs=HBM_SPEC,
        scratch_shapes=buffers(full, rows) + semaphores(6, 2),
    )
    back = to_experts(back)

    in_own, in_other = rows[:, :WIDE], rows[:, WIDE:PAIR]
    dy_own, dy_other = rows[:, PAIR : PAIR + WIDE], rows[:, PAIR + WIDE :]
    hidden, gate_grad, up_grad = full[:, :FFW], full[:, FFW : 2 * FFW], full[:, 2 * FFW :]
    down_part = swap(t_dot(dy_other, hidden).astype(BF)).astype(F32)
    part = swap(t_dot(in_other, full[:, FFW:]).astype(BF)).astype(F32)
    grad_down = (t_dot(dy_own, hidden) + down_part).astype(BF).T
    grad_gate = (t_dot(in_own, gate_grad) + part[:, :FFW]).astype(BF)
    grad_up = (t_dot(in_own, up_grad) + part[:, FFW:]).astype(BF)

    back = after(back, grad_down, grad_gate, grad_up)
    total = call(mix_kernel, shape(tokens.shape[0], 2 * PAIR, dtype=F32), pick, slot_gate, back)
    other = swap(total)
    token_grad = (total[:, :WIDE] + other[:, WIDE:PAIR]).astype(BF)
    mixed = (total[:, PAIR : PAIR + WIDE] + other[:, PAIR + WIDE :]).astype(BF)
    return mixed, token_grad, grad_gate[None], grad_up[None], grad_down[None]


def solution(mesh):
    fine = Mesh(mesh.devices.reshape(N_Y, 2, EXPERTS), ("y", "core", "expert"))
    dp = ("y", "core")
    placed = (
        P("expert", dp),
        P("expert", None),
        P("expert", None),
        P("expert", dp, None),
        P("expert", dp, None),
        P("expert", None, dp),
        P("expert", dp),
    )
    return jax.shard_map(
        body,
        mesh=fine,
        in_specs=placed,
        out_specs=(
            P("expert", dp),
            P("expert", dp),
            P("expert", dp, None),
            P("expert", dp, None),
            P("expert", None, dp),
        ),
        check_vma=False,
    )
```

time: 230 us -> 209 us (0.909)
  waiting for transfers between devices: 37.7 us -> 121 us
  blocking collectives: 70.8 us -> 0 us
  starting transfers between devices: 66 us -> 43.7 us
  local copies, waits for them, and re-layouts: 11.2 us -> 1.58 us
    all_to_all x2 -> x0, blocking collectives: 70.8 us -> none  [across(): return lax.all_to_all(parts, 'y', split_axis=0, concat_axis=0, tiled=True)]
    all_gather x1, waiting for transfers between devices: 0.02 us -> 50.4 us  [body(): full = lax.all_gather(shard, 'y', axis=0, tiled=True)]
    reduce_scatter x1, waiting for transfers between devices: 0.02 us -> 45.1 us  [body(): sums = lax.psum_scatter(parts, 'y', scatter_dimension=0, tiled=True)]
    ppermute x10 -> x7, starting transfers between devices: 42.2 us -> 26.1 us  [swap(): return lax.ppermute(array, 'core', [(0, 1), (1, 0)])]
    all_to_all x4 -> x2, waiting for transfers between devices: 34.9 us -> 23 us  [to_experts(): lax.all_to_all(rows, 'expert', split_axis=0, concat_axis=0, tiled=True)]
    unnamed x35 -> x12, local copies, waits for them, and re-layouts: 11.1 us -> 1.57 us
    all_to_all x4 -> x2, starting transfers between devices: 23.8 us -> 17.5 us  [to_experts(): lax.all_to_all(rows, 'expert', split_axis=0, concat_axis=0, tiled=True)]
    pallas_call x9 -> x5, Pallas kernels: 15.1 us -> 13.2 us  [call(): pl.pallas_call(kernel, out_shape=out_shape, compiler_params=pltpu.Compile...]
  transfers between devices with their start and end apart: 16 -> 11, of which waited for: 6 -> 6; matrix products, arithmetic and copies ran while one was open for 5% -> 6% of each run, Pallas kernels for 5% -> 0%
where the time goes in v3:
time: 209 us; the launch traced here: 208 us
  waiting for transfers between devices  121 us (58%)
  starting transfers between devices  43.7 us (21%)
  between operations  14.3 us (7%)
  Pallas kernels  13.2 us (6%)
  matrix products  11 us (5%)
  other arithmetic  3.48 us (2%)
    all_gather x1, waiting for transfers between devices, body(): full = lax.all_gather(shard, 'y', axis=0, tiled=True)  50.4 us
    reduce_scatter x1, waiting for transfers between devices, body(): sums = lax.psum_scatter(parts, 'y', scatter_dimension=0, tiled=True)  45.1 us
    ppermute x7, starting transfers between devices, swap(): return lax.ppermute(array, 'core', [(0, 1), (1, 0)])  26.1 us
    all_to_all x2, waiting for transfers between devices, to_experts(): lax.all_to_all(rows, 'expert', split_axis=0, concat_axis=0, tiled=True)  23 us
    all_to_all x2, starting transfers between devices, to_experts(): lax.all_to_all(rows, 'expert', split_axis=0, concat_axis=0, tiled=True)  17.5 us
    pallas_call x5, Pallas kernels, call(): pl.pallas_call(kernel, out_shape=out_shape, compiler_params=pltpu.Compile...  13.2 us
    dot_general x5, matrix products, t_dot(): lax.dot_general(left, right, (((0,), (0,)), ((), ())), preferred_element_...  11 us
  transfers between devices with their start and end apart: 11, of which 6 were waited for; matrix products, arithmetic and copies ran while one was open for 6% of the time, Pallas kernels for 0%

profile of v3, /device:TPU:1, one launch (start us, length us, event | category | flops | bytes accessed | tf_op | source)
XLA Modules:
  0.0 208.1 jit_solution(5745650106244622411)
XLA Ops:
  8.1 8.8 %collective-permute-start = (bf16[128,224]{1,0:T(8,128)(2,1)S(1)}, bf16[128,224]{1,0:T(8,128)(2,1)S(1)}, u32[]{:S(2)}, u32[]{:S(2)}) collective-permute-start(bf16[128,224]{1,0:T(8,128)(2,1)S(1)} %pad_maximum_fusion.3), channel_id=1, source_target_pairs={{0,32},{32,0},{1,33},{33,1},{2,34},{34,2},{3,35},{35,3},{4,36},{36... | collective-permute-start | bytes 172040 | tf_op jit(solution)/shard_map/ppermute | solution.py:218
  18.4 2.4 %send_kernel.1 = (bf16[512,64]{1,0:T(8,128)(2,1)S(1)}, f32[512,1]{1,0:T(8,128)S(1)}, bf16[512,896]{1,0:T(8,128)(2,1)}) custom-call(s32[1]{0:T(128)} %bitcast.core_ref, s32[8,64]{1,0:T(8,128)} %bitcast.28, f32[8,64]{1,0:T(8,128)} %bitcast.29, bf16[64,224]{1,0:T(8,128)(2,1)} %tokens_hbm.1, bf16[64,224]{1,0:T(8,128)(2,1)} %cotangent_hbm.1, ...), custom_call_target="tpu_custom_call" | custom-call | tf_op jit(solution)/shard_map/send_kernel/pallas_call | solution.py:186
  20.8 7.6 %all-to-all-start = ((bf16[32,16,896]{2,1,0:T(8,128)(2,1)}), bf16[32,16,896]{2,1,0:T(8,128)(2,1)}, u32[]{:S(2)}, u32[]{:S(2)}) async-start(bf16[32,16,896]{2,1,0:T(8,128)(2,1)} %bitcast.3), calls=%async_computation | async-start | bytes 1835008 | tf_op jit(solution)/shard_map/all_to_all | solution.py:213
  28.5 2.5 %collective-permute-start.3 = (bf16[224,1024]{1,0:T(8,128)(2,1)S(1)}, bf16[224,1024]{1,0:T(8,128)(2,1)S(1)}, u32[]{:S(2)}, u32[]{:S(2)}) collective-permute-start(bf16[224,1024]{1,0:T(8,128)(2,1)S(1)} %bitcast.21), channel_id=1, source_target_pairs={{0,32},{32,0},{1,33},{33,1},{2,34},{34,2},{3,35},{35,3},{4,36},{36... | collective-permute-start | bytes 1376264 | tf_op jit(solution)/shard_map/ppermute | solution.py:218
  31.1 1.9 collective-permute-start.2
  33.0 2.4 %collective-permute-start.1 = (bf16[224,1024]{1,0:T(8,128)(2,1)S(1)}, bf16[224,1024]{1,0:T(8,128)(2,1)S(1)}, u32[]{:S(2)}, u32[]{:S(2)}) collective-permute-start(bf16[224,1024]{1,0:T(8,128)(2,1)S(1)} %bitcast.25), channel_id=1, source_target_pairs={{0,32},{32,0},{1,33},{33,1},{2,34},{34,2},{3,35},{35,3},{4,36},{36... | collective-permute-start | bytes 1376264 | tf_op jit(solution)/shard_map/ppermute | solution.py:218
  35.5 1.4 collective-permute-done.1
  36.9 1.7 pad_maximum_fusion.2
  38.6 13.9 %all-to-all-done = bf16[32,16,896]{2,1,0:T(8,128)(2,1)} async-done(((bf16[32,16,896]{2,1,0:T(8,128)(2,1)}), bf16[32,16,896]{2,1,0:T(8,128)(2,1)}, u32[]{:S(2)}, u32[]{:S(2)}) %all-to-all-start) | async-done | bytes 917536 | tf_op jit(solution)/shard_map/all_to_all | solution.py:213
  52.4 4.0 %sums_kernel.1 = bf16[512,3072]{1,0:T(8,128)(2,1)} custom-call(bf16[512,896]{1,0:T(8,128)(2,1)} %bitcast.4.rows, bf16[512,1024]{1,0:T(8,128)(2,1)S(1)} %get-tuple-element.23.gate, bf16[512,1024]{1,0:T(8,128)(2,1)S(1)} %get-tuple-element.22.up, bf16[512,1024]{1,0:T(8,128)(2,1)S(1)} %get-tuple-element.21.down), custom_call_target="tpu_custom_call" | custom-call | tf_op jit(solution)/shard_map/sums_kernel/pallas_call | solution.py:186
  56.5 45.1 %reduce-scatter.2.cloned.1.call-done.sums_hbm = bf16[64,3072]{1,0:T(8,128)(2,1)} async-done(((bf16[512,3072]{1,0:T(8,128)(2,1)}), bf16[64,3072]{1,0:T(8,128)(2,1)}) %reduce-scatter.2.cloned.1.call-update) | async-done | bytes 393232 | tf_op jit(solution)/shard_map/reduce_scatter | solution.py:253
  101.6 1.9 shard_kernel.1
  103.5 50.4 %all-gather.2.cloned.1.call-done.full_hbm = bf16[512,3072]{1,0:T(8,128)(2,1)} async-done(((bf16[64,3072]{1,0:T(8,128)(2,1)}), bf16[512,3072]{1,0:T(8,128)(2,1)}) %all-gather.2.cloned.1.call-update) | async-done | bytes 3145744 | tf_op jit(solution)/shard_map/all_gather | solution.py:262
  153.9 4.3 %back_kernel.1 = bf16[512,896]{1,0:T(8,128)(2,1)S(1)} custom-call(bf16[512,3072]{1,0:T(8,128)(2,1)} %all-gather.2.cloned.1.call-done.full_hbm, bf16[512,1024]{1,0:T(8,128)(2,1)S(1)} %get-tuple-element.23.gate, bf16[512,1024]{1,0:T(8,128)(2,1)S(1)} %get-tuple-element.22.up, bf16[512,1024]{1,0:T(8,128)(2,1)S(1)} %get-tuple-element.21.down), custom_call_target="tpu_custom_call" | custom-call | tf_op jit(solution)/shard_map/back_kernel/pallas_call | solution.py:186
  159.1 9.9 %all-to-all-start.1 = ((bf16[32,16,896]{2,1,0:T(8,128)(2,1)}), bf16[32,16,896]{2,1,0:T(8,128)(2,1)S(1)}, u32[]{:S(2)}, u32[]{:S(2)}) async-start(bf16[32,16,896]{2,1,0:T(8,128)(2,1)} %bitcast.18), calls=%async_computation.2 | async-start | bytes 1835008 | tf_op jit(solution)/shard_map/all_to_all | solution.py:213
  169.1 2.6 %convolution_convert_fusion = bf16[224,2048]{1,0:T(8,128)(2,1)S(1)} fusion(bf16[512,3072]{1,0:T(8,128)(2,1)} %all-gather.2.cloned.1.call-done.full_hbm, bf16[512,896]{1,0:T(8,128)(2,1)} %bitcast.4.rows), kind=kOutput, calls=%fused_computation | convolution fusion | flops 470220800 | bytes 3276800 | tf_op jit(solution)/shard_map/dot_general | solution.py:37
  171.7 3.5 %collective-permute-start.5 = (bf16[224,2048]{1,0:T(8,128)(2,1)S(1)}, bf16[224,2048]{1,0:T(8,128)(2,1)S(1)}, u32[]{:S(2)}, u32[]{:S(2)}) collective-permute-start(bf16[224,2048]{1,0:T(8,128)(2,1)S(1)} %convolution_convert_fusion), channel_id=1, source_target_pairs={{0,32},{32,0},{1,33},{33,1},{2,34},{34,2},{3,35},{35,3},{4,36},{36... | collective-permute-start | bytes 2752520 | tf_op jit(solution)/shard_map/ppermute | solution.py:218
  175.2 1.5 convolution_convert_fusion.1
  176.6 1.9 collective-permute-start.4
  178.8 2.2 %fusion.9 = bf16[224,1024]{1,0:T(8,128)(2,1)} fusion(f32[224,2048]{1,0:T(8,128)S(1)} %convert_element_type.31, bf16[512,3072]{1,0:T(8,128)(2,1)S(1)} %copy-done.1, bf16[512,896]{1,0:T(8,128)(2,1)} %bitcast.4.rows), kind=kOutput, calls=%fused_computation.16 | convolution fusion | flops 235339776 | bytes 2686976 | tf_op jit(solution)/shard_map/dot_general | solution.py:37
  180.9 2.2 %fusion.8 = bf16[224,1024]{1,0:T(8,128)(2,1)} fusion(f32[224,2048]{1,0:T(8,128)S(1)} %convert_element_type.31, bf16[512,3072]{1,0:T(8,128)(2,1)S(1)} %copy-done.1, bf16[512,896]{1,0:T(8,128)(2,1)} %bitcast.4.rows), kind=kOutput, calls=%fused_computation.14 | convolution fusion | flops 235339776 | bytes 2686976 | tf_op jit(solution)/shard_map/dot_general | solution.py:37
  183.1 9.1 %all-to-all-done.1 = bf16[32,16,896]{2,1,0:T(8,128)(2,1)S(1)} async-done(((bf16[32,16,896]{2,1,0:T(8,128)(2,1)}), bf16[32,16,896]{2,1,0:T(8,128)(2,1)S(1)}, u32[]{:S(2)}, u32[]{:S(2)}) %all-to-all-start.1) | async-done | bytes 917536 | tf_op jit(solution)/shard_map/all_to_all | solution.py:213
  192.8 5.0 %collective-permute-start.6 = (f32[64,896]{1,0:T(8,128)S(1)}, f32[64,896]{1,0:T(8,128)S(1)}, u32[]{:S(2)}, u32[]{:S(2)}) collective-permute-start(f32[64,896]{1,0:T(8,128)S(1)} %mix_kernel.1), channel_id=1, source_target_pairs={{0,32},{32,0},{1,33},{33,1},{2,34},{34,2},{3,35},{35,3},{4,36},{36... | collective-permute-start | bytes 688136 | tf_op jit(solution)/shard_map/ppermute | solution.py:218
  197.9 2.6 %fusion.10 = bf16[1,1024,224]{1,2,0:T(8,128)(2,1)} fusion(bf16[224,1024]{1,0:T(8,128)(2,1)S(1)} %collective-permute-done.4, bf16[512,3072]{1,0:T(8,128)(2,1)} %all-gather.2.cloned.1.call-done.full_hbm, bf16[512,896]{1,0:T(8,128)(2,1)} %bitcast.4.rows), kind=kOutput, calls=%fused_computation.18 | convolution fusion | flops 235569152 | bytes 2228224 | tf_op jit(solution)/shard_map/dot_general | solution.py:37
  (27 shorter events, 5.0 us)
Async XLA Ops:
  7.2 25.9 %copy-start.4 = (bf16[1,224,1024]{2,1,0:T(8,128)(2,1)S(1)}, bf16[1,224,1024]{2,1,0:T(8,128)(2,1)}, u32[]{:S(2)}) copy-start(bf16[1,224,1024]{2,1,0:T(8,128)(2,1)} %param.10) | copy-start | bytes 1376260
  7.2 23.9 %copy-start.3 = (bf16[1,224,1024]{2,1,0:T(8,128)(2,1)S(1)}, bf16[1,224,1024]{2,1,0:T(8,128)(2,1)}, u32[]{:S(2)}) copy-start(bf16[1,224,1024]{2,1,0:T(8,128)(2,1)} %param.11) | copy-start | bytes 1376260
  7.2 21.3 %copy-start.2 = (bf16[1,1024,224]{1,2,0:T(8,128)(2,1)S(1)}, bf16[1,1024,224]{1,2,0:T(8,128)(2,1)}, u32[]{:S(2)}) copy-start(bf16[1,1024,224]{1,2,0:T(8,128)(2,1)} %param.12) | copy-start | bytes 1376260
  8.1 9.7 %collective-permute-start = (bf16[128,224]{1,0:T(8,128)(2,1)S(1)}, bf16[128,224]{1,0:T(8,128)(2,1)S(1)}, u32[]{:S(2)}, u32[]{:S(2)}) collective-permute-start(bf16[128,224]{1,0:T(8,128)(2,1)S(1)} %pad_maximum_fusion.3), channel_id=1, source_target_pairs={{0,32},{32,0},{1,33},{33,1},{2,34},{34,2},{3,35},{35,3},{4,36},{36... | collective-permute-start | bytes 172040 | tf_op jit(solution)/shard_map/ppermute | solution.py:218
  17.8 0.6 copy-start.5
  20.8 31.6 %all-to-all-start = ((bf16[32,16,896]{2,1,0:T(8,128)(2,1)}), bf16[32,16,896]{2,1,0:T(8,128)(2,1)}, u32[]{:S(2)}, u32[]{:S(2)}) async-start(bf16[32,16,896]{2,1,0:T(8,128)(2,1)} %bitcast.3), calls=%async_computation | async-start | bytes 1835008 | tf_op jit(solution)/shard_map/all_to_all | solution.py:213
  28.5 73.2 %reduce-scatter.2.cloned.1.call-start = ((), (), s32[]{:S(2)}) async-start(), calls=%async_computation.3 | async-start | bytes 3538944 | tf_op jit(solution)/shard_map/reduce_scatter | solution.py:253
  28.5 6.9 %collective-permute-start.3 = (bf16[224,1024]{1,0:T(8,128)(2,1)S(1)}, bf16[224,1024]{1,0:T(8,128)(2,1)S(1)}, u32[]{:S(2)}, u32[]{:S(2)}) collective-permute-start(bf16[224,1024]{1,0:T(8,128)(2,1)S(1)} %bitcast.21), channel_id=1, source_target_pairs={{0,32},{32,0},{1,33},{33,1},{2,34},{34,2},{3,35},{35,3},{4,36},{36... | collective-permute-start | bytes 1376264 | tf_op jit(solution)/shard_map/ppermute | solution.py:218
  31.1 4.4 %collective-permute-start.2 = (bf16[224,1024]{1,0:T(8,128)(2,1)S(1)}, bf16[224,1024]{1,0:T(8,128)(2,1)S(1)}, u32[]{:S(2)}, u32[]{:S(2)}) collective-permute-start(bf16[224,1024]{1,0:T(8,128)(2,1)S(1)} %bitcast.23), channel_id=1, source_target_pairs={{0,32},{32,0},{1,33},{33,1},{2,34},{34,2},{3,35},{35,3},{4,36},{36... | collective-permute-start | bytes 1376264 | tf_op jit(solution)/shard_map/ppermute | solution.py:218
  33.0 3.8 %collective-permute-start.1 = (bf16[224,1024]{1,0:T(8,128)(2,1)S(1)}, bf16[224,1024]{1,0:T(8,128)(2,1)S(1)}, u32[]{:S(2)}, u32[]{:S(2)}) collective-permute-start(bf16[224,1024]{1,0:T(8,128)(2,1)S(1)} %bitcast.25), channel_id=1, source_target_pairs={{0,32},{32,0},{1,33},{33,1},{2,34},{34,2},{3,35},{35,3},{4,36},{36... | collective-permute-start | bytes 1376264 | tf_op jit(solution)/shard_map/ppermute | solution.py:218
  56.5 97.4 %all-gather.2.cloned.1.call-start = ((), (), s32[]{:S(2)}) async-start(), calls=%async_computation.4 | async-start | bytes 3538944 | tf_op jit(solution)/shard_map/all_gather | solution.py:262
  158.2 0.9 copy-start
  159.1 33.1 %all-to-all-start.1 = ((bf16[32,16,896]{2,1,0:T(8,128)(2,1)}), bf16[32,16,896]{2,1,0:T(8,128)(2,1)S(1)}, u32[]{:S(2)}, u32[]{:S(2)}) async-start(bf16[32,16,896]{2,1,0:T(8,128)(2,1)} %bitcast.18), calls=%async_computation.2 | async-start | bytes 1835008 | tf_op jit(solution)/shard_map/all_to_all | solution.py:213
  169.1 6.1 %copy-start.1 = (bf16[512,3072]{1,0:T(8,128)(2,1)S(1)}, bf16[512,3072]{1,0:T(8,128)(2,1)}, u32[]{:S(2)}) copy-start(bf16[512,3072]{1,0:T(8,128)(2,1)} %all-gather.2.cloned.1.call-done.full_hbm) | copy-start | bytes 9437188
  171.7 6.9 %collective-permute-start.5 = (bf16[224,2048]{1,0:T(8,128)(2,1)S(1)}, bf16[224,2048]{1,0:T(8,128)(2,1)S(1)}, u32[]{:S(2)}, u32[]{:S(2)}) collective-permute-start(bf16[224,2048]{1,0:T(8,128)(2,1)S(1)} %convolution_convert_fusion), channel_id=1, source_target_pairs={{0,32},{32,0},{1,33},{33,1},{2,34},{34,2},{3,35},{35,3},{4,36},{36... | collective-permute-start | bytes 2752520 | tf_op jit(solution)/shard_map/ppermute | solution.py:218
  176.6 21.2 %collective-permute-start.4 = (bf16[224,1024]{1,0:T(8,128)(2,1)S(1)}, bf16[224,1024]{1,0:T(8,128)(2,1)S(1)}, u32[]{:S(2)}, u32[]{:S(2)}) collective-permute-start(bf16[224,1024]{1,0:T(8,128)(2,1)S(1)} %convolution_convert_fusion.1), channel_id=1, source_target_pairs={{0,32},{32,0},{1,33},{33,1},{2,34},{34,2},{3,35},{35,3},{4,36},{36... | collective-permute-start | bytes 1376264 | tf_op jit(solution)/shard_map/ppermute | solution.py:218
  192.8 7.7 %collective-permute-start.6 = (f32[64,896]{1,0:T(8,128)S(1)}, f32[64,896]{1,0:T(8,128)S(1)}, u32[]{:S(2)}, u32[]{:S(2)}) collective-permute-start(f32[64,896]{1,0:T(8,128)S(1)} %mix_kernel.1), channel_id=1, source_target_pairs={{0,32},{32,0},{1,33},{33,1},{2,34},{34,2},{3,35},{35,3},{4,36},{36... | collective-permute-start | bytes 688136 | tf_op jit(solution)/shard_map/ppermute | solution.py:218
Sparse Core Ops, SparseCore 0:
  56.6 44.9 reduce-scatter.1
  104.3 49.5 all-gather.1

commit v4 on v3

v4 whole, which is shorter than its diff:
```python
import jax
import jax.numpy as jnp
from jax import lax
from jax.experimental import pallas as pl
from jax.experimental.pallas import tpu as pltpu
from jax.sharding import Mesh, PartitionSpec as P

EXPERTS = 32
CAP = 32
HALF = CAP // 2
ROWS = EXPERTS * HALF
WIDE = 224
PAIR = 2 * WIDE
STACK = 512
JOIN = 2 * PAIR - STACK
FFW = 1024
N_Y = 8
SHARD = ROWS // N_Y
BF = jnp.bfloat16
F32 = jnp.float32
VMEM_LIMIT = 24 * 1024 * 1024


def iota(shape, dim):
    return lax.broadcasted_iota(jnp.int32, shape, dim)


def dot(left, right):
    return jnp.dot(left, right, preferred_element_type=F32)


def dot_t(left, right):
    return lax.dot_general(left, right, (((1,), (1,)), ((), ())), preferred_element_type=F32)


def t_dot(left, right):
    return lax.dot_general(left, right, (((0,), (0,)), ((), ())), preferred_element_type=F32)


def shape(*dims, dtype=BF):
    return jax.ShapeDtypeStruct(dims, dtype)


def start(copies):
    for copy in copies:
        copy.start()


def wait(copies):
    for copy in copies:
        copy.wait()


def copies_of(pairs, sems):
    return [pltpu.make_async_copy(src, dst, sems.at[i]) for i, (src, dst) in enumerate(pairs)]


def slot_table(ids_ref, gates_ref, first):
    tokens = ids_ref.shape[1]
    numbers = iota((EXPERTS, tokens), 0)
    chosen = jnp.zeros((EXPERTS, tokens), F32)
    weight = jnp.zeros((EXPERTS, tokens), F32)
    for k in range(ids_ref.shape[0]):
        hit = ids_ref[k : k + 1, :] == numbers
        chosen = chosen + jnp.where(hit, 1.0, 0.0)
        weight = weight + jnp.where(hit, gates_ref[k : k + 1, :], 0.0)
    earlier = jnp.where(iota((tokens, tokens), 0) < iota((tokens, tokens), 1), 1.0, 0.0)
    rank = dot(chosen.astype(BF), earlier.astype(BF))
    slot = jnp.where(chosen > 0.5, rank, -1.0).astype(jnp.int32) - first
    hit = slot[:, None, :] == iota((EXPERTS, HALF, tokens), 1)
    pick = jnp.where(hit, 1.0, 0.0).reshape(ROWS, tokens).astype(BF)
    gate = jnp.sum(jnp.where(hit, weight[:, None, :], 0.0), axis=2, keepdims=True)
    return pick, gate.reshape(ROWS, 1)


def send_kernel(
    core_ref,
    others_ref,
    ids_hbm,
    gates_hbm,
    tokens_hbm,
    cotangent_hbm,
    out_ref,
    ids_ref,
    gates_ref,
    tokens_ref,
    cotangent_ref,
    sems,
):
    loads = copies_of(
        (
            (ids_hbm, ids_ref),
            (gates_hbm, gates_ref),
            (tokens_hbm, tokens_ref),
            (cotangent_hbm, cotangent_ref),
        ),
        sems,
    )
    start(loads)
    wait(loads[:2])
    pick, gate = slot_table(ids_ref, gates_ref, core_ref[0] * HALF)
    wait(loads[2:])
    count = tokens_ref.shape[0]
    features = jnp.concatenate(
        [tokens_ref[...], others_ref[:count], cotangent_ref[...], others_ref[count:]], axis=1
    )
    rows = dot(pick, features)
    scale = jnp.where(iota((1, 2 * PAIR), 1) < PAIR, 1.0, gate)
    out_ref[...] = (rows * scale).astype(BF)


def table_kernel(ids_ref, gates_ref, pick_ref, gate_ref):
    for half in range(2):
        pick_ref[half], gate_ref[half] = slot_table(ids_ref, gates_ref, half * HALF)


def sums_kernel(rows, gate, up, down, out_hbm, out, sems):
    columns = [pl.ds(i * FFW, FFW) for i in range(3)]
    stores = copies_of([(out.at[:, c], out_hbm.at[:, c]) for c in columns], sems)
    for i, weights in enumerate((gate, up, down)):
        left = rows[:, :STACK] if i < 2 else rows[:, 2 * PAIR - STACK :]
        out[:, i * FFW : (i + 1) * FFW] = dot(left, weights[...]).astype(BF)
        stores[i].start()
    wait(stores)


def shard_kernel(sums_hbm, out_hbm, sums, out, in_sems, out_sems):
    columns = [pl.ds(i * FFW, FFW) for i in range(3)]
    loads = copies_of([(sums_hbm.at[:, c], sums.at[:, c]) for c in columns], in_sems)
    stores = copies_of([(out.at[:, c], out_hbm.at[:, c]) for c in columns], out_sems)
    start(loads)
    wait(loads[:2])
    gate_sum = sums[:, :FFW].astype(F32)
    up_sum = sums[:, FFW : 2 * FFW].astype(F32)
    logistic = jax.nn.sigmoid(gate_sum)
    silu = gate_sum * logistic
    out[:, :FFW] = (silu * up_sum).astype(BF)
    stores[0].start()
    loads[2].wait()
    total = sums[:, 2 * FFW :].astype(F32)
    slope = logistic * (1.0 + gate_sum * (1.0 - logistic))
    out[:, FFW : 2 * FFW] = (total * up_sum * slope).astype(BF)
    stores[1].start()
    out[:, 2 * FFW :] = (total * silu).astype(BF)
    stores[2].start()
    wait(stores)


def back_kernel(full_hbm, gate_hbm, up_hbm, down_hbm, out_ref, full, weights, sems):
    blocks = [(y, half) for y in range(N_Y) for half in range(2)]
    loads = copies_of(
        [(w, weights.at[i]) for i, w in enumerate((down_hbm, gate_hbm, up_hbm))]
        + [
            (
                full_hbm.at[pl.ds((2 * y + half) * SHARD, SHARD)],
                full.at[half, pl.ds(y * SHARD, SHARD)],
            )
            for y, half in blocks
        ],
        sems,
    )
    start(loads)
    wait(loads[:3])
    loads = loads[3:]
    step = ROWS // 2
    for i in range(2):
        wait(loads[i * N_Y : (i + 1) * N_Y])
        rows = slice(i * step, (i + 1) * step)
        parts = []
        for half in range(2):
            grad = dot_t(full[half, rows, FFW : 2 * FFW], weights[1])
            grad = grad + dot_t(full[half, rows, 2 * FFW :], weights[2])
            parts += [grad, dot_t(full[half, rows, :FFW], weights[0])]
        out_ref[rows] = jnp.concatenate(parts, axis=1).astype(BF)


def mix_kernel(pick_ref, gate_ref, back_ref, grad_ref, mixed_ref):
    totals = []
    for half in range(2):
        skip = half * (PAIR - JOIN)
        back = back_ref[:, half * JOIN : half * JOIN + STACK].astype(F32)
        lane = iota((1, STACK), 1)
        scaled = back * jnp.where(lane < skip + WIDE, 1.0, gate_ref[half])
        high = scaled.astype(BF)
        low = (scaled - high.astype(F32)).astype(BF)
        totals.append(t_dot(pick_ref[half], high) + t_dot(pick_ref[half], low))
    total = totals[0][:, :PAIR] + totals[1][:, STACK - PAIR :]
    grad_ref[...] = total[:, :WIDE].astype(BF)
    mixed_ref[...] = total[:, WIDE:].astype(BF)


HBM_SPEC = pl.BlockSpec(memory_space=pltpu.HBM)
VMEM_SPEC = pl.BlockSpec(memory_space=pltpu.VMEM)
SMEM_SPEC = pl.BlockSpec(memory_space=pltpu.SMEM)


def call(kernel, out_shape, *args, **kwargs):
    return pl.pallas_call(
        kernel,
        out_shape=out_shape,
        compiler_params=pltpu.CompilerParams(vmem_limit_bytes=VMEM_LIMIT),
        name=kernel.__name__,
        **kwargs,
    )(*args)


def in_hbm(*arrays):
    return [pltpu.with_memory_space_constraint(a, pltpu.HBM) for a in arrays]


def in_vmem(*arrays):
    return [pltpu.with_memory_space_constraint(a, pltpu.VMEM) for a in arrays]


def buffers(*arrays):
    return [pltpu.VMEM(a.shape, a.dtype) for a in arrays]


def semaphores(*counts):
    return [pltpu.SemaphoreType.DMA((n,)) for n in counts]


def to_experts(rows):
    rows = rows.reshape(EXPERTS, HALF, rows.shape[1])
    rows = lax.all_to_all(rows, "expert", split_axis=0, concat_axis=0, tiled=True)
    return rows.reshape(ROWS, -1)


def swap(array):
    return lax.ppermute(array, "core", [(0, 1), (1, 0)])


def after(array, *others):
    return lax.optimization_barrier((array,) + others)[0]


def body(tokens, expert_ids, gate_weights, w_gate, w_up, w_down, cotangent):
    gate_own, up_own, down_own = w_gate[0], w_up[0], w_down[0].T
    core = lax.axis_index("core")
    others = swap(jnp.concatenate([tokens, cotangent], axis=0))
    ids, gates = expert_ids.T, gate_weights.T
    inputs = (ids, gates, tokens, cotangent)
    send = call(
        send_kernel,
        shape(ROWS, 2 * PAIR),
        core.reshape(1),
        others,
        *in_hbm(*inputs),
        in_specs=[SMEM_SPEC, VMEM_SPEC] + [HBM_SPEC] * 4,
        scratch_shapes=buffers(*inputs) + semaphores(4),
    )
    rows = to_experts(send)
    gate_sent, up_sent, down_sent, _ = lax.optimization_barrier((gate_own, up_own, down_own, send))
    zeros = jnp.zeros((STACK - PAIR, FFW), BF)
    gate_stack = jnp.concatenate([gate_sent, swap(gate_sent), zeros], axis=0)
    up_stack = jnp.concatenate([up_sent, swap(up_sent), zeros], axis=0)
    down_stack = jnp.concatenate([zeros, down_sent, swap(down_sent)], axis=0)

    parts = call(
        sums_kernel,
        shape(ROWS, 3 * FFW),
        rows,
        *in_vmem(gate_stack, up_stack, down_stack),
        in_specs=[VMEM_SPEC] * 4,
        out_specs=HBM_SPEC,
        scratch_shapes=[pltpu.VMEM((ROWS, 3 * FFW), BF)] + semaphores(3),
    )
    sums = lax.psum_scatter(parts, "y", scatter_dimension=0, tiled=True)

    rows, ids, gates, _ = lax.optimization_barrier((rows, ids, gates, parts))
    pick, slot_gate = call(
        table_kernel,
        [shape(2, ROWS, tokens.shape[0]), shape(2, ROWS, 1, dtype=F32)],
        ids,
        gates,
    )
    own = jnp.concatenate([rows[:, :WIDE], rows[:, PAIR : PAIR + WIDE]], axis=1)
    other = jnp.concatenate([rows[:, WIDE:PAIR], rows[:, PAIR + WIDE :]], axis=1)
    other = swap(other)
    first = jnp.where(core == 0, own, other).reshape(N_Y, 1, SHARD, PAIR)
    second = jnp.where(core == 0, other, own).reshape(N_Y, 1, SHARD, PAIR)
    own = jnp.concatenate([first, second], axis=1).reshape(2 * ROWS, PAIR)
    rows_in, rows_dy = own[:, :WIDE], own[:, WIDE:]
    sums, rows_in, rows_dy, pick, slot_gate = lax.optimization_barrier(
        (sums, rows_in, rows_dy, pick, slot_gate)
    )

    shard = call(
        shard_kernel,
        shape(SHARD, 3 * FFW),
        *in_hbm(sums),
        in_specs=[HBM_SPEC],
        out_specs=HBM_SPEC,
        scratch_shapes=buffers(sums, sums) + semaphores(3, 3),
    )
    full = lax.all_gather(shard, ("y", "core"), axis=0, tiled=True)
    back = call(
        back_kernel,
        shape(ROWS, 2 * PAIR),
        *in_hbm(full, gate_own, up_own, down_own),
        in_specs=[HBM_SPEC] * 4,
        out_specs=VMEM_SPEC,
        scratch_shapes=[pltpu.VMEM((2, ROWS, 3 * FFW), BF), pltpu.VMEM((3, WIDE, FFW), BF)]
        + semaphores(3 + 2 * N_Y),
    )
    back = to_experts(back)

    grad_down = t_dot(rows_dy, full[:, :FFW]).astype(BF).T
    grad_gate = t_dot(rows_in, full[:, FFW : 2 * FFW]).astype(BF)
    grad_up = t_dot(rows_in, full[:, 2 * FFW :]).astype(BF)
    back = after(back, grad_down, grad_gate, grad_up)
    token_grad, mixed = call(mix_kernel, [shape(*tokens.shape)] * 2, pick, slot_gate, back)
    return mixed, token_grad, grad_gate[None], grad_up[None], grad_down[None]


def solution(mesh):
    fine = Mesh(mesh.devices.reshape(N_Y, 2, EXPERTS), ("y", "core", "expert"))
    dp = ("y", "core")
    placed = (
        P("expert", dp),
        P("expert", None),
        P("expert", None),
        P("expert", dp, None),
        P("expert", dp, None),
        P("expert", None, dp),
        P("expert", dp),
    )
    return jax.shard_map(
        body,
        mesh=fine,
        in_specs=placed,
        out_specs=(
            P("expert", dp),
            P("expert", dp),
            P("expert", dp, None),
            P("expert", dp, None),
            P("expert", None, dp),
        ),
        check_vma=False,
    )
```

time: 209 us -> 205 us (0.981)
  starting transfers between devices: 43.7 us -> 37.4 us
  matrix products: 11 us -> 7.66 us
    reduce_scatter x1, waiting for transfers between devices: 45.1 us -> 38.2 us  [body(): sums = lax.psum_scatter(parts, 'y', scatter_dimension=0, tiled=True)]
    ppermute x7 -> x5, starting transfers between devices: 26.1 us -> 19.8 us  [swap(): return lax.ppermute(array, 'core', [(0, 1), (1, 0)])]
    all_to_all x2, waiting for transfers between devices: 23 us -> 29.3 us  [to_experts(): lax.all_to_all(rows, 'expert', split_axis=0, concat_axis=0, tiled=True)]
    dot_general x5 -> x3, matrix products: 11 us -> 7.66 us  [t_dot(): lax.dot_general(left, right, (((0,), (0,)), ((), ())), preferred_element_...]
    pallas_call x5 -> x6, Pallas kernels: 13.2 us -> 14.5 us  [call(): pl.pallas_call(kernel, out_shape=out_shape, compiler_params=pltpu.Compile...]
  transfers between devices with their start and end apart: 11 -> 9, of which waited for: 6 -> 7; matrix products, arithmetic and copies ran while one was open for 6% -> 6% of each run, Pallas kernels for 0% -> 0%
where the time goes in v4:
time: 205 us; the launch traced here: 203 us
  waiting for transfers between devices  123 us (60%)
  starting transfers between devices  37.4 us (18%)
  Pallas kernels  14.5 us (7%)
  between operations  14.3 us (7%)
  matrix products  7.66 us (4%)
  other arithmetic  4.03 us (2%)
    all_gather x1, waiting for transfers between devices, body(): full = lax.all_gather(shard, ('y', 'core'), axis=0, tiled=True)  52.4 us
    reduce_scatter x1, waiting for transfers between devices, body(): sums = lax.psum_scatter(parts, 'y', scatter_dimension=0, tiled=True)  38.2 us
    all_to_all x2, waiting for transfers between devices, to_experts(): lax.all_to_all(rows, 'expert', split_axis=0, concat_axis=0, tiled=True)  29.3 us
    ppermute x5, starting transfers between devices, swap(): return lax.ppermute(array, 'core', [(0, 1), (1, 0)])  19.8 us
    all_to_all x2, starting transfers between devices, to_experts(): lax.all_to_all(rows, 'expert', split_axis=0, concat_axis=0, tiled=True)  17.4 us
    pallas_call x6, Pallas kernels, call(): pl.pallas_call(kernel, out_shape=out_shape, compiler_params=pltpu.Compile...  14.5 us
    dot_general x3, matrix products, t_dot(): lax.dot_general(left, right, (((0,), (0,)), ((), ())), preferred_element_...  7.66 us
  transfers between devices with their start and end apart: 9, of which 7 were waited for; matrix products, arithmetic and copies ran while one was open for 6% of the time, Pallas kernels for 0%

profile of v4, /device:TPU:1, one launch (start us, length us, event | category | flops | bytes accessed | tf_op | source)
XLA Modules:
  0.0 202.9 jit_solution(5115138218782078323)
XLA Ops:
  7.2 0.9 pad_maximum_fusion.6
  8.1 8.8 %collective-permute-start = (bf16[128,224]{1,0:T(8,128)(2,1)S(1)}, bf16[128,224]{1,0:T(8,128)(2,1)S(1)}, u32[]{:S(2)}, u32[]{:S(2)}) collective-permute-start(bf16[128,224]{1,0:T(8,128)(2,1)S(1)} %pad_maximum_fusion.6), channel_id=1, source_target_pairs={{0,32},{32,0},{1,33},{33,1},{2,34},{34,2},{3,35},{35,3},{4,36},{36... | collective-permute-start | bytes 172040 | tf_op jit(solution)/shard_map/ppermute | solution.py:230
  17.8 2.4 %send_kernel.1 = bf16[512,896]{1,0:T(8,128)(2,1)} custom-call(s32[1]{0:T(128)} %bitcast.core_ref, bf16[128,224]{1,0:T(8,128)(2,1)S(1)} %collective-permute-done.others_ref, s32[8,64]{1,0:T(8,128)} %bitcast.28, f32[8,64]{1,0:T(8,128)} %bitcast.30, bf16[64,224]{1,0:T(8,128)(2,1)} %tokens_hbm.1, bf16[64,224]{1,0:T(8,128)(2,1)} %cotangent_hbm.1), custom_call_target="tpu_custom_call" | custom-call | tf_op jit(solution)/shard_map/send_kernel/pallas_call | solution.py:198
  20.2 7.5 %all-to-all-start = ((bf16[32,16,896]{2,1,0:T(8,128)(2,1)}), bf16[32,16,896]{2,1,0:T(8,128)(2,1)S(1)}, u32[]{:S(2)}, u32[]{:S(2)}) async-start(bf16[32,16,896]{2,1,0:T(8,128)(2,1)} %bitcast.3), calls=%async_computation | async-start | bytes 1835008 | tf_op jit(solution)/shard_map/all_to_all | solution.py:225
  27.8 2.5 %collective-permute-start.1 = (bf16[224,1024]{1,0:T(8,128)(2,1)S(1)}, bf16[224,1024]{1,0:T(8,128)(2,1)S(1)}, u32[]{:S(2)}, u32[]{:S(2)}) collective-permute-start(bf16[224,1024]{1,0:T(8,128)(2,1)S(1)} %bitcast.43), channel_id=1, source_target_pairs={{0,32},{32,0},{1,33},{33,1},{2,34},{34,2},{3,35},{35,3},{4,36},{36... | collective-permute-start | bytes 1376264 | tf_op jit(solution)/shard_map/ppermute | solution.py:230
  30.3 1.9 collective-permute-start.2
  32.3 2.4 %collective-permute-start.3 = (bf16[224,1024]{1,0:T(8,128)(2,1)S(1)}, bf16[224,1024]{1,0:T(8,128)(2,1)S(1)}, u32[]{:S(2)}, u32[]{:S(2)}) collective-permute-start(bf16[224,1024]{1,0:T(8,128)(2,1)S(1)} %bitcast.36), channel_id=1, source_target_pairs={{0,32},{32,0},{1,33},{33,1},{2,34},{34,2},{3,35},{35,3},{4,36},{36... | collective-permute-start | bytes 1376264 | tf_op jit(solution)/shard_map/ppermute | solution.py:230
  34.7 1.4 collective-permute-done.3
  36.1 2.5 %pad_maximum_fusion.2 = (bf16[512,1024]{1,0:T(8,128)(2,1)S(1)}, bf16[512,1024]{1,0:T(8,128)(2,1)S(1)}, bf16[512,1024]{1,0:T(8,128)(2,1)}) fusion(bf16[224,1024]{1,0:T(8,128)(2,1)S(1)} %collective-permute-done.3, bf16[224,1024]{1,0:T(8,128)(2,1)S(1)} %bitcast.37, bf16[64,1024]{1,0:T(8,128)(2,1)S(1)} %broadcast_in_dim.12, ...), kind=kLoop, calls=%fused_computation.11 | loop fusion | flops 8912896 | bytes 6029312 | tf_op jit(solution)/shard_map/concatenate | solution.py:257
  38.7 13.0 %all-to-all-done = bf16[32,16,896]{2,1,0:T(8,128)(2,1)S(1)} async-done(((bf16[32,16,896]{2,1,0:T(8,128)(2,1)}), bf16[32,16,896]{2,1,0:T(8,128)(2,1)S(1)}, u32[]{:S(2)}, u32[]{:S(2)}) %all-to-all-start) | async-done | bytes 917536 | tf_op jit(solution)/shard_map/all_to_all | solution.py:225
  51.7 1.2 copy-done
  52.9 2.8 %sums_kernel.1 = bf16[512,3072]{1,0:T(8,128)(2,1)} custom-call(bf16[512,896]{1,0:T(8,128)(2,1)S(1)} %bitcast.25, bf16[512,1024]{1,0:T(8,128)(2,1)S(1)} %copy-done, bf16[512,1024]{1,0:T(8,128)(2,1)S(1)} %get-tuple-element.46.up, bf16[512,1024]{1,0:T(8,128)(2,1)S(1)} %get-tuple-element.45.down), custom_call_target="tpu_custom_call" | custom-call | tf_op jit(solution)/shard_map/sums_kernel/pallas_call | solution.py:198
  56.4 4.2 %collective-permute-start.4 = (bf16[512,448]{1,0:T(8,128)(2,1)S(1)}, bf16[512,448]{1,0:T(8,128)(2,1)S(1)}, u32[]{:S(2)}, u32[]{:S(2)}) collective-permute-start(bf16[512,448]{1,0:T(8,128)(2,1)S(1)} %pad_maximum_fusion.5), channel_id=1, source_target_pairs={{0,32},{32,0},{1,33},{33,1},{2,34},{34,2},{3,35},{35,3},{4,36},{36... | collective-permute-start | bytes 1376264 | tf_op jit(solution)/shard_map/ppermute | solution.py:230
  61.0 1.1 collective-permute-done.4
  62.7 38.2 %reduce-scatter.2.cloned.1.call-done.sums_hbm = bf16[64,3072]{1,0:T(8,128)(2,1)} async-done(((bf16[512,3072]{1,0:T(8,128)(2,1)}), bf16[64,3072]{1,0:T(8,128)(2,1)}) %reduce-scatter.2.cloned.1.call-update) | async-done | bytes 393232 | tf_op jit(solution)/shard_map/reduce_scatter | solution.py:268
  101.0 1.9 shard_kernel.1
  102.9 52.4 %all-gather.2.cloned.1.call-done.full_hbm = bf16[1024,3072]{1,0:T(8,128)(2,1)} async-done(((bf16[64,3072]{1,0:T(8,128)(2,1)}), bf16[1024,3072]{1,0:T(8,128)(2,1)}) %all-gather.2.cloned.1.call-update) | async-done | bytes 6291472 | tf_op jit(solution)/shard_map/all_gather | solution.py:296
  155.3 5.5 %back_kernel.1 = bf16[512,896]{1,0:T(8,128)(2,1)} custom-call(bf16[1024,3072]{1,0:T(8,128)(2,1)} %all-gather.2.cloned.1.call-done.full_hbm, bf16[224,1024]{1,0:T(8,128)(2,1)} %bitcast.42, bf16[224,1024]{1,0:T(8,128)(2,1)} %bitcast.39, bf16[224,1024]{1,0:T(8,128)(2,1)} %bitcast.35), custom_call_target="tpu_custom_call" | custom-call | tf_op jit(solution)/shard_map/back_kernel/pallas_call | solution.py:198
  160.8 9.9 %all-to-all-start.1 = ((bf16[32,16,896]{2,1,0:T(8,128)(2,1)}), bf16[32,16,896]{2,1,0:T(8,128)(2,1)S(1)}, u32[]{:S(2)}, u32[]{:S(2)}) async-start(bf16[32,16,896]{2,1,0:T(8,128)(2,1)} %bitcast.15), calls=%async_computation.2 | async-start | bytes 1835008 | tf_op jit(solution)/shard_map/all_to_all | solution.py:225
  170.7 3.2 %fusion.12 = bf16[224,1024]{1,0:T(8,128)(2,1)} fusion(bf16[1024,224]{1,0:T(8,128)(2,1)S(1)} %get-tuple-element.33, bf16[1024,3072]{1,0:T(8,128)(2,1)} %all-gather.2.cloned.1.call-done.full_hbm), kind=kOutput, calls=%fused_computation.10 | convolution fusion | flops 469991424 | bytes 3014656 | tf_op jit(solution)/shard_map/dot_general | solution.py:37
  173.9 3.0 %fusion.9 = bf16[224,1024]{1,0:T(8,128)(2,1)} fusion(bf16[1024,224]{1,0:T(8,128)(2,1)S(1)} %get-tuple-element.33, bf16[1024,3072]{1,0:T(8,128)(2,1)} %all-gather.2.cloned.1.call-done.full_hbm), kind=kOutput, calls=%fused_computation.9 | convolution fusion | flops 469991424 | bytes 3014656 | tf_op jit(solution)/shard_map/dot_general | solution.py:37
  176.9 1.5 fusion.6
  178.4 16.2 %all-to-all-done.1 = bf16[32,16,896]{2,1,0:T(8,128)(2,1)S(1)} async-done(((bf16[32,16,896]{2,1,0:T(8,128)(2,1)}), bf16[32,16,896]{2,1,0:T(8,128)(2,1)S(1)}, u32[]{:S(2)}, u32[]{:S(2)}) %all-to-all-start.1) | async-done | bytes 917536 | tf_op jit(solution)/shard_map/all_to_all | solution.py:225
  194.6 1.5 mix_kernel.1
  (27 shorter events, 2.6 us)
Async XLA Ops:
  7.2 25.1 %copy-start.4 = (bf16[1,1024,224]{1,2,0:T(8,128)(2,1)S(1)}, bf16[1,1024,224]{1,2,0:T(8,128)(2,1)}, u32[]{:S(2)}) copy-start(bf16[1,1024,224]{1,2,0:T(8,128)(2,1)} %param.12) | copy-start | bytes 1376260
  7.2 23.2 %copy-start.5 = (bf16[1,224,1024]{2,1,0:T(8,128)(2,1)S(1)}, bf16[1,224,1024]{2,1,0:T(8,128)(2,1)}, u32[]{:S(2)}) copy-start(bf16[1,224,1024]{2,1,0:T(8,128)(2,1)} %param.11) | copy-start | bytes 1376260
  7.2 20.6 %copy-start.6 = (bf16[1,224,1024]{2,1,0:T(8,128)(2,1)S(1)}, bf16[1,224,1024]{2,1,0:T(8,128)(2,1)}, u32[]{:S(2)}) copy-start(bf16[1,224,1024]{2,1,0:T(8,128)(2,1)} %param.10) | copy-start | bytes 1376260
  8.1 9.7 %collective-permute-start = (bf16[128,224]{1,0:T(8,128)(2,1)S(1)}, bf16[128,224]{1,0:T(8,128)(2,1)S(1)}, u32[]{:S(2)}, u32[]{:S(2)}) collective-permute-start(bf16[128,224]{1,0:T(8,128)(2,1)S(1)} %pad_maximum_fusion.6), channel_id=1, source_target_pairs={{0,32},{32,0},{1,33},{33,1},{2,34},{34,2},{3,35},{35,3},{4,36},{36... | collective-permute-start | bytes 172040 | tf_op jit(solution)/shard_map/ppermute | solution.py:230
  20.2 31.5 %all-to-all-start = ((bf16[32,16,896]{2,1,0:T(8,128)(2,1)}), bf16[32,16,896]{2,1,0:T(8,128)(2,1)S(1)}, u32[]{:S(2)}, u32[]{:S(2)}) async-start(bf16[32,16,896]{2,1,0:T(8,128)(2,1)} %bitcast.3), calls=%async_computation | async-start | bytes 1835008 | tf_op jit(solution)/shard_map/all_to_all | solution.py:225
  27.7 73.3 %reduce-scatter.2.cloned.1.call-start = ((), (), s32[]{:S(2)}) async-start(), calls=%async_computation.3 | async-start | bytes 3538944 | tf_op jit(solution)/shard_map/reduce_scatter | solution.py:268
  27.8 6.9 %collective-permute-start.1 = (bf16[224,1024]{1,0:T(8,128)(2,1)S(1)}, bf16[224,1024]{1,0:T(8,128)(2,1)S(1)}, u32[]{:S(2)}, u32[]{:S(2)}) collective-permute-start(bf16[224,1024]{1,0:T(8,128)(2,1)S(1)} %bitcast.43), channel_id=1, source_target_pairs={{0,32},{32,0},{1,33},{33,1},{2,34},{34,2},{3,35},{35,3},{4,36},{36... | collective-permute-start | bytes 1376264 | tf_op jit(solution)/shard_map/ppermute | solution.py:230
  30.3 4.4 %collective-permute-start.2 = (bf16[224,1024]{1,0:T(8,128)(2,1)S(1)}, bf16[224,1024]{1,0:T(8,128)(2,1)S(1)}, u32[]{:S(2)}, u32[]{:S(2)}) collective-permute-start(bf16[224,1024]{1,0:T(8,128)(2,1)S(1)} %bitcast.40), channel_id=1, source_target_pairs={{0,32},{32,0},{1,33},{33,1},{2,34},{34,2},{3,35},{35,3},{4,36},{36... | collective-permute-start | bytes 1376264 | tf_op jit(solution)/shard_map/ppermute | solution.py:230
  32.3 3.8 %collective-permute-start.3 = (bf16[224,1024]{1,0:T(8,128)(2,1)S(1)}, bf16[224,1024]{1,0:T(8,128)(2,1)S(1)}, u32[]{:S(2)}, u32[]{:S(2)}) collective-permute-start(bf16[224,1024]{1,0:T(8,128)(2,1)S(1)} %bitcast.36), channel_id=1, source_target_pairs={{0,32},{32,0},{1,33},{33,1},{2,34},{34,2},{3,35},{35,3},{4,36},{36... | collective-permute-start | bytes 1376264 | tf_op jit(solution)/shard_map/ppermute | solution.py:230
  51.7 1.2 copy-start
  55.8 4.8 %copy-start.1 = (s32[64,8]{0,1:T(8,128)S(1)}, s32[64,8]{0,1:T(8,128)}, u32[]{:S(2)}) copy-start(s32[64,8]{0,1:T(8,128)} %param.8) | copy-start | bytes 6148
  55.8 4.8 %copy-start.2 = (f32[64,8]{0,1:T(8,128)S(1)}, f32[64,8]{0,1:T(8,128)}, u32[]{:S(2)}) copy-start(f32[64,8]{0,1:T(8,128)} %param.9) | copy-start | bytes 6148
  55.8 99.5 %all-gather.2.cloned.1.call-start = ((), (), s32[]{:S(2)}) async-start(), calls=%async_computation.4 | async-start | bytes 6684672 | tf_op jit(solution)/shard_map/all_gather | solution.py:296
  56.4 5.7 %collective-permute-start.4 = (bf16[512,448]{1,0:T(8,128)(2,1)S(1)}, bf16[512,448]{1,0:T(8,128)(2,1)S(1)}, u32[]{:S(2)}, u32[]{:S(2)}) collective-permute-start(bf16[512,448]{1,0:T(8,128)(2,1)S(1)} %pad_maximum_fusion.5), channel_id=1, source_target_pairs={{0,32},{32,0},{1,33},{33,1},{2,34},{34,2},{3,35},{35,3},{4,36},{36... | collective-permute-start | bytes 1376264 | tf_op jit(solution)/shard_map/ppermute | solution.py:230
  160.8 33.8 %all-to-all-start.1 = ((bf16[32,16,896]{2,1,0:T(8,128)(2,1)}), bf16[32,16,896]{2,1,0:T(8,128)(2,1)S(1)}, u32[]{:S(2)}, u32[]{:S(2)}) async-start(bf16[32,16,896]{2,1,0:T(8,128)(2,1)} %bitcast.15), calls=%async_computation.2 | async-start | bytes 1835008 | tf_op jit(solution)/shard_map/all_to_all | solution.py:225
  170.7 6.2 %copy-start.3 = (bf16[1024,3072]{1,0:T(8,128)(2,1)S(1)}, bf16[1024,3072]{1,0:T(8,128)(2,1)}, u32[]{:S(2)}) copy-start(bf16[1024,3072]{1,0:T(8,128)(2,1)} %all-gather.2.cloned.1.call-done.full_hbm) | copy-start | bytes 18874372
Sparse Core Ops, SparseCore 0:
  55.9 45.0 reduce-scatter.1
  103.7 51.5 all-gather.1

commit v5 on v4

v5 whole, which is shorter than its diff:
```python
import jax
import jax.numpy as jnp
from jax import lax
from jax.experimental import pallas as pl
from jax.experimental.pallas import tpu as pltpu
from jax.sharding import Mesh, PartitionSpec as P

EXPERTS = 32
CAP = 32
HALF = CAP // 2
QUAD = 4
QUADS = HALF // QUAD
MAIN = QUADS - 1
QROWS = EXPERTS * QUAD
WIDE = 224
PAIR = 2 * WIDE
STACK = 512
JOIN = 2 * PAIR - STACK
FFW = 1024
N_Y = 8
BF = jnp.bfloat16
F32 = jnp.float32
VMEM_LIMIT = 24 * 1024 * 1024


def iota(shape, dim):
    return lax.broadcasted_iota(jnp.int32, shape, dim)


def dot(left, right):
    return jnp.dot(left, right, preferred_element_type=F32)


def dot_t(left, right):
    return lax.dot_general(left, right, (((1,), (1,)), ((), ())), preferred_element_type=F32)


def t_dot(left, right):
    return lax.dot_general(left, right, (((0,), (0,)), ((), ())), preferred_element_type=F32)


def shape(*dims, dtype=BF):
    return jax.ShapeDtypeStruct(dims, dtype)


def start(copies):
    for copy in copies:
        copy.start()


def wait(copies):
    for copy in copies:
        copy.wait()


def copies_of(pairs, sems):
    return [pltpu.make_async_copy(src, dst, sems.at[i]) for i, (src, dst) in enumerate(pairs)]


def slot_table(ids_ref, gates_ref, firsts):
    tokens = ids_ref.shape[1]
    numbers = iota((EXPERTS, tokens), 0)
    chosen = jnp.zeros((EXPERTS, tokens), F32)
    weight = jnp.zeros((EXPERTS, tokens), F32)
    for k in range(ids_ref.shape[0]):
        hit = ids_ref[k : k + 1, :] == numbers
        chosen = chosen + jnp.where(hit, 1.0, 0.0)
        weight = weight + jnp.where(hit, gates_ref[k : k + 1, :], 0.0)
    earlier = jnp.where(iota((tokens, tokens), 0) < iota((tokens, tokens), 1), 1.0, 0.0)
    rank = dot(chosen.astype(BF), earlier.astype(BF))
    rank = jnp.where(chosen > 0.5, rank, -1.0).astype(jnp.int32)
    tables = []
    for first in firsts:
        hit = (rank - first)[:, None, :] == iota((EXPERTS, QUAD, tokens), 1)
        pick = jnp.where(hit, 1.0, 0.0).reshape(QROWS, tokens)
        gate = jnp.where(hit, weight[:, None, :], 0.0).reshape(QROWS, tokens)
        tables.append((pick.astype(BF), jnp.sum(gate, axis=1, keepdims=True)))
    return tables


def send_kernel(
    core_ref,
    others_ref,
    ids_hbm,
    gates_hbm,
    tokens_hbm,
    cotangent_hbm,
    main_ref,
    last_ref,
    ids_ref,
    gates_ref,
    tokens_ref,
    cotangent_ref,
    sems,
):
    loads = copies_of(
        (
            (ids_hbm, ids_ref),
            (gates_hbm, gates_ref),
            (tokens_hbm, tokens_ref),
            (cotangent_hbm, cotangent_ref),
        ),
        sems,
    )
    start(loads)
    wait(loads[:2])
    firsts = [core_ref[0] * HALF + QUAD * q for q in range(QUADS)]
    tables = slot_table(ids_ref, gates_ref, firsts)
    wait(loads[2:])
    count = tokens_ref.shape[0]
    features = jnp.concatenate(
        [tokens_ref[...], others_ref[:count], cotangent_ref[...], others_ref[count:]], axis=1
    )
    for q, (pick, gate) in enumerate(tables):
        scale = jnp.where(iota((1, 2 * PAIR), 1) < PAIR, 1.0, gate)
        rows = (dot(pick, features) * scale).reshape(EXPERTS, QUAD, 2 * PAIR).astype(BF)
        if q < MAIN:
            main_ref[:, q] = rows
        else:
            last_ref[:, 0] = rows


def table_kernel(ids_ref, gates_ref, pick_ref, gate_ref):
    firsts = [QUAD * q for q in range(2 * QUADS)]
    for i, (pick, gate) in enumerate(slot_table(ids_ref, gates_ref, firsts)):
        half, q = i // QUADS, i % QUADS
        pick_ref[half, q * QROWS : (q + 1) * QROWS] = pick
        gate_ref[half, q * QROWS : (q + 1) * QROWS] = gate


def sums_kernel(quads, gate, up, down, rows, out_hbm, out, sems):
    columns = [pl.ds(i * FFW, FFW) for i in range(3)]
    stores = copies_of([(out.at[:, c], out_hbm.at[:, c]) for c in columns], sems)
    for q in range(quads.shape[1]):
        block = quads[:, q].astype(F32).reshape(QROWS, 2 * PAIR)
        rows[q * QROWS : (q + 1) * QROWS] = block.astype(BF)
    for i, weights in enumerate((gate, up, down)):
        left = rows[:, :STACK] if i < 2 else rows[:, 2 * PAIR - STACK :]
        out[:, i * FFW : (i + 1) * FFW] = dot(left, weights[...]).astype(BF)
        stores[i].start()
    wait(stores)


def hidden_arrays(gate_sum, up_sum, total):
    logistic = jax.nn.sigmoid(gate_sum)
    silu = gate_sum * logistic
    slope = logistic * (1.0 + gate_sum * (1.0 - logistic))
    return silu * up_sum, total * up_sum * slope, total * silu


def shard_kernel(sums_hbm, out_hbm, sums, out, in_sem, out_sem):
    load = pltpu.make_async_copy(sums_hbm, sums, in_sem.at[0])
    store = pltpu.make_async_copy(out, out_hbm, out_sem.at[0])
    load.start()
    load.wait()
    results = hidden_arrays(*[sums[:, i * FFW : (i + 1) * FFW].astype(F32) for i in range(3)])
    for i, result in enumerate(results):
        out[:, i * FFW : (i + 1) * FFW] = result.astype(BF)
    store.start()
    store.wait()


def add_kernel(parts_ref, out_ref):
    totals = []
    for i in range(3):
        columns = slice(i * FFW, (i + 1) * FFW)
        total = parts_ref[0, :, columns].astype(F32)
        for y in range(1, N_Y):
            total = total + parts_ref[y, :, columns].astype(F32)
        totals.append(total)
    for i, result in enumerate(hidden_arrays(*totals)):
        out_ref[:, i * FFW : (i + 1) * FFW] = result.astype(BF)


def back_parts(full, weights):
    grad = dot_t(full[:, FFW : 2 * FFW], weights[1]) + dot_t(full[:, 2 * FFW :], weights[2])
    return [grad, dot_t(full[:, :FFW], weights[0])]


def back_kernel(full_hbm, gate_hbm, up_hbm, down_hbm, out_ref, full, weights, sems):
    size = full.shape[1] // N_Y
    loads = copies_of(
        [(w, weights.at[i]) for i, w in enumerate((down_hbm, gate_hbm, up_hbm))]
        + [
            (full_hbm.at[pl.ds((2 * y + half) * size, size)], full.at[half, pl.ds(y * size, size)])
            for half in range(2)
            for y in range(N_Y)
        ],
        sems,
    )
    start(loads)
    wait(loads[:3])
    parts = []
    for half in range(2):
        wait(loads[3 + half * N_Y : 3 + (half + 1) * N_Y])
        parts += back_parts(full.at[half], weights)
    result = jnp.concatenate(parts, axis=1)
    for q in range(MAIN):
        block = result[q * QROWS : (q + 1) * QROWS]
        out_ref[:, q] = block.reshape(EXPERTS, QUAD, 2 * PAIR).astype(BF)


def back_last_kernel(core_ref, own, other, gate, up, down, out_ref):
    weights = (down[...], gate[...], up[...])
    own, other = back_parts(own, weights), back_parts(other, weights)
    is_first = core_ref[0] == 0
    result = jnp.where(
        is_first, jnp.concatenate(own + other, axis=1), jnp.concatenate(other + own, axis=1)
    )
    out_ref[:, 0] = result.reshape(EXPERTS, QUAD, 2 * PAIR).astype(BF)


def mix_kernel(pick_ref, gate_ref, main_ref, last_ref, grad_ref, mixed_ref):
    quads = [main_ref[:, q] for q in range(MAIN)] + [last_ref[:, 0]]
    back = jnp.concatenate([q.astype(F32).reshape(QROWS, 2 * PAIR) for q in quads], axis=0)
    totals = []
    for half in range(2):
        skip = half * (PAIR - JOIN)
        lane = iota((1, STACK), 1)
        scale = jnp.where(lane < skip + WIDE, 1.0, gate_ref[half])
        scaled = back[:, half * JOIN : half * JOIN + STACK] * scale
        high = scaled.astype(BF)
        low = (scaled - high.astype(F32)).astype(BF)
        totals.append(t_dot(pick_ref[half], high) + t_dot(pick_ref[half], low))
    total = totals[0][:, :PAIR] + totals[1][:, STACK - PAIR :]
    grad_ref[...] = total[:, :WIDE].astype(BF)
    mixed_ref[...] = total[:, WIDE:].astype(BF)


HBM_SPEC = pl.BlockSpec(memory_space=pltpu.HBM)
VMEM_SPEC = pl.BlockSpec(memory_space=pltpu.VMEM)
SMEM_SPEC = pl.BlockSpec(memory_space=pltpu.SMEM)


def call(kernel, out_shape, *args, **kwargs):
    return pl.pallas_call(
        kernel,
        out_shape=out_shape,
        compiler_params=pltpu.CompilerParams(vmem_limit_bytes=VMEM_LIMIT),
        name=kernel.__name__,
        **kwargs,
    )(*args)


def in_hbm(*arrays):
    return [pltpu.with_memory_space_constraint(a, pltpu.HBM) for a in arrays]


def in_vmem(*arrays):
    return [pltpu.with_memory_space_constraint(a, pltpu.VMEM) for a in arrays]


def buffers(*arrays):
    return [pltpu.VMEM(a.shape, a.dtype) for a in arrays]


def semaphores(*counts):
    return [pltpu.SemaphoreType.DMA((n,)) for n in counts]


def across(quads, axis):
    return lax.all_to_all(quads, axis, split_axis=0, concat_axis=0, tiled=True)


def swap(array):
    return lax.ppermute(array, "core", [(0, 1), (1, 0)])


def after(array, *others):
    return lax.optimization_barrier((array,) + others)[0]


def sums_call(quads, stacks):
    rows = quads.shape[1] * QROWS
    return call(
        sums_kernel,
        [shape(rows, 2 * PAIR), shape(rows, 3 * FFW)],
        quads,
        *in_vmem(*stacks),
        in_specs=[VMEM_SPEC] * 4,
        out_specs=[VMEM_SPEC, HBM_SPEC],
        scratch_shapes=[pltpu.VMEM((rows, 3 * FFW), BF)] + semaphores(3),
    )


def split_features(rows):
    own = jnp.concatenate([rows[:, :WIDE], rows[:, PAIR : PAIR + WIDE]], axis=1)
    other = jnp.concatenate([rows[:, WIDE:PAIR], rows[:, PAIR + WIDE :]], axis=1)
    return own, other


def grad_products(rows, full):
    rows_in, rows_dy = rows[:, :WIDE], rows[:, WIDE:]
    return (
        t_dot(rows_in, full[:, FFW : 2 * FFW]),
        t_dot(rows_in, full[:, 2 * FFW :]),
        t_dot(rows_dy, full[:, :FFW]),
    )


def body(tokens, expert_ids, gate_weights, w_gate, w_up, w_down, cotangent):
    gate_own, up_own, down_own = w_gate[0], w_up[0], w_down[0].T
    core = lax.axis_index("core")
    others = swap(jnp.concatenate([tokens, cotangent], axis=0))
    ids, gates = expert_ids.T, gate_weights.T
    inputs = (ids, gates, tokens, cotangent)
    send_main, send_last = call(
        send_kernel,
        [shape(EXPERTS, MAIN, QUAD, 2 * PAIR), shape(EXPERTS, 1, QUAD, 2 * PAIR)],
        core.reshape(1),
        others,
        *in_hbm(*inputs),
        in_specs=[SMEM_SPEC, VMEM_SPEC] + [HBM_SPEC] * 4,
        scratch_shapes=buffers(*inputs) + semaphores(4),
    )
    quads = across(send_main, "expert")
    gate_sent, up_sent, down_sent, _ = lax.optimization_barrier(
        (gate_own, up_own, down_own, send_main)
    )
    zeros = jnp.zeros((STACK - PAIR, FFW), BF)
    stacks = (
        jnp.concatenate([gate_sent, swap(gate_sent), zeros], axis=0),
        jnp.concatenate([up_sent, swap(up_sent), zeros], axis=0),
        jnp.concatenate([zeros, down_sent, swap(down_sent)], axis=0),
    )
    rows, parts = sums_call(quads, stacks)
    sums = lax.psum_scatter(parts, "y", scatter_dimension=0, tiled=True)

    quads = across(after(send_last, parts), "expert")
    rows_last, parts_last = sums_call(quads, stacks)
    parts_last = across(parts_last.reshape(N_Y, QROWS // N_Y, 3 * FFW), "y")

    sums = after(sums, parts_last)
    shard = call(
        shard_kernel,
        shape(*sums.shape),
        *in_hbm(sums),
        in_specs=[HBM_SPEC],
        out_specs=HBM_SPEC,
        scratch_shapes=buffers(sums, sums) + semaphores(1, 1),
    )
    full = lax.all_gather(shard, ("y", "core"), axis=0, tiled=True)

    shard_last = call(add_kernel, shape(QROWS // N_Y, 3 * FFW), after(parts_last, shard))
    full_last = lax.all_gather(shard_last, "y", axis=0, tiled=True)
    other_last = swap(full_last)
    back_last = call(
        back_last_kernel,
        shape(EXPERTS, 1, QUAD, 2 * PAIR),
        core.reshape(1),
        full_last,
        other_last,
        gate_own,
        up_own,
        down_own,
        in_specs=[SMEM_SPEC] + [VMEM_SPEC] * 5,
    )
    back_last = across(back_last, "expert")

    rows, rows_last, ids, gates, _ = lax.optimization_barrier(
        (rows, rows_last, ids, gates, shard_last)
    )
    pick, slot_gate = call(
        table_kernel,
        [
            shape(2, QUADS * QROWS, tokens.shape[0]),
            shape(2, QUADS * QROWS, 1, dtype=F32),
        ],
        ids,
        gates,
    )
    own, other = split_features(jnp.concatenate([rows, rows_last], axis=0))
    other = swap(other)
    count = MAIN * QROWS
    grads_last = [
        a + b
        for a, b in zip(
            grad_products(own[count:], full_last), grad_products(other[count:], other_last)
        )
    ]
    own, other = own[:count], other[:count]
    first = jnp.where(core == 0, own, other).reshape(N_Y, 1, -1, PAIR)
    second = jnp.where(core == 0, other, own).reshape(N_Y, 1, -1, PAIR)
    own = jnp.concatenate([first, second], axis=1).reshape(2 * count, PAIR)

    full, back_last, own, *grads_last = lax.optimization_barrier(
        (full, back_last, own, *grads_last)
    )
    back = call(
        back_kernel,
        shape(EXPERTS, MAIN, QUAD, 2 * PAIR),
        *in_hbm(full, gate_own, up_own, down_own),
        in_specs=[HBM_SPEC] * 4,
        out_specs=VMEM_SPEC,
        scratch_shapes=[pltpu.VMEM((2, count, 3 * FFW), BF), pltpu.VMEM((3, WIDE, FFW), BF)]
        + semaphores(3 + 2 * N_Y),
    )
    back = across(back, "expert")
    grads = [(a + b).astype(BF) for a, b in zip(grad_products(own, full), grads_last)]
    back = after(back, *grads)
    token_grad, mixed = call(
        mix_kernel, [shape(*tokens.shape)] * 2, pick, slot_gate, back, back_last
    )
    return mixed, token_grad, grads[0][None], grads[1][None], grads[2].T[None]


def solution(mesh):
    fine = Mesh(mesh.devices.reshape(N_Y, 2, EXPERTS), ("y", "core", "expert"))
    dp = ("y", "core")
    placed = (
        P("expert", dp),
        P("expert", None),
        P("expert", None),
        P("expert", dp, None),
        P("expert", dp, None),
        P("expert", None, dp),
        P("expert", dp),
    )
    return jax.shard_map(
        body,
        mesh=fine,
        in_specs=placed,
        out_specs=(
            P("expert", dp),
            P("expert", dp),
            P("expert", dp, None),
            P("expert", dp, None),
            P("expert", None, dp),
        ),
        check_vma=False,
    )
```

time: 205 us -> 212 us (1.034)
  waiting for transfers between devices: 123 us -> 31.2 us
  blocking collectives: 0 us -> 74.1 us
  starting transfers between devices: 37.4 us -> 50.4 us
  matrix products: 7.66 us -> 12 us
  Pallas kernels: 14.5 us -> 17.6 us
  local copies, waits for them, and re-layouts: 1.84 us -> 4.07 us
    all_gather x1, waiting for transfers between devices: 52.4 us -> 0.01 us  [body(): full = lax.all_gather(shard, ('y', 'core'), axis=0, tiled=True)]
    all_to_all x0 -> x2, blocking collectives: none -> 52.3 us  [across(): return lax.all_to_all(quads, axis, split_axis=0, concat_axis=0, tiled=True)]
    reduce_scatter x1, waiting for transfers between devices: 38.2 us -> 1.87 us  [body(): sums = lax.psum_scatter(parts, 'y', scatter_dimension=0, tiled=True)]
    all_gather x0 -> x1, blocking collectives: none -> 21.9 us  [body(): full_last = lax.all_gather(shard_last, 'y', axis=0, tiled=True)]
    ppermute x5 -> x6, starting transfers between devices: 19.8 us -> 27.6 us  [swap(): return lax.ppermute(array, 'core', [(0, 1), (1, 0)])]
    all_to_all x2 -> x3, starting transfers between devices: 17.4 us -> 22.7 us  [across(): return lax.all_to_all(quads, axis, split_axis=0, concat_axis=0, tiled=True)]
    dot_general x3 -> x9, matrix products: 7.66 us -> 12 us  [t_dot(): lax.dot_general(left, right, (((0,), (0,)), ((), ())), preferred_element_...]
    pallas_call x6 -> x9, Pallas kernels: 14.5 us -> 17.6 us  [call(): pl.pallas_call(kernel, out_shape=out_shape, compiler_params=pltpu.Compile...]
  transfers between devices with their start and end apart: 9 -> 11, of which waited for: 7 -> 6; matrix products, arithmetic and copies ran while one was open for 6% -> 8% of each run, Pallas kernels for 0% -> 2%
where the time goes in v5:
time: 212 us; the launch traced here: 209 us
  blocking collectives  74.1 us (35%)
  starting transfers between devices  50.4 us (24%)
  waiting for transfers between devices  31.2 us (15%)
  Pallas kernels  17.6 us (8%)
  between operations  14.4 us (7%)
  matrix products  12 us (6%)
  other arithmetic  5.03 us (2%)
  local copies, waits for them, and re-layouts  4.07 us (2%)
    all_to_all x2, blocking collectives, across(): return lax.all_to_all(quads, axis, split_axis=0, concat_axis=0, tiled=True)  52.3 us
    ppermute x6, starting transfers between devices, swap(): return lax.ppermute(array, 'core', [(0, 1), (1, 0)])  27.6 us
    all_to_all x3, waiting for transfers between devices, across(): return lax.all_to_all(quads, axis, split_axis=0, concat_axis=0, tiled=True)  26.8 us
    all_to_all x3, starting transfers between devices, across(): return lax.all_to_all(quads, axis, split_axis=0, concat_axis=0, tiled=True)  22.7 us
    all_gather x1, blocking collectives, body(): full_last = lax.all_gather(shard_last, 'y', axis=0, tiled=True)  21.9 us
    pallas_call x9, Pallas kernels, call(): pl.pallas_call(kernel, out_shape=out_shape, compiler_params=pltpu.Compile...  17.6 us
    dot_general x9, matrix products, t_dot(): lax.dot_general(left, right, (((0,), (0,)), ((), ())), preferred_element_...  12 us
  transfers between devices with their start and end apart: 11, of which 6 were waited for; matrix products, arithmetic and copies ran while one was open for 8% of the time, Pallas kernels for 2%

profile of v5, /device:TPU:1, one launch (start us, length us, event | category | flops | bytes accessed | tf_op | source)
XLA Modules:
  0.0 208.7 jit_solution(14922102867749606281)
XLA Ops:
  8.0 8.8 %collective-permute-start = (bf16[128,224]{1,0:T(8,128)(2,1)S(1)}, bf16[128,224]{1,0:T(8,128)(2,1)S(1)}, u32[]{:S(2)}, u32[]{:S(2)}) collective-permute-start(bf16[128,224]{1,0:T(8,128)(2,1)S(1)} %pad_maximum_fusion.6), channel_id=1, source_target_pairs={{0,32},{32,0},{1,33},{33,1},{2,34},{34,2},{3,35},{35,3},{4,36},{36... | collective-permute-start | bytes 172040 | tf_op jit(solution)/shard_map/ppermute | solution.py:266
  17.6 2.5 %send_kernel.1 = (bf16[32,3,4,896]{3,2,1,0:T(4,128)(2,1)}, bf16[32,1,4,896]{3,2,1,0:T(4,128)(2,1)S(1)}) custom-call(s32[1]{0:T(128)} %bitcast.core_ref, bf16[128,224]{1,0:T(8,128)(2,1)S(1)} %collective-permute-done.others_ref, s32[8,64]{1,0:T(8,128)} %bitcast.34, f32[8,64]{1,0:T(8,128)} %bitcast.36, bf16[64,224]{1,0:T(8,128)(2,1)} %tokens_hbm.1, ...), custom_call_target="tpu_custom_call" | custom-call | tf_op jit(solution)/shard_map/send_kernel/pallas_call | solution.py:236
  20.1 7.6 %all-to-all-start = ((bf16[32,3,4,896]{3,2,1,0:T(4,128)(2,1)}), bf16[32,3,4,896]{3,2,1,0:T(4,128)(2,1)}, u32[]{:S(2)}, u32[]{:S(2)}) async-start(bf16[32,3,4,896]{3,2,1,0:T(4,128)(2,1)} %get-tuple-element.32), calls=%async_computation | async-start | bytes 1376256 | tf_op jit(solution)/shard_map/all_to_all | solution.py:262
  27.8 2.5 %collective-permute-start.1 = (bf16[224,1024]{1,0:T(8,128)(2,1)}, bf16[224,1024]{1,0:T(8,128)(2,1)S(1)}, u32[]{:S(2)}, u32[]{:S(2)}) collective-permute-start(bf16[224,1024]{1,0:T(8,128)(2,1)} %bitcast.29), channel_id=1, source_target_pairs={{0,32},{32,0},{1,33},{33,1},{2,34},{34,2},{3,35},{35,3},{4,36},{36... | collective-permute-start | bytes 1376264 | tf_op jit(solution)/shard_map/ppermute | solution.py:266
  30.3 1.9 collective-permute-start.2
  32.3 2.4 %collective-permute-start.3 = (bf16[224,1024]{1,0:T(8,128)(2,1)}, bf16[224,1024]{1,0:T(8,128)(2,1)S(1)}, u32[]{:S(2)}, u32[]{:S(2)}) collective-permute-start(bf16[224,1024]{1,0:T(8,128)(2,1)} %bitcast.21), channel_id=1, source_target_pairs={{0,32},{32,0},{1,33},{33,1},{2,34},{34,2},{3,35},{35,3},{4,36},{36... | collective-permute-start | bytes 1376264 | tf_op jit(solution)/shard_map/ppermute | solution.py:266
  38.0 9.4 %all-to-all-done.quads = bf16[32,3,4,896]{3,2,1,0:T(4,128)(2,1)} async-done(((bf16[32,3,4,896]{3,2,1,0:T(4,128)(2,1)}), bf16[32,3,4,896]{3,2,1,0:T(4,128)(2,1)}, u32[]{:S(2)}, u32[]{:S(2)}) %all-to-all-start) | async-done | bytes 688160 | tf_op jit(solution)/shard_map/all_to_all | solution.py:262
  47.4 3.1 %sums_kernel.2 = (bf16[384,896]{1,0:T(8,128)(2,1)S(1)}, bf16[384,3072]{1,0:T(8,128)(2,1)S(1)}) custom-call(bf16[32,3,4,896]{3,2,1,0:T(4,128)(2,1)} %all-to-all-done.quads, bf16[512,1024]{1,0:T(8,128)(2,1)S(1)} %get-tuple-element.67.gate, bf16[512,1024]{1,0:T(8,128)(2,1)S(1)} %get-tuple-element.66.up, bf16[512,1024]{1,0:T(8,128)(2,1)S(1)} %get-tuple-element.65.down), custom_call_target="tpu_custom_call" | custom-call | tf_op jit(solution)/shard_map/sums_kernel/pallas_call | solution.py:236
  52.9 15.4 %all_to_all.25.quads = bf16[32,1,4,896]{3,2,1,0:T(4,128)(2,1)S(1)} all-to-all(bf16[32,1,4,896]{3,2,1,0:T(4,128)(2,1)S(1)} %get-tuple-element.39), channel_id=1, replica_groups=mesh['y'=8,'core'=2,'expert'=32] {'expert'}, dimensions={0} | all-to-all | bytes 458752 | tf_op jit(solution)/shard_map/all_to_all | solution.py:262
  69.3 36.9 %all_to_all.26.parts_ref = bf16[8,16,3072]{2,1,0:T(8,128)(2,1)S(1)} all-to-all(bf16[8,16,3072]{2,1,0:T(8,128)(2,1)S(1)} %bitcast.33), channel_id=1, replica_groups=mesh['y'=8,'core'=2,'expert'=32] {'y'}, dimensions={0} | all-to-all | bytes 1572864 | tf_op jit(solution)/shard_map/all_to_all | solution.py:262
  106.2 1.9 reduce-scatter.2.cloned.1.call-done.sums_hbm
  108.1 1.8 shard_kernel.1
  110.7 4.6 %collective-permute-start.5 = (bf16[512,448]{1,0:T(8,128)(2,1)S(1)}, bf16[512,448]{1,0:T(8,128)(2,1)S(1)}, u32[]{:S(2)}, u32[]{:S(2)}) collective-permute-start(bf16[512,448]{1,0:T(8,128)(2,1)S(1)} %pad_maximum_fusion.4), channel_id=1, source_target_pairs={{0,32},{32,0},{1,33},{33,1},{2,34},{34,2},{3,35},{35,3},{4,36},{36... | collective-permute-start | bytes 1376264 | tf_op jit(solution)/shard_map/ppermute | solution.py:266
  115.4 21.9 %all_gather.7.own = bf16[128,3072]{1,0:T(8,128)(2,1)S(1)} all-gather(bf16[16,3072]{1,0:T(8,128)(2,1)S(1)} %add_kernel.1), channel_id=1, replica_groups=mesh['y'=8,'core'=2,'expert'=32] {'y'}, dimensions={0}, use_global_device_ids=true | all-gather | bytes 884736 | tf_op jit(solution)/shard_map/all_gather | solution.py:345
  137.3 7.3 %collective-permute-start.4 = (bf16[128,3072]{1,0:T(8,128)(2,1)S(1)}, bf16[128,3072]{1,0:T(8,128)(2,1)S(1)}, u32[]{:S(2)}, u32[]{:S(2)}) collective-permute-start(bf16[128,3072]{1,0:T(8,128)(2,1)S(1)} %all_gather.7.own), channel_id=1, source_target_pairs={{0,32},{32,0},{1,33},{33,1},{2,34},{34,2},{3,35},{35,3},{4,36},{36... | collective-permute-start | bytes 2359304 | tf_op jit(solution)/shard_map/ppermute | solution.py:266
  148.8 1.9 back_last_kernel.1
  150.7 10.8 %all-to-all-start.3 = ((bf16[32,1,4,896]{3,2,1,0:T(4,128)(2,1)}), bf16[32,1,4,896]{3,2,1,0:T(4,128)(2,1)S(1)}, u32[]{:S(2)}, u32[]{:S(2)}) async-start(bf16[32,1,4,896]{3,2,1,0:T(4,128)(2,1)} %back_last_kernel.1), calls=%async_computation.4 | async-start | bytes 458752 | tf_op jit(solution)/shard_map/all_to_all | solution.py:262
  161.5 2.6 %convolution_add_fusion = f32[224,1024]{1,0:T(8,128)} fusion(f32[224,1024]{1,0:T(8,128)} %fusion.10, bf16[128,3072]{1,0:T(8,128)(2,1)S(1)} %collective-permute-done.4.other, bf16[512,448]{1,0:T(8,128)(2,1)} %copy-done.12), kind=kOutput, calls=%fused_computation.8 | convolution fusion | flops 58949632 | bytes 2162688 | tf_op jit(solution)/shard_map/dot_general | solution.py:39
  164.1 2.1 %convolution_add_fusion.1 = f32[224,1024]{1,0:T(8,128)} fusion(f32[224,1024]{1,0:T(8,128)S(1)} %fusion.13, bf16[128,3072]{1,0:T(8,128)(2,1)S(1)} %collective-permute-done.4.other, bf16[512,448]{1,0:T(8,128)(2,1)} %copy-done.12), kind=kOutput, calls=%fused_computation.9 | convolution fusion | flops 58949632 | bytes 2162688 | tf_op jit(solution)/shard_map/dot_general | solution.py:39
  167.3 5.4 %all-to-all-done.3.last_ref = bf16[32,1,4,896]{3,2,1,0:T(4,128)(2,1)S(1)} async-done(((bf16[32,1,4,896]{3,2,1,0:T(4,128)(2,1)}), bf16[32,1,4,896]{3,2,1,0:T(4,128)(2,1)S(1)}, u32[]{:S(2)}, u32[]{:S(2)}) %all-to-all-start.3) | async-done | bytes 229408 | tf_op jit(solution)/shard_map/all_to_all | solution.py:262
  172.7 5.2 %back_kernel.1 = bf16[32,3,4,896]{3,2,1,0:T(4,128)(2,1)} custom-call(bf16[768,3072]{1,0:T(8,128)(2,1)} %all-gather.2.cloned.1.call-done.full_hbm, bf16[224,1024]{1,0:T(8,128)(2,1)} %bitcast.31, bf16[224,1024]{1,0:T(8,128)(2,1)} %bitcast.27, bf16[224,1024]{1,0:T(8,128)(2,1)} %bitcast.23), custom_call_target="tpu_custom_call" | custom-call | tf_op jit(solution)/shard_map/back_kernel/pallas_call | solution.py:236
  177.9 4.3 %all-to-all-start.4 = ((bf16[32,3,4,896]{3,2,1,0:T(4,128)(2,1)}), bf16[32,3,4,896]{3,2,1,0:T(4,128)(2,1)S(1)}, u32[]{:S(2)}, u32[]{:S(2)}) async-start(bf16[32,3,4,896]{3,2,1,0:T(4,128)(2,1)} %back_kernel.1), calls=%async_computation.5 | async-start | bytes 1376256 | tf_op jit(solution)/shard_map/all_to_all | solution.py:262
  182.2 2.1 %fusion.4 = f32[224,1024]{1,0:T(8,128)S(1)} fusion(bf16[768,3072]{1,0:T(8,128)(2,1)} %all-gather.2.cloned.1.call-done.full_hbm, bf16[768,448]{1,0:T(8,128)(2,1)S(1)} %bitcast.40), kind=kOutput, calls=%fused_computation.4 | convolution fusion | flops 352321536 | bytes 2883584 | tf_op jit(solution)/shard_map/dot_general | solution.py:39
  188.4 12.0 %all-to-all-done.4.main_ref = bf16[32,3,4,896]{3,2,1,0:T(4,128)(2,1)S(1)} async-done(((bf16[32,3,4,896]{3,2,1,0:T(4,128)(2,1)}), bf16[32,3,4,896]{3,2,1,0:T(4,128)(2,1)S(1)}, u32[]{:S(2)}, u32[]{:S(2)}) %all-to-all-start.4) | async-done | bytes 688160 | tf_op jit(solution)/shard_map/all_to_all | solution.py:262
  (58 shorter events, 20.0 us)
Async XLA Ops:
  8.0 9.7 %collective-permute-start = (bf16[128,224]{1,0:T(8,128)(2,1)S(1)}, bf16[128,224]{1,0:T(8,128)(2,1)S(1)}, u32[]{:S(2)}, u32[]{:S(2)}) collective-permute-start(bf16[128,224]{1,0:T(8,128)(2,1)S(1)} %pad_maximum_fusion.6), channel_id=1, source_target_pairs={{0,32},{32,0},{1,33},{33,1},{2,34},{34,2},{3,35},{35,3},{4,36},{36... | collective-permute-start | bytes 172040 | tf_op jit(solution)/shard_map/ppermute | solution.py:266
  20.1 27.3 %all-to-all-start = ((bf16[32,3,4,896]{3,2,1,0:T(4,128)(2,1)}), bf16[32,3,4,896]{3,2,1,0:T(4,128)(2,1)}, u32[]{:S(2)}, u32[]{:S(2)}) async-start(bf16[32,3,4,896]{3,2,1,0:T(4,128)(2,1)} %get-tuple-element.32), calls=%async_computation | async-start | bytes 1376256 | tf_op jit(solution)/shard_map/all_to_all | solution.py:262
  27.7 80.3 %reduce-scatter.2.cloned.1.call-start = ((), (), s32[]{:S(2)}) async-start(), calls=%async_computation.6 | async-start | bytes 2654208 | tf_op jit(solution)/shard_map/reduce_scatter | solution.py:327
  27.8 6.9 %collective-permute-start.1 = (bf16[224,1024]{1,0:T(8,128)(2,1)}, bf16[224,1024]{1,0:T(8,128)(2,1)S(1)}, u32[]{:S(2)}, u32[]{:S(2)}) collective-permute-start(bf16[224,1024]{1,0:T(8,128)(2,1)} %bitcast.29), channel_id=1, source_target_pairs={{0,32},{32,0},{1,33},{33,1},{2,34},{34,2},{3,35},{35,3},{4,36},{36... | collective-permute-start | bytes 1376264 | tf_op jit(solution)/shard_map/ppermute | solution.py:266
  30.3 4.4 %collective-permute-start.2 = (bf16[224,1024]{1,0:T(8,128)(2,1)}, bf16[224,1024]{1,0:T(8,128)(2,1)S(1)}, u32[]{:S(2)}, u32[]{:S(2)}) collective-permute-start(bf16[224,1024]{1,0:T(8,128)(2,1)} %bitcast.25), channel_id=1, source_target_pairs={{0,32},{32,0},{1,33},{33,1},{2,34},{34,2},{3,35},{35,3},{4,36},{36... | collective-permute-start | bytes 1376264 | tf_op jit(solution)/shard_map/ppermute | solution.py:266
  32.3 4.0 %collective-permute-start.3 = (bf16[224,1024]{1,0:T(8,128)(2,1)}, bf16[224,1024]{1,0:T(8,128)(2,1)S(1)}, u32[]{:S(2)}, u32[]{:S(2)}) collective-permute-start(bf16[224,1024]{1,0:T(8,128)(2,1)} %bitcast.21), channel_id=1, source_target_pairs={{0,32},{32,0},{1,33},{33,1},{2,34},{34,2},{3,35},{35,3},{4,36},{36... | collective-permute-start | bytes 1376264 | tf_op jit(solution)/shard_map/ppermute | solution.py:266
  50.5 1.4 copy-start.3
  51.9 0.9 copy-start.4
  52.8 119.9 %all-gather.2.cloned.1.call-start = ((), (), s32[]{:S(2)}) async-start(), calls=%async_computation.7 | async-start | bytes 5013504 | tf_op jit(solution)/shard_map/all_gather | solution.py:342
  69.3 40.8 %copy-start.5 = (bf16[384,896]{1,0:T(8,128)(2,1)S(1)}, bf16[384,896]{1,0:T(8,128)(2,1)}, u32[]{:S(2)}) copy-start(bf16[384,896]{1,0:T(8,128)(2,1)} %copy-done.4) | copy-start | bytes 2064388
  110.2 34.4 %copy-start.6 = (s32[64,8]{0,1:T(8,128)S(1)}, s32[64,8]{0,1:T(8,128)}, u32[]{:S(2)}) copy-start(s32[64,8]{0,1:T(8,128)} %param.8) | copy-start | bytes 6148
  110.2 34.4 %copy-start.7 = (f32[64,8]{0,1:T(8,128)S(1)}, f32[64,8]{0,1:T(8,128)}, u32[]{:S(2)}) copy-start(f32[64,8]{0,1:T(8,128)} %param.9) | copy-start | bytes 6148
  110.7 37.2 %collective-permute-start.5 = (bf16[512,448]{1,0:T(8,128)(2,1)S(1)}, bf16[512,448]{1,0:T(8,128)(2,1)S(1)}, u32[]{:S(2)}, u32[]{:S(2)}) collective-permute-start(bf16[512,448]{1,0:T(8,128)(2,1)S(1)} %pad_maximum_fusion.4), channel_id=1, source_target_pairs={{0,32},{32,0},{1,33},{33,1},{2,34},{34,2},{3,35},{35,3},{4,36},{36... | collective-permute-start | bytes 1376264 | tf_op jit(solution)/shard_map/ppermute | solution.py:266
  137.3 11.0 %collective-permute-start.4 = (bf16[128,3072]{1,0:T(8,128)(2,1)S(1)}, bf16[128,3072]{1,0:T(8,128)(2,1)S(1)}, u32[]{:S(2)}, u32[]{:S(2)}) collective-permute-start(bf16[128,3072]{1,0:T(8,128)(2,1)S(1)} %all_gather.7.own), channel_id=1, source_target_pairs={{0,32},{32,0},{1,33},{33,1},{2,34},{34,2},{3,35},{35,3},{4,36},{36... | collective-permute-start | bytes 2359304 | tf_op jit(solution)/shard_map/ppermute | solution.py:266
  146.7 2.1 %copy-start = (bf16[1,1024,224]{1,2,0:T(8,128)(2,1)S(1)}, bf16[1,1024,224]{1,2,0:T(8,128)(2,1)}, u32[]{:S(2)}) copy-start(bf16[1,1024,224]{1,2,0:T(8,128)(2,1)} %param.12) | copy-start | bytes 1376260
  146.7 2.1 %copy-start.1 = (bf16[1,224,1024]{2,1,0:T(8,128)(2,1)S(1)}, bf16[1,224,1024]{2,1,0:T(8,128)(2,1)}, u32[]{:S(2)}) copy-start(bf16[1,224,1024]{2,1,0:T(8,128)(2,1)} %param.11) | copy-start | bytes 1376260
  146.7 2.1 copy-start.2
  147.9 0.8 copy-start.12
  150.7 22.0 %all-to-all-start.3 = ((bf16[32,1,4,896]{3,2,1,0:T(4,128)(2,1)}), bf16[32,1,4,896]{3,2,1,0:T(4,128)(2,1)S(1)}, u32[]{:S(2)}, u32[]{:S(2)}) async-start(bf16[32,1,4,896]{3,2,1,0:T(4,128)(2,1)} %back_last_kernel.1), calls=%async_computation.4 | async-start | bytes 458752 | tf_op jit(solution)/shard_map/all_to_all | solution.py:262
  161.5 4.7 %copy-start.9 = (f32[224,1024]{1,0:T(8,128)S(1)}, f32[224,1024]{1,0:T(8,128)}, u32[]{:S(2)}) copy-start(f32[224,1024]{1,0:T(8,128)} %fusion.16) | copy-start | bytes 2752516
  177.9 22.5 %all-to-all-start.4 = ((bf16[32,3,4,896]{3,2,1,0:T(4,128)(2,1)}), bf16[32,3,4,896]{3,2,1,0:T(4,128)(2,1)S(1)}, u32[]{:S(2)}, u32[]{:S(2)}) async-start(bf16[32,3,4,896]{3,2,1,0:T(4,128)(2,1)} %back_kernel.1), calls=%async_computation.5 | async-start | bytes 1376256 | tf_op jit(solution)/shard_map/all_to_all | solution.py:262
  182.2 3.0 %copy-start.8 = (bf16[768,3072]{1,0:T(8,128)(2,1)S(1)}, bf16[768,3072]{1,0:T(8,128)(2,1)}, u32[]{:S(2)}) copy-start(bf16[768,3072]{1,0:T(8,128)(2,1)} %all-gather.2.cloned.1.call-done.full_hbm) | copy-start | bytes 14155780
  185.7 1.2 copy-start.10
  185.7 1.5 copy-start.11
Sparse Core Ops, SparseCore 0:
  53.0 55.0 reduce-scatter.1
  110.8 50.1 all-gather.1

commit v6 on v5

--- a/solution.py
+++ b/solution.py
@@ -12,12 +12,15 @@
 QUADS = HALF // QUAD
 MAIN = QUADS - 1
 QROWS = EXPERTS * QUAD
+ROWS = QUADS * QROWS
 WIDE = 224
 PAIR = 2 * WIDE
 STACK = 512
 JOIN = 2 * PAIR - STACK
 FFW = 1024
 N_Y = 8
+PIECE = QROWS // N_Y
+SHARD = ROWS // N_Y
 BF = jnp.bfloat16
 F32 = jnp.float32
 VMEM_LIMIT = 24 * 1024 * 1024
@@ -85,8 +88,7 @@
     gates_hbm,
     tokens_hbm,
     cotangent_hbm,
-    main_ref,
-    last_ref,
+    out_ref,
     ids_ref,
     gates_ref,
     tokens_ref,
@@ -113,11 +115,8 @@
     )
     for q, (pick, gate) in enumerate(tables):
         scale = jnp.where(iota((1, 2 * PAIR), 1) < PAIR, 1.0, gate)
-        rows = (dot(pick, features) * scale).reshape(EXPERTS, QUAD, 2 * PAIR).astype(BF)
-        if q < MAIN:
-            main_ref[:, q] = rows
-        else:
-            last_ref[:, 0] = rows
+        rows = (dot(pick, features) * scale).reshape(EXPERTS, QUAD, 2 * PAIR)
+        out_ref[:, q] = rows.astype(BF)
 
 
 def table_kernel(ids_ref, gates_ref, pick_ref, gate_ref):
@@ -131,9 +130,11 @@
 def sums_kernel(quads, gate, up, down, rows, out_hbm, out, sems):
     columns = [pl.ds(i * FFW, FFW) for i in range(3)]
     stores = copies_of([(out.at[:, c], out_hbm.at[:, c]) for c in columns], sems)
-    for q in range(quads.shape[1]):
-        block = quads[:, q].astype(F32).reshape(QROWS, 2 * PAIR)
-        rows[q * QROWS : (q + 1) * QROWS] = block.astype(BF)
+    for q in range(QUADS):
+        block = quads[:, q].astype(F32).reshape(QROWS, 2 * PAIR).astype(BF)
+        for y in range(N_Y):
+            at = y * SHARD + q * PIECE
+            rows[at : at + PIECE] = block[y * PIECE : (y + 1) * PIECE]
     for i, weights in enumerate((gate, up, down)):
         left = rows[:, :STACK] if i < 2 else rows[:, 2 * PAIR - STACK :]
         out[:, i * FFW : (i + 1) * FFW] = dot(left, weights[...]).astype(BF)
@@ -141,35 +142,23 @@
     wait(stores)
 
 
-def hidden_arrays(gate_sum, up_sum, total):
+def shard_kernel(sums_hbm, main_hbm, last_hbm, sums, out, in_sem, out_sems):
+    load = pltpu.make_async_copy(sums_hbm, sums, in_sem.at[0])
+    cut = SHARD - PIECE
+    stores = copies_of(
+        ((out.at[pl.ds(0, cut)], main_hbm), (out.at[pl.ds(cut, PIECE)], last_hbm)), out_sems
+    )
+    load.start()
+    load.wait()
+    gate_sum, up_sum, total = [sums[:, i * FFW : (i + 1) * FFW].astype(F32) for i in range(3)]
     logistic = jax.nn.sigmoid(gate_sum)
     silu = gate_sum * logistic
     slope = logistic * (1.0 + gate_sum * (1.0 - logistic))
-    return silu * up_sum, total * up_sum * slope, total * silu
-
-
-def shard_kernel(sums_hbm, out_hbm, sums, out, in_sem, out_sem):
-    load = pltpu.make_async_copy(sums_hbm, sums, in_sem.at[0])
-    store = pltpu.make_async_copy(out, out_hbm, out_sem.at[0])
-    load.start()
-    load.wait()
-    results = hidden_arrays(*[sums[:, i * FFW : (i + 1) * FFW].astype(F32) for i in range(3)])
-    for i, result in enumerate(results):
-        out[:, i * FFW : (i + 1) * FFW] = result.astype(BF)
-    store.start()
-    store.wait()
-
-
-def add_kernel(parts_ref, out_ref):
-    totals = []
-    for i in range(3):
-        columns = slice(i * FFW, (i + 1) * FFW)
-        total = parts_ref[0, :, columns].astype(F32)
-        for y in range(1, N_Y):
-            total = total + parts_ref[y, :, columns].astype(F32)
-        totals.append(total)
-    for i, result in enumerate(hidden_arrays(*totals)):
-        out_ref[:, i * FFW : (i + 1) * FFW] = result.astype(BF)
+    out[:, :FFW] = (silu * up_sum).astype(BF)
+    out[:, FFW : 2 * FFW] = (total * up_sum * slope).astype(BF)
+    out[:, 2 * FFW :] = (total * silu).astype(BF)
+    start(stores)
+    wait(stores)
 
 
 def back_parts(full, weights):
@@ -196,35 +185,49 @@
         parts += back_parts(full.at[half], weights)
     result = jnp.concatenate(parts, axis=1)
     for q in range(MAIN):
-        block = result[q * QROWS : (q + 1) * QROWS]
+        starts = [y * size + q * PIECE for y in range(N_Y)]
+        block = jnp.concatenate([result[at : at + PIECE] for at in starts], axis=0)
         out_ref[:, q] = block.reshape(EXPERTS, QUAD, 2 * PAIR).astype(BF)
 
 
-def back_last_kernel(core_ref, own, other, gate, up, down, out_ref):
-    weights = (down[...], gate[...], up[...])
-    own, other = back_parts(own, weights), back_parts(other, weights)
-    is_first = core_ref[0] == 0
-    result = jnp.where(
-        is_first, jnp.concatenate(own + other, axis=1), jnp.concatenate(other + own, axis=1)
-    )
-    out_ref[:, 0] = result.reshape(EXPERTS, QUAD, 2 * PAIR).astype(BF)
-
-
-def mix_kernel(pick_ref, gate_ref, main_ref, last_ref, grad_ref, mixed_ref):
-    quads = [main_ref[:, q] for q in range(MAIN)] + [last_ref[:, 0]]
+def back_last_kernel(full, gate, up, down, out_ref):
+    result = dot_t(full[:, :FFW], down[...])
+    grad = dot_t(full[:, FFW : 2 * FFW], gate[...]) + dot_t(full[:, 2 * FFW :], up[...])
+    middle = grad[:, JOIN:] + result[:, : STACK - JOIN]
+    rows = jnp.concatenate([grad[:, :JOIN], middle, result[:, STACK - JOIN :]], axis=1)
+    out_ref[:, 0] = rows.reshape(EXPERTS, QUAD, 2 * PAIR).astype(BF)
+
+
+def gated_sum(pick, scaled):
+    high = scaled.astype(BF)
+    low = (scaled - high.astype(F32)).astype(BF)
+    return t_dot(pick, high) + t_dot(pick, low)
+
+
+def mix_last_kernel(core_ref, pick_ref, gate_ref, last_ref, out_ref):
+    back = last_ref[:, 0].astype(F32).reshape(QROWS, 2 * PAIR)
+    rows = pl.ds(MAIN * QROWS, QROWS)
+    scale = jnp.where(iota((1, 2 * PAIR), 1) < PAIR, 1.0, gate_ref[core_ref[0], rows])
+    out_ref[...] = gated_sum(pick_ref[core_ref[0], rows], back * scale)
+
+
+def mix_kernel(pick_ref, gate_ref, main_ref, own_ref, other_ref, grad_ref, mixed_ref):
+    quads = [main_ref[:, q] for q in range(MAIN)]
     back = jnp.concatenate([q.astype(F32).reshape(QROWS, 2 * PAIR) for q in quads], axis=0)
+    rows = slice(0, MAIN * QROWS)
     totals = []
     for half in range(2):
         skip = half * (PAIR - JOIN)
         lane = iota((1, STACK), 1)
-        scale = jnp.where(lane < skip + WIDE, 1.0, gate_ref[half])
+        scale = jnp.where(lane < skip + WIDE, 1.0, gate_ref[half, rows])
         scaled = back[:, half * JOIN : half * JOIN + STACK] * scale
-        high = scaled.astype(BF)
-        low = (scaled - high.astype(F32)).astype(BF)
-        totals.append(t_dot(pick_ref[half], high) + t_dot(pick_ref[half], low))
+        totals.append(gated_sum(pick_ref[half, rows], scaled))
     total = totals[0][:, :PAIR] + totals[1][:, STACK - PAIR :]
-    grad_ref[...] = total[:, :WIDE].astype(BF)
-    mixed_ref[...] = total[:, WIDE:].astype(BF)
+    own, other = own_ref[...], other_ref[...]
+    grad = total[:, :WIDE] + own[:, :WIDE] + other[:, WIDE:PAIR]
+    mixed = total[:, WIDE:] + own[:, PAIR : PAIR + WIDE] + other[:, PAIR + WIDE :]
+    grad_ref[...] = grad.astype(BF)
+    mixed_ref[...] = mixed.astype(BF)
 
 
 HBM_SPEC = pl.BlockSpec(memory_space=pltpu.HBM)
@@ -270,19 +273,6 @@
     return lax.optimization_barrier((array,) + others)[0]
 
 
-def sums_call(quads, stacks):
-    rows = quads.shape[1] * QROWS
-    return call(
-        sums_kernel,
-        [shape(rows, 2 * PAIR), shape(rows, 3 * FFW)],
-        quads,
-        *in_vmem(*stacks),
-        in_specs=[VMEM_SPEC] * 4,
-        out_specs=[VMEM_SPEC, HBM_SPEC],
-        scratch_shapes=[pltpu.VMEM((rows, 3 * FFW), BF)] + semaphores(3),
-    )
-
-
 def split_features(rows):
     own = jnp.concatenate([rows[:, :WIDE], rows[:, PAIR : PAIR + WIDE]], axis=1)
     other = jnp.concatenate([rows[:, WIDE:PAIR], rows[:, PAIR + WIDE :]], axis=1)
@@ -304,102 +294,105 @@
     others = swap(jnp.concatenate([tokens, cotangent], axis=0))
     ids, gates = expert_ids.T, gate_weights.T
     inputs = (ids, gates, tokens, cotangent)
-    send_main, send_last = call(
+    send = call(
         send_kernel,
-        [shape(EXPERTS, MAIN, QUAD, 2 * PAIR), shape(EXPERTS, 1, QUAD, 2 * PAIR)],
+        shape(EXPERTS, QUADS, QUAD, 2 * PAIR),
         core.reshape(1),
         others,
         *in_hbm(*inputs),
         in_specs=[SMEM_SPEC, VMEM_SPEC] + [HBM_SPEC] * 4,
         scratch_shapes=buffers(*inputs) + semaphores(4),
     )
-    quads = across(send_main, "expert")
-    gate_sent, up_sent, down_sent, _ = lax.optimization_barrier(
-        (gate_own, up_own, down_own, send_main)
-    )
+    quads = across(send, "expert")
+    gate_sent, up_sent, down_sent, _ = lax.optimization_barrier((gate_own, up_own, down_own, send))
     zeros = jnp.zeros((STACK - PAIR, FFW), BF)
     stacks = (
         jnp.concatenate([gate_sent, swap(gate_sent), zeros], axis=0),
         jnp.concatenate([up_sent, swap(up_sent), zeros], axis=0),
         jnp.concatenate([zeros, down_sent, swap(down_sent)], axis=0),
     )
-    rows, parts = sums_call(quads, stacks)
+    rows, parts = call(
+        sums_kernel,
+        [shape(ROWS, 2 * PAIR), shape(ROWS, 3 * FFW)],
+        quads,
+        *in_vmem(*stacks),
+        in_specs=[VMEM_SPEC] * 4,
+        out_specs=[VMEM_SPEC, HBM_SPEC],
+        scratch_shapes=[pltpu.VMEM((ROWS, 3 * FFW), BF)] + semaphores(3),
+    )
     sums = lax.psum_scatter(parts, "y", scatter_dimension=0, tiled=True)
 
-    quads = across(after(send_last, parts), "expert")
-    rows_last, parts_last = sums_call(quads, stacks)
-    parts_last = across(parts_last.reshape(N_Y, QROWS // N_Y, 3 * FFW), "y")
-
-    sums = after(sums, parts_last)
-    shard = call(
+    rows, ids, gates, _ = lax.optimization_barrier((rows, ids, gates, parts))
+    pick, slot_gate = call(
+        table_kernel,
+        [shape(2, ROWS, tokens.shape[0]), shape(2, ROWS, 1, dtype=F32)],
+        ids,
+        gates,
+    )
+    own, other = split_features(rows)
+    other = swap(other)
+    own, other = own.reshape(N_Y, SHARD, PAIR), other.reshape(N_Y, SHARD, PAIR)
+    cut = SHARD - PIECE
+    own_last = own[:, cut:].reshape(QROWS, PAIR)
+    other_last = other[:, cut:].reshape(QROWS, PAIR)
+    first = jnp.where(core == 0, own, other)[:, None, :cut]
+    second = jnp.where(core == 0, other, own)[:, None, :cut]
+    main = jnp.concatenate([first, second], axis=1).reshape(2 * MAIN * QROWS, PAIR)
+    sums, main, own_last, other_last, pick, slot_gate = lax.optimization_barrier(
+        (sums, main, own_last, other_last, pick, slot_gate)
+    )
+
+    shard, shard_last = call(
         shard_kernel,
-        shape(*sums.shape),
+        [shape(cut, 3 * FFW), shape(PIECE, 3 * FFW)],
         *in_hbm(sums),
         in_specs=[HBM_SPEC],
-        out_specs=HBM_SPEC,
-        scratch_shapes=buffers(sums, sums) + semaphores(1, 1),
+        out_specs=[HBM_SPEC] * 2,
+        scratch_shapes=buffers(sums, sums) + semaphores(1, 2),
     )
     full = lax.all_gather(shard, ("y", "core"), axis=0, tiled=True)
 
-    shard_last = call(add_kernel, shape(QROWS // N_Y, 3 * FFW), after(parts_last, shard))
     full_last = lax.all_gather(shard_last, "y", axis=0, tiled=True)
-    other_last = swap(full_last)
-    back_last = call(
-        back_last_kernel,
-        shape(EXPERTS, 1, QUAD, 2 * PAIR),
-        core.reshape(1),
-        full_last,
-        other_last,
-        gate_own,
-        up_own,
-        down_own,
-        in_specs=[SMEM_SPEC] + [VMEM_SPEC] * 5,
-    )
-    back_last = across(back_last, "expert")
-
-    rows, rows_last, ids, gates, _ = lax.optimization_barrier(
-        (rows, rows_last, ids, gates, shard_last)
-    )
-    pick, slot_gate = call(
-        table_kernel,
-        [
-            shape(2, QUADS * QROWS, tokens.shape[0]),
-            shape(2, QUADS * QROWS, 1, dtype=F32),
-        ],
-        ids,
-        gates,
-    )
-    own, other = split_features(jnp.concatenate([rows, rows_last], axis=0))
-    other = swap(other)
-    count = MAIN * QROWS
+    send_last = call(
+        back_last_kernel, shape(EXPERTS, 1, QUAD, 2 * PAIR), full_last, *in_vmem(*stacks)
+    )
+    back_last = across(send_last, "expert")
+    full_last = after(full_last, send_last)
     grads_last = [
         a + b
         for a, b in zip(
-            grad_products(own[count:], full_last), grad_products(other[count:], other_last)
+            grad_products(own_last, full_last), grad_products(other_last, swap(full_last))
         )
     ]
-    own, other = own[:count], other[:count]
-    first = jnp.where(core == 0, own, other).reshape(N_Y, 1, -1, PAIR)
-    second = jnp.where(core == 0, other, own).reshape(N_Y, 1, -1, PAIR)
-    own = jnp.concatenate([first, second], axis=1).reshape(2 * count, PAIR)
-
-    full, back_last, own, *grads_last = lax.optimization_barrier(
-        (full, back_last, own, *grads_last)
-    )
+
     back = call(
         back_kernel,
         shape(EXPERTS, MAIN, QUAD, 2 * PAIR),
         *in_hbm(full, gate_own, up_own, down_own),
         in_specs=[HBM_SPEC] * 4,
         out_specs=VMEM_SPEC,
-        scratch_shapes=[pltpu.VMEM((2, count, 3 * FFW), BF), pltpu.VMEM((3, WIDE, FFW), BF)]
+        scratch_shapes=[
+            pltpu.VMEM((2, MAIN * QROWS, 3 * FFW), BF),
+            pltpu.VMEM((3, WIDE, FFW), BF),
+        ]
         + semaphores(3 + 2 * N_Y),
     )
+    back_last = after(back_last, back)
+    total_last = call(
+        mix_last_kernel,
+        shape(tokens.shape[0], 2 * PAIR, dtype=F32),
+        core.reshape(1),
+        pick,
+        slot_gate,
+        back_last,
+        in_specs=[SMEM_SPEC] + [VMEM_SPEC] * 3,
+    )
+    other_total = swap(total_last)
     back = across(back, "expert")
-    grads = [(a + b).astype(BF) for a, b in zip(grad_products(own, full), grads_last)]
-    back = after(back, *grads)
+    grads = [(a + b).astype(BF) for a, b in zip(grad_products(main, full), grads_last)]
+    back = after(back, other_total, *grads)
     token_grad, mixed = call(
-        mix_kernel, [shape(*tokens.shape)] * 2, pick, slot_gate, back, back_last
+        mix_kernel, [shape(*tokens.shape)] * 2, pick, slot_gate, back, total_last, other_total
     )
     return mixed, token_grad, grads[0][None], grads[1][None], grads[2].T[None]
 

time: 212 us -> 204 us (0.962)
  blocking collectives: 74.1 us -> 23.8 us
  waiting for transfers between devices: 31.2 us -> 54.9 us
  starting transfers between devices: 50.4 us -> 60.2 us
  local copies, waits for them, and re-layouts: 4.07 us -> 9.33 us
  matrix products: 12 us -> 15.4 us
    all_to_all x2 -> x0, blocking collectives: 52.3 us -> none  [across(): return lax.all_to_all(quads, axis, split_axis=0, concat_axis=0, tiled=True)]
    reduce_scatter x1, waiting for transfers between devices: 1.87 us -> 30.7 us  [body(): sums = lax.psum_scatter(parts, 'y', scatter_dimension=0, tiled=True)]
    ppermute x6 -> x7, starting transfers between devices: 27.6 us -> 33.5 us  [swap(): return lax.ppermute(array, 'core', [(0, 1), (1, 0)])]
    all_to_all x3, waiting for transfers between devices: 26.8 us -> 21.9 us  [across(): return lax.all_to_all(quads, axis, split_axis=0, concat_axis=0, tiled=True)]
    all_to_all x3, starting transfers between devices: 22.7 us -> 26.6 us  [across(): return lax.all_to_all(quads, axis, split_axis=0, concat_axis=0, tiled=True)]
    dot_general x9, matrix products: 12 us -> 15.4 us  [t_dot(): lax.dot_general(left, right, (((0,), (0,)), ((), ())), preferred_element_...]
    slice x0 -> x2, local copies, waits for them, and re-layouts: none -> 2.23 us  [the longest x1 1.56 us: body(): other_last = other[:, cut:].reshape(QROWS, PAIR)]
    unnamed x27 -> x32, local copies, waits for them, and re-layouts: 3.7 us -> 4.78 us
  transfers between devices with their start and end apart: 11 -> 12, of which waited for: 6 -> 5; matrix products, arithmetic and copies ran while one was open for 8% -> 13% of each run, Pallas kernels for 2% -> 4%
where the time goes in v6:
time: 204 us; the launch traced here: 202 us
  starting transfers between devices  60.2 us (30%)
  waiting for transfers between devices  54.9 us (27%)
  blocking collectives  23.8 us (12%)
  Pallas kernels  17.6 us (9%)
  matrix products  15.4 us (8%)
  between operations  14.4 us (7%)
  local copies, waits for them, and re-layouts  9.33 us (5%)
  other arithmetic  6.75 us (3%)
    ppermute x7, starting transfers between devices, swap(): return lax.ppermute(array, 'core', [(0, 1), (1, 0)])  33.5 us
    reduce_scatter x1, waiting for transfers between devices, body(): sums = lax.psum_scatter(parts, 'y', scatter_dimension=0, tiled=True)  30.7 us
    all_to_all x3, starting transfers between devices, across(): return lax.all_to_all(quads, axis, split_axis=0, concat_axis=0, tiled=True)  26.6 us
    all_gather x1, blocking collectives, body(): full_last = lax.all_gather(shard_last, 'y', axis=0, tiled=True)  23.8 us
    all_to_all x3, waiting for transfers between devices, across(): return lax.all_to_all(quads, axis, split_axis=0, concat_axis=0, tiled=True)  21.9 us
    pallas_call x8, Pallas kernels, call(): pl.pallas_call(kernel, out_shape=out_shape, compiler_params=pltpu.Compile...  17.6 us
    dot_general x9, matrix products, t_dot(): lax.dot_general(left, right, (((0,), (0,)), ((), ())), preferred_element_...  15.4 us
    unnamed x32, local copies, waits for them, and re-layouts  4.78 us
  transfers between devices with their start and end apart: 12, of which 5 were waited for; matrix products, arithmetic and copies ran while one was open for 13% of the time, Pallas kernels for 4%

profile of v6, /device:TPU:1, one launch (start us, length us, event | category | flops | bytes accessed | tf_op | source)
XLA Modules:
  0.0 202.4 jit_solution(7872978193672697003)
XLA Ops:
  8.1 8.8 %collective-permute-start = (bf16[128,224]{1,0:T(8,128)(2,1)S(1)}, bf16[128,224]{1,0:T(8,128)(2,1)S(1)}, u32[]{:S(2)}, u32[]{:S(2)}) collective-permute-start(bf16[128,224]{1,0:T(8,128)(2,1)S(1)} %pad_maximum_fusion.6), channel_id=1, source_target_pairs={{0,32},{32,0},{1,33},{33,1},{2,34},{34,2},{3,35},{35,3},{4,36},{36... | collective-permute-start | bytes 172040 | tf_op jit(solution)/shard_map/ppermute | solution.py:269
  17.8 2.6 %send_kernel.1 = bf16[32,4,4,896]{3,2,1,0:T(4,128)(2,1)} custom-call(s32[1]{0:T(128)} %bitcast.core_ref, bf16[128,224]{1,0:T(8,128)(2,1)S(1)} %collective-permute-done.others_ref, s32[8,64]{1,0:T(8,128)} %bitcast.23, f32[8,64]{1,0:T(8,128)} %bitcast.25, bf16[64,224]{1,0:T(8,128)(2,1)} %tokens_hbm.1, bf16[64,224]{1,0:T(8,128)(2,1)} %cotangent_hbm.1), custom_call_target="tpu_custom_call" | custom-call | tf_op jit(solution)/shard_map/send_kernel/pallas_call | solution.py:239
  20.3 7.6 %all-to-all-start = ((bf16[32,4,4,896]{3,2,1,0:T(4,128)(2,1)}), bf16[32,4,4,896]{3,2,1,0:T(4,128)(2,1)}, u32[]{:S(2)}, u32[]{:S(2)}) async-start(bf16[32,4,4,896]{3,2,1,0:T(4,128)(2,1)} %send_kernel.1), calls=%async_computation | async-start | bytes 1835008 | tf_op jit(solution)/shard_map/all_to_all | solution.py:265
  28.1 2.5 %collective-permute-start.1 = (bf16[224,1024]{1,0:T(8,128)(2,1)S(1)}, bf16[224,1024]{1,0:T(8,128)(2,1)S(1)}, u32[]{:S(2)}, u32[]{:S(2)}) collective-permute-start(bf16[224,1024]{1,0:T(8,128)(2,1)S(1)} %bitcast.37), channel_id=1, source_target_pairs={{0,32},{32,0},{1,33},{33,1},{2,34},{34,2},{3,35},{35,3},{4,36},{36... | collective-permute-start | bytes 1376264 | tf_op jit(solution)/shard_map/ppermute | solution.py:269
  30.6 1.9 collective-permute-start.2
  32.6 2.4 %collective-permute-start.3 = (bf16[224,1024]{1,0:T(8,128)(2,1)S(1)}, bf16[224,1024]{1,0:T(8,128)(2,1)S(1)}, u32[]{:S(2)}, u32[]{:S(2)}) collective-permute-start(bf16[224,1024]{1,0:T(8,128)(2,1)S(1)} %bitcast.31), channel_id=1, source_target_pairs={{0,32},{32,0},{1,33},{33,1},{2,34},{34,2},{3,35},{35,3},{4,36},{36... | collective-permute-start | bytes 1376264 | tf_op jit(solution)/shard_map/ppermute | solution.py:269
  36.4 1.7 pad_maximum_fusion.2
  38.1 13.9 %all-to-all-done.quads = bf16[32,4,4,896]{3,2,1,0:T(4,128)(2,1)} async-done(((bf16[32,4,4,896]{3,2,1,0:T(4,128)(2,1)}), bf16[32,4,4,896]{3,2,1,0:T(4,128)(2,1)}, u32[]{:S(2)}, u32[]{:S(2)}) %all-to-all-start) | async-done | bytes 917536 | tf_op jit(solution)/shard_map/all_to_all | solution.py:265
  52.0 3.9 %sums_kernel.1 = (bf16[512,896]{1,0:T(8,128)(2,1)S(1)}, bf16[512,3072]{1,0:T(8,128)(2,1)S(1)}) custom-call(bf16[32,4,4,896]{3,2,1,0:T(4,128)(2,1)} %all-to-all-done.quads, bf16[512,1024]{1,0:T(8,128)(2,1)S(1)} %get-tuple-element.59.gate, bf16[512,1024]{1,0:T(8,128)(2,1)S(1)} %get-tuple-element.58.up, bf16[512,1024]{1,0:T(8,128)(2,1)S(1)} %get-tuple-element.57.down), custom_call_target="tpu_custom_call" | custom-call | tf_op jit(solution)/shard_map/sums_kernel/pallas_call | solution.py:239
  58.5 2.3 %fusion.45 = (bf16[512,224]{1,0:T(8,128)(2,1)S(1)}, bf16[512,224]{1,0:T(8,128)(2,1)S(1)}, bf16[512,224]{1,0:T(8,128)(2,1)S(1)}, bf16[512,224]{1,0:T(8,128)(2,1)}) fusion(bf16[512,896]{1,0:T(8,128)(2,1)} %copy-done.3), kind=kLoop, calls=%fused_computation.43 | loop fusion | bytes 1835008 | tf_op jit(solution)/shard_map/slice | solution.py:277
  61.8 4.2 %collective-permute-start.4 = (bf16[512,448]{1,0:T(8,128)(2,1)}, bf16[512,448]{1,0:T(8,128)(2,1)}, u32[]{:S(2)}, u32[]{:S(2)}) collective-permute-start(bf16[512,448]{1,0:T(8,128)(2,1)} %pad_maximum_fusion.5), channel_id=1, source_target_pairs={{0,32},{32,0},{1,33},{33,1},{2,34},{34,2},{3,35},{35,3},{4,36},{36... | collective-permute-start | bytes 1376264 | tf_op jit(solution)/shard_map/ppermute | solution.py:269
  72.7 30.7 %reduce-scatter.2.cloned.1.call-done.sums_hbm = bf16[64,3072]{1,0:T(8,128)(2,1)} async-done(((bf16[512,3072]{1,0:T(8,128)(2,1)}), bf16[64,3072]{1,0:T(8,128)(2,1)}) %reduce-scatter.2.cloned.1.call-update) | async-done | bytes 393232 | tf_op jit(solution)/shard_map/reduce_scatter | solution.py:323
  105.6 23.8 %all_gather.7.full = bf16[128,3072]{1,0:T(8,128)(2,1)} all-gather(bf16[16,3072]{1,0:T(8,128)(2,1)S(1)} %get-tuple-element.42), channel_id=1, replica_groups=mesh['y'=8,'core'=2,'expert'=32] {'y'}, dimensions={0}, use_global_device_ids=true | all-gather | bytes 884736 | tf_op jit(solution)/shard_map/all_gather | solution.py:355
  129.4 2.4 %back_last_kernel.1 = bf16[32,1,4,896]{3,2,1,0:T(4,128)(2,1)S(1)} custom-call(bf16[128,3072]{1,0:T(8,128)(2,1)} %all_gather.7.full, bf16[512,1024]{1,0:T(8,128)(2,1)S(1)} %get-tuple-element.59.gate, bf16[512,1024]{1,0:T(8,128)(2,1)S(1)} %get-tuple-element.58.up, bf16[512,1024]{1,0:T(8,128)(2,1)S(1)} %get-tuple-element.57.down), custom_call_target="tpu_custom_call" | custom-call | tf_op jit(solution)/shard_map/back_last_kernel/pallas_call | solution.py:239
  132.4 10.9 %collective-permute-start.6 = (bf16[128,3072]{1,0:T(8,128)(2,1)}, bf16[128,3072]{1,0:T(8,128)(2,1)}, u32[]{:S(2)}, u32[]{:S(2)}) collective-permute-start(bf16[128,3072]{1,0:T(8,128)(2,1)} %all_gather.7.full), channel_id=1, source_target_pairs={{0,32},{32,0},{1,33},{33,1},{2,34},{34,2},{3,35},{35,3},{4,36},{36... | collective-permute-start | bytes 2359304 | tf_op jit(solution)/shard_map/ppermute | solution.py:269
  143.3 9.8 %all-to-all-start.2 = ((bf16[32,1,4,896]{3,2,1,0:T(4,128)(2,1)}), bf16[32,1,4,896]{3,2,1,0:T(4,128)(2,1)S(1)}, u32[]{:S(2)}, u32[]{:S(2)}) async-start(bf16[32,1,4,896]{3,2,1,0:T(4,128)(2,1)} %copy-done.4), calls=%async_computation.3 | async-start | bytes 458752 | tf_op jit(solution)/shard_map/all_to_all | solution.py:265
  154.4 2.2 %fusion.35 = f32[224,1024]{1,0:T(8,128)} fusion(bf16[128,3072]{1,0:T(8,128)(2,1)} %all_gather.7.full, bf16[128,448]{1,0:T(8,128)(2,1)S(1)} %bitcast.42), kind=kOutput, calls=%fused_computation.32 | convolution fusion | flops 58720256 | bytes 1245184 | tf_op jit(solution)/shard_map/dot_general | solution.py:42
  157.9 2.3 %convolution_add_fusion = f32[1024,224]{0,1:T(8,128)} fusion(f32[1024,224]{0,1:T(8,128)S(1)} %fusion.33, bf16[128,3072]{1,0:T(8,128)(2,1)} %collective-permute-done.6, bf16[128,448]{1,0:T(8,128)(2,1)S(1)} %bitcast.38), kind=kOutput, calls=%fused_computation.11 | convolution fusion | flops 58949632 | bytes 2162688 | tf_op jit(solution)/shard_map/dot_general | solution.py:42
  160.2 5.2 %back_kernel.1 = bf16[32,3,4,896]{3,2,1,0:T(4,128)(2,1)} custom-call(bf16[768,3072]{1,0:T(8,128)(2,1)} %all-gather.2.cloned.1.call-done.full_hbm, bf16[224,1024]{1,0:T(8,128)(2,1)} %bitcast.36, bf16[224,1024]{1,0:T(8,128)(2,1)} %bitcast.33, bf16[224,1024]{1,0:T(8,128)(2,1)} %bitcast.30), custom_call_target="tpu_custom_call" | custom-call | tf_op jit(solution)/shard_map/back_kernel/pallas_call | solution.py:239
  165.5 9.2 %all-to-all-start.1 = ((bf16[32,3,4,896]{3,2,1,0:T(4,128)(2,1)}), bf16[32,3,4,896]{3,2,1,0:T(4,128)(2,1)S(1)}, u32[]{:S(2)}, u32[]{:S(2)}) async-start(bf16[32,3,4,896]{3,2,1,0:T(4,128)(2,1)} %back_kernel.1), calls=%async_computation.2 | async-start | bytes 1376256 | tf_op jit(solution)/shard_map/all_to_all | solution.py:265
  174.7 1.7 convolution_add_fusion.1
  178.2 2.8 %collective-permute-start.5 = (f32[64,896]{1,0:T(8,128)S(1)}, f32[64,896]{1,0:T(8,128)S(1)}, u32[]{:S(2)}, u32[]{:S(2)}) collective-permute-start(f32[64,896]{1,0:T(8,128)S(1)} %mix_last_kernel.1.own_ref), channel_id=1, source_target_pairs={{0,32},{32,0},{1,33},{33,1},{2,34},{34,2},{3,35},{35,3},{4,36},{36... | collective-permute-start | bytes 688136 | tf_op jit(solution)/shard_map/ppermute | solution.py:269
  181.0 2.3 %fusion.18 = bf16[224,1024]{1,0:T(8,128)(2,1)} fusion(f32[224,1024]{1,0:T(8,128)S(1)} %convolution_add_fusion.1, bf16[768,3072]{1,0:T(8,128)(2,1)S(1)} %copy-done.8, bf16[768,448]{1,0:T(8,128)(2,1)} %bitcast.44), kind=kOutput, calls=%fused_computation.15 | convolution fusion | flops 352780288 | bytes 3342336 | tf_op jit(solution)/shard_map/dot_general | solution.py:42
  186.2 8.0 %all-to-all-done.1.main_ref = bf16[32,3,4,896]{3,2,1,0:T(4,128)(2,1)S(1)} async-done(((bf16[32,3,4,896]{3,2,1,0:T(4,128)(2,1)}), bf16[32,3,4,896]{3,2,1,0:T(4,128)(2,1)S(1)}, u32[]{:S(2)}, u32[]{:S(2)}) %all-to-all-start.1) | async-done | bytes 688160 | tf_op jit(solution)/shard_map/all_to_all | solution.py:265
  (62 shorter events, 24.9 us)
Async XLA Ops:
  7.2 20.9 %copy-start.11 = (bf16[1,224,1024]{2,1,0:T(8,128)(2,1)S(1)}, bf16[1,224,1024]{2,1,0:T(8,128)(2,1)}, u32[]{:S(2)}) copy-start(bf16[1,224,1024]{2,1,0:T(8,128)(2,1)} %param.10) | copy-start | bytes 1376260
  7.2 23.4 %copy-start.10 = (bf16[1,224,1024]{2,1,0:T(8,128)(2,1)S(1)}, bf16[1,224,1024]{2,1,0:T(8,128)(2,1)}, u32[]{:S(2)}) copy-start(bf16[1,224,1024]{2,1,0:T(8,128)(2,1)} %param.11) | copy-start | bytes 1376260
  7.2 25.4 %copy-start.9 = (bf16[1,1024,224]{1,2,0:T(8,128)(2,1)S(1)}, bf16[1,1024,224]{1,2,0:T(8,128)(2,1)}, u32[]{:S(2)}) copy-start(bf16[1,1024,224]{1,2,0:T(8,128)(2,1)} %param.12) | copy-start | bytes 1376260
  8.1 9.7 %collective-permute-start = (bf16[128,224]{1,0:T(8,128)(2,1)S(1)}, bf16[128,224]{1,0:T(8,128)(2,1)S(1)}, u32[]{:S(2)}, u32[]{:S(2)}) collective-permute-start(bf16[128,224]{1,0:T(8,128)(2,1)S(1)} %pad_maximum_fusion.6), channel_id=1, source_target_pairs={{0,32},{32,0},{1,33},{33,1},{2,34},{34,2},{3,35},{35,3},{4,36},{36... | collective-permute-start | bytes 172040 | tf_op jit(solution)/shard_map/ppermute | solution.py:269
  20.3 31.6 %all-to-all-start = ((bf16[32,4,4,896]{3,2,1,0:T(4,128)(2,1)}), bf16[32,4,4,896]{3,2,1,0:T(4,128)(2,1)}, u32[]{:S(2)}, u32[]{:S(2)}) async-start(bf16[32,4,4,896]{3,2,1,0:T(4,128)(2,1)} %send_kernel.1), calls=%async_computation | async-start | bytes 1835008 | tf_op jit(solution)/shard_map/all_to_all | solution.py:265
  28.0 75.4 %reduce-scatter.2.cloned.1.call-start = ((), (), s32[]{:S(2)}) async-start(), calls=%async_computation.4 | async-start | bytes 3538944 | tf_op jit(solution)/shard_map/reduce_scatter | solution.py:323
  28.1 6.9 %collective-permute-start.1 = (bf16[224,1024]{1,0:T(8,128)(2,1)S(1)}, bf16[224,1024]{1,0:T(8,128)(2,1)S(1)}, u32[]{:S(2)}, u32[]{:S(2)}) collective-permute-start(bf16[224,1024]{1,0:T(8,128)(2,1)S(1)} %bitcast.37), channel_id=1, source_target_pairs={{0,32},{32,0},{1,33},{33,1},{2,34},{34,2},{3,35},{35,3},{4,36},{36... | collective-permute-start | bytes 1376264 | tf_op jit(solution)/shard_map/ppermute | solution.py:269
  30.6 4.4 %collective-permute-start.2 = (bf16[224,1024]{1,0:T(8,128)(2,1)S(1)}, bf16[224,1024]{1,0:T(8,128)(2,1)S(1)}, u32[]{:S(2)}, u32[]{:S(2)}) collective-permute-start(bf16[224,1024]{1,0:T(8,128)(2,1)S(1)} %bitcast.34), channel_id=1, source_target_pairs={{0,32},{32,0},{1,33},{33,1},{2,34},{34,2},{3,35},{35,3},{4,36},{36... | collective-permute-start | bytes 1376264 | tf_op jit(solution)/shard_map/ppermute | solution.py:269
  32.6 3.8 %collective-permute-start.3 = (bf16[224,1024]{1,0:T(8,128)(2,1)S(1)}, bf16[224,1024]{1,0:T(8,128)(2,1)S(1)}, u32[]{:S(2)}, u32[]{:S(2)}) collective-permute-start(bf16[224,1024]{1,0:T(8,128)(2,1)S(1)} %bitcast.31), channel_id=1, source_target_pairs={{0,32},{32,0},{1,33},{33,1},{2,34},{34,2},{3,35},{35,3},{4,36},{36... | collective-permute-start | bytes 1376264 | tf_op jit(solution)/shard_map/ppermute | solution.py:269
  55.8 1.6 copy-start
  58.4 101.8 %all-gather.2.cloned.1.call-start = ((), (), s32[]{:S(2)}) async-start(), calls=%async_computation.5 | async-start | bytes 5013504 | tf_op jit(solution)/shard_map/all_gather | solution.py:353
  58.5 9.3 %copy-start.6 = (s32[64,8]{0,1:T(8,128)S(1)}, s32[64,8]{0,1:T(8,128)}, u32[]{:S(2)}) copy-start(s32[64,8]{0,1:T(8,128)} %param.8) | copy-start | bytes 6148
  58.5 9.3 %copy-start.7 = (f32[64,8]{0,1:T(8,128)S(1)}, f32[64,8]{0,1:T(8,128)}, u32[]{:S(2)}) copy-start(f32[64,8]{0,1:T(8,128)} %param.9) | copy-start | bytes 6148
  61.8 7.3 %collective-permute-start.4 = (bf16[512,448]{1,0:T(8,128)(2,1)}, bf16[512,448]{1,0:T(8,128)(2,1)}, u32[]{:S(2)}, u32[]{:S(2)}) collective-permute-start(bf16[512,448]{1,0:T(8,128)(2,1)} %pad_maximum_fusion.5), channel_id=1, source_target_pairs={{0,32},{32,0},{1,33},{33,1},{2,34},{34,2},{3,35},{35,3},{4,36},{36... | collective-permute-start | bytes 1376264 | tf_op jit(solution)/shard_map/ppermute | solution.py:269
  129.4 23.7 %copy-start.14 = (bf16[8,16,448]{2,1,0:T(8,128)(2,1)S(1)}, bf16[8,16,448]{2,1,0:T(8,128)(2,1)}, u32[]{:S(2)}) copy-start(bf16[8,16,448]{2,1,0:T(8,128)(2,1)} %slice.96) | copy-start | bytes 344068
  132.4 25.5 %copy-start.13 = (bf16[8,16,448]{2,1,0:T(8,128)(2,1)S(1)}, bf16[8,16,448]{2,1,0:T(8,128)(2,1)}, u32[]{:S(2)}) copy-start(bf16[8,16,448]{2,1,0:T(8,128)(2,1)} %slice.97) | copy-start | bytes 344068
  132.4 25.5 %collective-permute-start.6 = (bf16[128,3072]{1,0:T(8,128)(2,1)}, bf16[128,3072]{1,0:T(8,128)(2,1)}, u32[]{:S(2)}, u32[]{:S(2)}) collective-permute-start(bf16[128,3072]{1,0:T(8,128)(2,1)} %all_gather.7.full), channel_id=1, source_target_pairs={{0,32},{32,0},{1,33},{33,1},{2,34},{34,2},{3,35},{35,3},{4,36},{36... | collective-permute-start | bytes 2359304 | tf_op jit(solution)/shard_map/ppermute | solution.py:269
  143.3 22.1 %all-to-all-start.2 = ((bf16[32,1,4,896]{3,2,1,0:T(4,128)(2,1)}), bf16[32,1,4,896]{3,2,1,0:T(4,128)(2,1)S(1)}, u32[]{:S(2)}, u32[]{:S(2)}) async-start(bf16[32,1,4,896]{3,2,1,0:T(4,128)(2,1)} %copy-done.4), calls=%async_computation.3 | async-start | bytes 458752 | tf_op jit(solution)/shard_map/all_to_all | solution.py:265
  165.5 28.7 %all-to-all-start.1 = ((bf16[32,3,4,896]{3,2,1,0:T(4,128)(2,1)}), bf16[32,3,4,896]{3,2,1,0:T(4,128)(2,1)S(1)}, u32[]{:S(2)}, u32[]{:S(2)}) async-start(bf16[32,3,4,896]{3,2,1,0:T(4,128)(2,1)} %back_kernel.1), calls=%async_computation.2 | async-start | bytes 1376256 | tf_op jit(solution)/shard_map/all_to_all | solution.py:265
  174.7 3.2 %copy-start.2 = (f32[2,512,1]{2,1,0:T(8,128)S(1)}, f32[2,512,1]{2,1,0:T(8,128)}, u32[]{:S(2)}) copy-start(f32[2,512,1]{2,1,0:T(8,128)} %copy-done.1) | copy-start | bytes 12292
  174.7 6.3 %copy-start.8 = (bf16[768,3072]{1,0:T(8,128)(2,1)S(1)}, bf16[768,3072]{1,0:T(8,128)(2,1)}, u32[]{:S(2)}) copy-start(bf16[768,3072]{1,0:T(8,128)(2,1)} %all-gather.2.cloned.1.call-done.full_hbm) | copy-start | bytes 14155780
  177.9 5.5 %copy-start.15 = (bf16[8,2,48,448]{3,2,1,0:T(8,128)(2,1)S(1)}, bf16[8,2,48,448]{3,2,1,0:T(8,128)(2,1)}, u32[]{:S(2)}) copy-start(bf16[8,2,48,448]{3,2,1,0:T(8,128)(2,1)} %pad_maximum_fusion.3) | copy-start | bytes 2064388
  178.2 7.9 %collective-permute-start.5 = (f32[64,896]{1,0:T(8,128)S(1)}, f32[64,896]{1,0:T(8,128)S(1)}, u32[]{:S(2)}, u32[]{:S(2)}) collective-permute-start(f32[64,896]{1,0:T(8,128)S(1)} %mix_last_kernel.1.own_ref), channel_id=1, source_target_pairs={{0,32},{32,0},{1,33},{33,1},{2,34},{34,2},{3,35},{35,3},{4,36},{36... | collective-permute-start | bytes 688136 | tf_op jit(solution)/shard_map/ppermute | solution.py:269
  183.3 1.3 copy-start.12
  (4 other events, 3.1 us)
Sparse Core Ops, SparseCore 0:
  58.5 44.8 reduce-scatter.1
  106.1 50.0 all-gather.1

commit v7 on v6

--- a/solution.py
+++ b/solution.py
@@ -127,7 +127,7 @@
         gate_ref[half, q * QROWS : (q + 1) * QROWS] = gate
 
 
-def sums_kernel(quads, gate, up, down, rows, out_hbm, out, sems):
+def sums_kernel(quads, gate, up, down, rows_hbm, out_hbm, rows, out, sems):
     columns = [pl.ds(i * FFW, FFW) for i in range(3)]
     stores = copies_of([(out.at[:, c], out_hbm.at[:, c]) for c in columns], sems)
     for q in range(QUADS):
@@ -135,30 +135,32 @@
         for y in range(N_Y):
             at = y * SHARD + q * PIECE
             rows[at : at + PIECE] = block[y * PIECE : (y + 1) * PIECE]
+    rows_store = pltpu.make_async_copy(rows, rows_hbm, sems.at[3])
+    rows_store.start()
     for i, weights in enumerate((gate, up, down)):
         left = rows[:, :STACK] if i < 2 else rows[:, 2 * PAIR - STACK :]
         out[:, i * FFW : (i + 1) * FFW] = dot(left, weights[...]).astype(BF)
         stores[i].start()
-    wait(stores)
-
-
-def shard_kernel(sums_hbm, main_hbm, last_hbm, sums, out, in_sem, out_sems):
+    wait(stores + [rows_store])
+
+
+def shard_kernel(sums_hbm, main_hbm, last_ref, sums, main, in_sem, out_sem):
     load = pltpu.make_async_copy(sums_hbm, sums, in_sem.at[0])
-    cut = SHARD - PIECE
-    stores = copies_of(
-        ((out.at[pl.ds(0, cut)], main_hbm), (out.at[pl.ds(cut, PIECE)], last_hbm)), out_sems
-    )
+    store = pltpu.make_async_copy(main, main_hbm, out_sem.at[0])
     load.start()
     load.wait()
     gate_sum, up_sum, total = [sums[:, i * FFW : (i + 1) * FFW].astype(F32) for i in range(3)]
     logistic = jax.nn.sigmoid(gate_sum)
     silu = gate_sum * logistic
     slope = logistic * (1.0 + gate_sum * (1.0 - logistic))
-    out[:, :FFW] = (silu * up_sum).astype(BF)
-    out[:, FFW : 2 * FFW] = (total * up_sum * slope).astype(BF)
-    out[:, 2 * FFW :] = (total * silu).astype(BF)
-    start(stores)
-    wait(stores)
+    results = [silu * up_sum, total * up_sum * slope, total * silu]
+    cut = SHARD - PIECE
+    for i, result in enumerate(results):
+        main[:, i * FFW : (i + 1) * FFW] = result[:cut].astype(BF)
+    store.start()
+    for i, result in enumerate(results):
+        last_ref[:, i * FFW : (i + 1) * FFW] = result[cut:].astype(BF)
+    store.wait()
 
 
 def back_parts(full, weights):
@@ -313,12 +315,13 @@
     )
     rows, parts = call(
         sums_kernel,
-        [shape(ROWS, 2 * PAIR), shape(ROWS, 3 * FFW)],
+        [pltpu.HBM((ROWS, 2 * PAIR), BF), pltpu.HBM((ROWS, 3 * FFW), BF)],
         quads,
         *in_vmem(*stacks),
         in_specs=[VMEM_SPEC] * 4,
-        out_specs=[VMEM_SPEC, HBM_SPEC],
-        scratch_shapes=[pltpu.VMEM((ROWS, 3 * FFW), BF)] + semaphores(3),
+        out_specs=[HBM_SPEC] * 2,
+        scratch_shapes=[pltpu.VMEM((ROWS, 2 * PAIR), BF), pltpu.VMEM((ROWS, 3 * FFW), BF)]
+        + semaphores(4),
     )
     sums = lax.psum_scatter(parts, "y", scatter_dimension=0, tiled=True)
 
@@ -342,13 +345,14 @@
         (sums, main, own_last, other_last, pick, slot_gate)
     )
 
+    shard_shape = shape(cut, 3 * FFW)
     shard, shard_last = call(
         shard_kernel,
-        [shape(cut, 3 * FFW), shape(PIECE, 3 * FFW)],
+        [pltpu.HBM((cut, 3 * FFW), BF), shape(PIECE, 3 * FFW)],
         *in_hbm(sums),
         in_specs=[HBM_SPEC],
-        out_specs=[HBM_SPEC] * 2,
-        scratch_shapes=buffers(sums, sums) + semaphores(1, 2),
+        out_specs=[HBM_SPEC, VMEM_SPEC],
+        scratch_shapes=buffers(sums, shard_shape) + semaphores(1, 1),
     )
     full = lax.all_gather(shard, ("y", "core"), axis=0, tiled=True)
 
@@ -357,13 +361,6 @@
         back_last_kernel, shape(EXPERTS, 1, QUAD, 2 * PAIR), full_last, *in_vmem(*stacks)
     )
     back_last = across(send_last, "expert")
-    full_last = after(full_last, send_last)
-    grads_last = [
-        a + b
-        for a, b in zip(
-            grad_products(own_last, full_last), grad_products(other_last, swap(full_last))
-        )
-    ]
 
     back = call(
         back_kernel,
@@ -389,6 +386,13 @@
     )
     other_total = swap(total_last)
     back = across(back, "expert")
+    full_last = after(full_last, total_last)
+    grads_last = [
+        a + b
+        for a, b in zip(
+            grad_products(own_last, full_last), grad_products(other_last, swap(full_last))
+        )
+    ]
     grads = [(a + b).astype(BF) for a, b in zip(grad_products(main, full), grads_last)]
     back = after(back, other_total, *grads)
     token_grad, mixed = call(

time: 204 us -> 202 us (level)
  waiting for transfers between devices: 54.9 us -> 73.8 us
  starting transfers between devices: 60.2 us -> 52.1 us
  matrix products: 15.4 us -> 9.19 us
  blocking collectives: 23.8 us -> 20.6 us
  local copies, waits for them, and re-layouts: 9.33 us -> 6.99 us
    all_gather x1, waiting for transfers between devices: 0.01 us -> 16.4 us  [body(): full = lax.all_gather(shard, ('y', 'core'), axis=0, tiled=True)]
    ppermute x7, starting transfers between devices: 33.5 us -> 24.2 us  [swap(): return lax.ppermute(array, 'core', [(0, 1), (1, 0)])]
    dot_general x9, matrix products: 15.4 us -> 9.19 us  [t_dot(): lax.dot_general(left, right, (((0,), (0,)), ((), ())), preferred_element_...]
    all_gather x1, blocking collectives: 23.8 us -> 20.6 us  [body(): full_last = lax.all_gather(shard_last, 'y', axis=0, tiled=True)]
    unnamed x32 -> x28, local copies, waits for them, and re-layouts: 4.78 us -> 2.43 us
    all_to_all x3, waiting for transfers between devices: 21.9 us -> 24.2 us  [across(): return lax.all_to_all(quads, axis, split_axis=0, concat_axis=0, tiled=True)]
  transfers between devices with their start and end apart: 12 -> 12, of which waited for: 5 -> 6; matrix products, arithmetic and copies ran while one was open for 13% -> 10% of each run, Pallas kernels for 4% -> 3%
where the time goes in v7:
time: 202 us; the launch traced here: 201 us
  waiting for transfers between devices  73.8 us (37%)
  starting transfers between devices  52.1 us (26%)
  blocking collectives  20.6 us (10%)
  Pallas kernels  17.1 us (8%)
  between operations  14.4 us (7%)
  matrix products  9.19 us (5%)
  local copies, waits for them, and re-layouts  6.99 us (3%)
  other arithmetic  6.81 us (3%)
    reduce_scatter x1, waiting for transfers between devices, body(): sums = lax.psum_scatter(parts, 'y', scatter_dimension=0, tiled=True)  30.8 us
    all_to_all x3, starting transfers between devices, across(): return lax.all_to_all(quads, axis, split_axis=0, concat_axis=0, tiled=True)  27.9 us
    all_to_all x3, waiting for transfers between devices, across(): return lax.all_to_all(quads, axis, split_axis=0, concat_axis=0, tiled=True)  24.2 us
    ppermute x7, starting transfers between devices, swap(): return lax.ppermute(array, 'core', [(0, 1), (1, 0)])  24.2 us
    all_gather x1, blocking collectives, body(): full_last = lax.all_gather(shard_last, 'y', axis=0, tiled=True)  20.6 us
    pallas_call x8, Pallas kernels, call(): pl.pallas_call(kernel, out_shape=out_shape, compiler_params=pltpu.Compile...  17.1 us
    all_gather x1, waiting for transfers between devices, body(): full = lax.all_gather(shard, ('y', 'core'), axis=0, tiled=True)  16.4 us
    dot_general x9, matrix products, t_dot(): lax.dot_general(left, right, (((0,), (0,)), ((), ())), preferred_element_...  9.19 us
  transfers between devices with their start and end apart: 12, of which 6 were waited for; matrix products, arithmetic and copies ran while one was open for 10% of the time, Pallas kernels for 3%

profile of v7, /device:TPU:1, one launch (start us, length us, event | category | flops | bytes accessed | tf_op | source)
XLA Modules:
  0.0 201.0 jit_solution(9670117312118617533)
XLA Ops:
  8.1 8.8 %collective-permute-start = (bf16[128,224]{1,0:T(8,128)(2,1)S(1)}, bf16[128,224]{1,0:T(8,128)(2,1)S(1)}, u32[]{:S(2)}, u32[]{:S(2)}) collective-permute-start(bf16[128,224]{1,0:T(8,128)(2,1)S(1)} %pad_maximum_fusion.6), channel_id=1, source_target_pairs={{0,32},{32,0},{1,33},{33,1},{2,34},{34,2},{3,35},{35,3},{4,36},{36... | collective-permute-start | bytes 172040 | tf_op jit(solution)/shard_map/ppermute | solution.py:271
  17.8 2.6 %send_kernel.1 = bf16[32,4,4,896]{3,2,1,0:T(4,128)(2,1)} custom-call(s32[1]{0:T(128)} %bitcast.core_ref, bf16[128,224]{1,0:T(8,128)(2,1)S(1)} %collective-permute-done.others_ref, s32[8,64]{1,0:T(8,128)} %bitcast.23, f32[8,64]{1,0:T(8,128)} %bitcast.25, bf16[64,224]{1,0:T(8,128)(2,1)} %tokens_hbm.1, bf16[64,224]{1,0:T(8,128)(2,1)} %cotangent_hbm.1), custom_call_target="tpu_custom_call" | custom-call | tf_op jit(solution)/shard_map/send_kernel/pallas_call | solution.py:241
  20.4 7.6 %all-to-all-start = ((bf16[32,4,4,896]{3,2,1,0:T(4,128)(2,1)}), bf16[32,4,4,896]{3,2,1,0:T(4,128)(2,1)}, u32[]{:S(2)}, u32[]{:S(2)}) async-start(bf16[32,4,4,896]{3,2,1,0:T(4,128)(2,1)} %send_kernel.1), calls=%async_computation | async-start | bytes 1835008 | tf_op jit(solution)/shard_map/all_to_all | solution.py:267
  28.1 2.5 %collective-permute-start.1 = (bf16[224,1024]{1,0:T(8,128)(2,1)S(1)}, bf16[224,1024]{1,0:T(8,128)(2,1)S(1)}, u32[]{:S(2)}, u32[]{:S(2)}) collective-permute-start(bf16[224,1024]{1,0:T(8,128)(2,1)S(1)} %bitcast.37), channel_id=1, source_target_pairs={{0,32},{32,0},{1,33},{33,1},{2,34},{34,2},{3,35},{35,3},{4,36},{36... | collective-permute-start | bytes 1376264 | tf_op jit(solution)/shard_map/ppermute | solution.py:271
  30.6 1.9 collective-permute-start.2
  32.6 2.4 %collective-permute-start.3 = (bf16[224,1024]{1,0:T(8,128)(2,1)S(1)}, bf16[224,1024]{1,0:T(8,128)(2,1)S(1)}, u32[]{:S(2)}, u32[]{:S(2)}) collective-permute-start(bf16[224,1024]{1,0:T(8,128)(2,1)S(1)} %bitcast.31), channel_id=1, source_target_pairs={{0,32},{32,0},{1,33},{33,1},{2,34},{34,2},{3,35},{35,3},{4,36},{36... | collective-permute-start | bytes 1376264 | tf_op jit(solution)/shard_map/ppermute | solution.py:271
  36.4 1.7 pad_maximum_fusion.2
  38.1 13.9 %all-to-all-done.quads = bf16[32,4,4,896]{3,2,1,0:T(4,128)(2,1)} async-done(((bf16[32,4,4,896]{3,2,1,0:T(4,128)(2,1)}), bf16[32,4,4,896]{3,2,1,0:T(4,128)(2,1)}, u32[]{:S(2)}, u32[]{:S(2)}) %all-to-all-start) | async-done | bytes 917536 | tf_op jit(solution)/shard_map/all_to_all | solution.py:267
  52.0 4.1 %sums_kernel.1 = (bf16[512,896]{1,0:T(8,128)(2,1)}, bf16[512,3072]{1,0:T(8,128)(2,1)}) custom-call(bf16[32,4,4,896]{3,2,1,0:T(4,128)(2,1)} %all-to-all-done.quads, bf16[512,1024]{1,0:T(8,128)(2,1)S(1)} %get-tuple-element.59.gate, bf16[512,1024]{1,0:T(8,128)(2,1)S(1)} %get-tuple-element.58.up, bf16[512,1024]{1,0:T(8,128)(2,1)S(1)} %get-tuple-element.57.down), custom_call_target="tpu_custom_call" | custom-call | tf_op jit(solution)/shard_map/sums_kernel/pallas_call | solution.py:241
  56.2 2.3 %fusion.45 = (bf16[512,224]{1,0:T(8,128)(2,1)S(1)}, bf16[512,224]{1,0:T(8,128)(2,1)S(1)}, bf16[512,224]{1,0:T(8,128)(2,1)S(1)}, bf16[512,224]{1,0:T(8,128)(2,1)}) fusion(bf16[512,896]{1,0:T(8,128)(2,1)} %get-tuple-element.33), kind=kLoop, calls=%fused_computation.43 | loop fusion | bytes 1835008 | tf_op jit(solution)/shard_map/slice | solution.py:279
  59.5 4.2 %collective-permute-start.4 = (bf16[512,448]{1,0:T(8,128)(2,1)}, bf16[512,448]{1,0:T(8,128)(2,1)}, u32[]{:S(2)}, u32[]{:S(2)}) collective-permute-start(bf16[512,448]{1,0:T(8,128)(2,1)} %pad_maximum_fusion.5), channel_id=1, source_target_pairs={{0,32},{32,0},{1,33},{33,1},{2,34},{34,2},{3,35},{35,3},{4,36},{36... | collective-permute-start | bytes 1376264 | tf_op jit(solution)/shard_map/ppermute | solution.py:271
  66.8 1.6 slice.97
  70.5 30.8 %reduce-scatter.2.cloned.1.call-done.sums_hbm = bf16[64,3072]{1,0:T(8,128)(2,1)} async-done(((bf16[512,3072]{1,0:T(8,128)(2,1)}), bf16[64,3072]{1,0:T(8,128)(2,1)}) %reduce-scatter.2.cloned.1.call-update) | async-done | bytes 393232 | tf_op jit(solution)/shard_map/reduce_scatter | solution.py:326
  101.3 1.8 shard_kernel.1
  103.2 20.6 %all_gather.7.full = bf16[128,3072]{1,0:T(8,128)(2,1)S(1)} all-gather(bf16[16,3072]{1,0:T(8,128)(2,1)S(1)} %get-tuple-element.42), channel_id=1, replica_groups=mesh['y'=8,'core'=2,'expert'=32] {'y'}, dimensions={0}, use_global_device_ids=true | all-gather | bytes 884736 | tf_op jit(solution)/shard_map/all_gather | solution.py:359
  126.5 10.2 %all-to-all-start.2 = ((bf16[32,1,4,896]{3,2,1,0:T(4,128)(2,1)}), bf16[32,1,4,896]{3,2,1,0:T(4,128)(2,1)S(1)}, u32[]{:S(2)}, u32[]{:S(2)}) async-start(bf16[32,1,4,896]{3,2,1,0:T(4,128)(2,1)} %copy-done.4), calls=%async_computation.3 | async-start | bytes 458752 | tf_op jit(solution)/shard_map/all_to_all | solution.py:267
  136.8 16.4 %all-gather.2.cloned.1.call-done.full_hbm = bf16[768,3072]{1,0:T(8,128)(2,1)} async-done(((bf16[48,3072]{1,0:T(8,128)(2,1)}), bf16[768,3072]{1,0:T(8,128)(2,1)}) %all-gather.2.cloned.1.call-update) | async-done | bytes 4718608 | tf_op jit(solution)/shard_map/all_gather | solution.py:357
  153.2 5.2 %back_kernel.1 = bf16[32,3,4,896]{3,2,1,0:T(4,128)(2,1)} custom-call(bf16[768,3072]{1,0:T(8,128)(2,1)} %all-gather.2.cloned.1.call-done.full_hbm, bf16[224,1024]{1,0:T(8,128)(2,1)} %bitcast.36, bf16[224,1024]{1,0:T(8,128)(2,1)} %bitcast.33, bf16[224,1024]{1,0:T(8,128)(2,1)} %bitcast.30), custom_call_target="tpu_custom_call" | custom-call | tf_op jit(solution)/shard_map/back_kernel/pallas_call | solution.py:241
  158.8 2.2 %collective-permute-start.6 = (bf16[128,3072]{1,0:T(8,128)(2,1)S(1)}, bf16[128,3072]{1,0:T(8,128)(2,1)}, u32[]{:S(2)}, u32[]{:S(2)}) collective-permute-start(bf16[128,3072]{1,0:T(8,128)(2,1)S(1)} %copy-done.1), channel_id=1, source_target_pairs={{0,32},{32,0},{1,33},{33,1},{2,34},{34,2},{3,35},{35,3},{4,36},{36... | collective-permute-start | bytes 2359304 | tf_op jit(solution)/shard_map/ppermute | solution.py:271
  161.0 2.1 %collective-permute-start.5 = (f32[64,896]{1,0:T(8,128)S(1)}, f32[64,896]{1,0:T(8,128)S(1)}, u32[]{:S(2)}, u32[]{:S(2)}) collective-permute-start(f32[64,896]{1,0:T(8,128)S(1)} %mix_last_kernel.1.own_ref), channel_id=1, source_target_pairs={{0,32},{32,0},{1,33},{33,1},{2,34},{34,2},{3,35},{35,3},{4,36},{36... | collective-permute-start | bytes 688136 | tf_op jit(solution)/shard_map/ppermute | solution.py:271
  163.1 10.0 %all-to-all-start.1 = ((bf16[32,3,4,896]{3,2,1,0:T(4,128)(2,1)}), bf16[32,3,4,896]{3,2,1,0:T(4,128)(2,1)S(1)}, u32[]{:S(2)}, u32[]{:S(2)}) async-start(bf16[32,3,4,896]{3,2,1,0:T(4,128)(2,1)} %back_kernel.1), calls=%async_computation.2 | async-start | bytes 1376256 | tf_op jit(solution)/shard_map/all_to_all | solution.py:267
  174.2 1.5 convolution_add_fusion
  181.0 1.5 fusion.24
  182.5 10.3 %all-to-all-done.1.main_ref = bf16[32,3,4,896]{3,2,1,0:T(4,128)(2,1)S(1)} async-done(((bf16[32,3,4,896]{3,2,1,0:T(4,128)(2,1)}), bf16[32,3,4,896]{3,2,1,0:T(4,128)(2,1)S(1)}, u32[]{:S(2)}, u32[]{:S(2)}) %all-to-all-start.1) | async-done | bytes 688160 | tf_op jit(solution)/shard_map/all_to_all | solution.py:267
  (58 shorter events, 20.2 us)
Async XLA Ops:
  7.2 20.9 %copy-start.10 = (bf16[1,224,1024]{2,1,0:T(8,128)(2,1)S(1)}, bf16[1,224,1024]{2,1,0:T(8,128)(2,1)}, u32[]{:S(2)}) copy-start(bf16[1,224,1024]{2,1,0:T(8,128)(2,1)} %param.10) | copy-start | bytes 1376260
  7.2 23.4 %copy-start.9 = (bf16[1,224,1024]{2,1,0:T(8,128)(2,1)S(1)}, bf16[1,224,1024]{2,1,0:T(8,128)(2,1)}, u32[]{:S(2)}) copy-start(bf16[1,224,1024]{2,1,0:T(8,128)(2,1)} %param.11) | copy-start | bytes 1376260
  7.2 25.4 %copy-start.8 = (bf16[1,1024,224]{1,2,0:T(8,128)(2,1)S(1)}, bf16[1,1024,224]{1,2,0:T(8,128)(2,1)}, u32[]{:S(2)}) copy-start(bf16[1,1024,224]{1,2,0:T(8,128)(2,1)} %param.12) | copy-start | bytes 1376260
  8.1 9.7 %collective-permute-start = (bf16[128,224]{1,0:T(8,128)(2,1)S(1)}, bf16[128,224]{1,0:T(8,128)(2,1)S(1)}, u32[]{:S(2)}, u32[]{:S(2)}) collective-permute-start(bf16[128,224]{1,0:T(8,128)(2,1)S(1)} %pad_maximum_fusion.6), channel_id=1, source_target_pairs={{0,32},{32,0},{1,33},{33,1},{2,34},{34,2},{3,35},{35,3},{4,36},{36... | collective-permute-start | bytes 172040 | tf_op jit(solution)/shard_map/ppermute | solution.py:271
  20.4 31.6 %all-to-all-start = ((bf16[32,4,4,896]{3,2,1,0:T(4,128)(2,1)}), bf16[32,4,4,896]{3,2,1,0:T(4,128)(2,1)}, u32[]{:S(2)}, u32[]{:S(2)}) async-start(bf16[32,4,4,896]{3,2,1,0:T(4,128)(2,1)} %send_kernel.1), calls=%async_computation | async-start | bytes 1835008 | tf_op jit(solution)/shard_map/all_to_all | solution.py:267
  28.0 73.3 %reduce-scatter.2.cloned.1.call-start = ((), (), s32[]{:S(2)}) async-start(), calls=%async_computation.4 | async-start | bytes 3538944 | tf_op jit(solution)/shard_map/reduce_scatter | solution.py:326
  28.1 6.9 %collective-permute-start.1 = (bf16[224,1024]{1,0:T(8,128)(2,1)S(1)}, bf16[224,1024]{1,0:T(8,128)(2,1)S(1)}, u32[]{:S(2)}, u32[]{:S(2)}) collective-permute-start(bf16[224,1024]{1,0:T(8,128)(2,1)S(1)} %bitcast.37), channel_id=1, source_target_pairs={{0,32},{32,0},{1,33},{33,1},{2,34},{34,2},{3,35},{35,3},{4,36},{36... | collective-permute-start | bytes 1376264 | tf_op jit(solution)/shard_map/ppermute | solution.py:271
  30.6 4.4 %collective-permute-start.2 = (bf16[224,1024]{1,0:T(8,128)(2,1)S(1)}, bf16[224,1024]{1,0:T(8,128)(2,1)S(1)}, u32[]{:S(2)}, u32[]{:S(2)}) collective-permute-start(bf16[224,1024]{1,0:T(8,128)(2,1)S(1)} %bitcast.34), channel_id=1, source_target_pairs={{0,32},{32,0},{1,33},{33,1},{2,34},{34,2},{3,35},{35,3},{4,36},{36... | collective-permute-start | bytes 1376264 | tf_op jit(solution)/shard_map/ppermute | solution.py:271
  32.6 3.8 %collective-permute-start.3 = (bf16[224,1024]{1,0:T(8,128)(2,1)S(1)}, bf16[224,1024]{1,0:T(8,128)(2,1)S(1)}, u32[]{:S(2)}, u32[]{:S(2)}) collective-permute-start(bf16[224,1024]{1,0:T(8,128)(2,1)S(1)} %bitcast.31), channel_id=1, source_target_pairs={{0,32},{32,0},{1,33},{33,1},{2,34},{34,2},{3,35},{35,3},{4,36},{36... | collective-permute-start | bytes 1376264 | tf_op jit(solution)/shard_map/ppermute | solution.py:271
  56.1 97.1 %all-gather.2.cloned.1.call-start = ((), (), s32[]{:S(2)}) async-start(), calls=%async_computation.5 | async-start | bytes 5013504 | tf_op jit(solution)/shard_map/all_gather | solution.py:357
  56.1 9.4 %copy-start.5 = (s32[64,8]{0,1:T(8,128)S(1)}, s32[64,8]{0,1:T(8,128)}, u32[]{:S(2)}) copy-start(s32[64,8]{0,1:T(8,128)} %param.8) | copy-start | bytes 6148
  56.2 9.4 %copy-start.6 = (f32[64,8]{0,1:T(8,128)S(1)}, f32[64,8]{0,1:T(8,128)}, u32[]{:S(2)}) copy-start(f32[64,8]{0,1:T(8,128)} %param.9) | copy-start | bytes 6148
  59.5 7.3 %collective-permute-start.4 = (bf16[512,448]{1,0:T(8,128)(2,1)}, bf16[512,448]{1,0:T(8,128)(2,1)}, u32[]{:S(2)}, u32[]{:S(2)}) collective-permute-start(bf16[512,448]{1,0:T(8,128)(2,1)} %pad_maximum_fusion.5), channel_id=1, source_target_pairs={{0,32},{32,0},{1,33},{33,1},{2,34},{34,2},{3,35},{35,3},{4,36},{36... | collective-permute-start | bytes 1376264 | tf_op jit(solution)/shard_map/ppermute | solution.py:271
  125.0 0.9 copy-start
  126.5 31.9 %all-to-all-start.2 = ((bf16[32,1,4,896]{3,2,1,0:T(4,128)(2,1)}), bf16[32,1,4,896]{3,2,1,0:T(4,128)(2,1)S(1)}, u32[]{:S(2)}, u32[]{:S(2)}) async-start(bf16[32,1,4,896]{3,2,1,0:T(4,128)(2,1)} %copy-done.4), calls=%async_computation.3 | async-start | bytes 458752 | tf_op jit(solution)/shard_map/all_to_all | solution.py:267
  136.8 21.7 %copy-start.3 = (f32[2,512,1]{2,1,0:T(8,128)S(1)}, f32[2,512,1]{2,1,0:T(8,128)}, u32[]{:S(2)}) copy-start(f32[2,512,1]{2,1,0:T(8,128)} %copy-done.2) | copy-start | bytes 12292
  136.8 22.0 %copy-start.1 = (bf16[128,3072]{1,0:T(8,128)(2,1)S(1)}, bf16[128,3072]{1,0:T(8,128)(2,1)}, u32[]{:S(2)}) copy-start(bf16[128,3072]{1,0:T(8,128)(2,1)} %copy-done) | copy-start | bytes 2359300
  158.4 14.8 %copy-start.12 = (bf16[8,16,448]{2,1,0:T(8,128)(2,1)S(1)}, bf16[8,16,448]{2,1,0:T(8,128)(2,1)}, u32[]{:S(2)}) copy-start(bf16[8,16,448]{2,1,0:T(8,128)(2,1)} %slice.96) | copy-start | bytes 344068
  158.8 15.4 %collective-permute-start.6 = (bf16[128,3072]{1,0:T(8,128)(2,1)S(1)}, bf16[128,3072]{1,0:T(8,128)(2,1)}, u32[]{:S(2)}, u32[]{:S(2)}) collective-permute-start(bf16[128,3072]{1,0:T(8,128)(2,1)S(1)} %copy-done.1), channel_id=1, source_target_pairs={{0,32},{32,0},{1,33},{33,1},{2,34},{34,2},{3,35},{35,3},{4,36},{36... | collective-permute-start | bytes 2359304 | tf_op jit(solution)/shard_map/ppermute | solution.py:271
  161.0 21.5 %collective-permute-start.5 = (f32[64,896]{1,0:T(8,128)S(1)}, f32[64,896]{1,0:T(8,128)S(1)}, u32[]{:S(2)}, u32[]{:S(2)}) collective-permute-start(f32[64,896]{1,0:T(8,128)S(1)} %mix_last_kernel.1.own_ref), channel_id=1, source_target_pairs={{0,32},{32,0},{1,33},{33,1},{2,34},{34,2},{3,35},{35,3},{4,36},{36... | collective-permute-start | bytes 688136 | tf_op jit(solution)/shard_map/ppermute | solution.py:271
  163.1 29.7 %all-to-all-start.1 = ((bf16[32,3,4,896]{3,2,1,0:T(4,128)(2,1)}), bf16[32,3,4,896]{3,2,1,0:T(4,128)(2,1)S(1)}, u32[]{:S(2)}, u32[]{:S(2)}) async-start(bf16[32,3,4,896]{3,2,1,0:T(4,128)(2,1)} %back_kernel.1), calls=%async_computation.2 | async-start | bytes 1376256 | tf_op jit(solution)/shard_map/all_to_all | solution.py:267
  173.2 1.0 copy-start.11
  174.2 4.1 %copy-start.7 = (bf16[768,3072]{1,0:T(8,128)(2,1)S(1)}, bf16[768,3072]{1,0:T(8,128)(2,1)}, u32[]{:S(2)}) copy-start(bf16[768,3072]{1,0:T(8,128)(2,1)} %all-gather.2.cloned.1.call-done.full_hbm) | copy-start | bytes 14155780
  175.7 2.6 %copy-start.13 = (bf16[8,2,48,448]{3,2,1,0:T(8,128)(2,1)S(1)}, bf16[8,2,48,448]{3,2,1,0:T(8,128)(2,1)}, u32[]{:S(2)}) copy-start(bf16[8,2,48,448]{3,2,1,0:T(8,128)(2,1)} %pad_maximum_fusion.3) | copy-start | bytes 2064388
  (2 other events, 1.5 us)
Sparse Core Ops, SparseCore 0:
  56.2 45.0 reduce-scatter.1
  104.0 49.1 all-gather.1

commit v8 on v7

--- a/solution.py
+++ b/solution.py
@@ -200,6 +200,22 @@
     out_ref[:, 0] = rows.reshape(EXPERTS, QUAD, 2 * PAIR).astype(BF)
 
 
+def grads_kernel(*refs):
+    hbm, (gate_ref, up_ref, down_ref), bufs, sems = refs[:6], refs[6:9], refs[9:15], refs[15]
+    full_hbm, full = hbm[0], bufs[0]
+    columns = [pl.ds(i * FFW, FFW) for i in range(3)]
+    pairs = list(zip(hbm[1:], bufs[1:])) + [(full_hbm.at[:, c], full.at[:, c]) for c in columns]
+    loads = copies_of(pairs, sems)
+    start(loads)
+    wait(loads[:5])
+    for i, (out, first) in enumerate(((down_ref, WIDE), (gate_ref, 0), (up_ref, 0))):
+        loads[5 + i].wait()
+        total = 0.0
+        for sums, rows in zip(bufs[:3], bufs[3:]):
+            total = total + t_dot(rows[:, first : first + WIDE], sums[:, columns[i]])
+        out[...] = total.astype(BF)
+
+
 def gated_sum(pick, scaled):
     high = scaled.astype(BF)
     low = (scaled - high.astype(F32)).astype(BF)
@@ -281,15 +297,6 @@
     return own, other
 
 
-def grad_products(rows, full):
-    rows_in, rows_dy = rows[:, :WIDE], rows[:, WIDE:]
-    return (
-        t_dot(rows_in, full[:, FFW : 2 * FFW]),
-        t_dot(rows_in, full[:, 2 * FFW :]),
-        t_dot(rows_dy, full[:, :FFW]),
-    )
-
-
 def body(tokens, expert_ids, gate_weights, w_gate, w_up, w_down, cotangent):
     gate_own, up_own, down_own = w_gate[0], w_up[0], w_down[0].T
     core = lax.axis_index("core")
@@ -361,6 +368,7 @@
         back_last_kernel, shape(EXPERTS, 1, QUAD, 2 * PAIR), full_last, *in_vmem(*stacks)
     )
     back_last = across(send_last, "expert")
+    full_other = swap(after(full_last, send_last))
 
     back = call(
         back_kernel,
@@ -374,7 +382,16 @@
         ]
         + semaphores(3 + 2 * N_Y),
     )
-    back_last = after(back_last, back)
+    grad_inputs = (full, full_last, full_other, after(main, back), own_last, other_last)
+    grads = call(
+        grads_kernel,
+        [shape(WIDE, FFW)] * 3,
+        *in_hbm(*grad_inputs),
+        in_specs=[HBM_SPEC] * 6,
+        scratch_shapes=buffers(*grad_inputs) + semaphores(8),
+    )
+    back = across(back, "expert")
+    back_last = after(back_last, grads[2])
     total_last = call(
         mix_last_kernel,
         shape(tokens.shape[0], 2 * PAIR, dtype=F32),
@@ -385,15 +402,6 @@
         in_specs=[SMEM_SPEC] + [VMEM_SPEC] * 3,
     )
     other_total = swap(total_last)
-    back = across(back, "expert")
-    full_last = after(full_last, total_last)
-    grads_last = [
-        a + b
-        for a, b in zip(
-            grad_products(own_last, full_last), grad_products(other_last, swap(full_last))
-        )
-    ]
-    grads = [(a + b).astype(BF) for a, b in zip(grad_products(main, full), grads_last)]
     back = after(back, other_total, *grads)
     token_grad, mixed = call(
         mix_kernel, [shape(*tokens.shape)] * 2, pick, slot_gate, back, total_last, other_total

time: 202 us -> 197 us (0.975)
  matrix products: 9.19 us -> 0 us
  Pallas kernels: 17.1 us -> 22.8 us
  waiting for transfers between devices: 73.8 us -> 71.7 us
    dot_general x9 -> x0, matrix products: 9.19 us -> none  [t_dot(): lax.dot_general(left, right, (((0,), (0,)), ((), ())), preferred_element_...]
    pallas_call x8 -> x9, Pallas kernels: 17.1 us -> 22.8 us  [call(): pl.pallas_call(kernel, out_shape=out_shape, compiler_params=pltpu.Compile...]
    all_to_all x3, waiting for transfers between devices: 24.2 us -> 18.8 us  [across(): return lax.all_to_all(quads, axis, split_axis=0, concat_axis=0, tiled=True)]
    ppermute x7, waiting for transfers between devices: 2.29 us -> 5.27 us  [swap(): return lax.ppermute(array, 'core', [(0, 1), (1, 0)])]
  transfers between devices with their start and end apart: 12 -> 12, of which waited for: 6 -> 8; matrix products, arithmetic and copies ran while one was open for 10% -> 5% of each run, Pallas kernels for 3% -> 7%
where the time goes in v8:
time: 197 us; the launch traced here: 196 us
  waiting for transfers between devices  71.7 us (36%)
  starting transfers between devices  51.8 us (26%)
  Pallas kernels  22.8 us (12%)
  blocking collectives  20.8 us (11%)
  between operations  14.4 us (7%)
  local copies, waits for them, and re-layouts  8.88 us (5%)
  other arithmetic  5.9 us (3%)
    reduce_scatter x1, waiting for transfers between devices, body(): sums = lax.psum_scatter(parts, 'y', scatter_dimension=0, tiled=True)  30.5 us
    all_to_all x3, starting transfers between devices, across(): return lax.all_to_all(quads, axis, split_axis=0, concat_axis=0, tiled=True)  27 us
    ppermute x7, starting transfers between devices, swap(): return lax.ppermute(array, 'core', [(0, 1), (1, 0)])  24.7 us
    pallas_call x9, Pallas kernels, call(): pl.pallas_call(kernel, out_shape=out_shape, compiler_params=pltpu.Compile...  22.8 us
    all_gather x1, blocking collectives, body(): full_last = lax.all_gather(shard_last, 'y', axis=0, tiled=True)  20.8 us
    all_to_all x3, waiting for transfers between devices, across(): return lax.all_to_all(quads, axis, split_axis=0, concat_axis=0, tiled=True)  18.8 us
    all_gather x1, waiting for transfers between devices, body(): full = lax.all_gather(shard, ('y', 'core'), axis=0, tiled=True)  17.1 us
    ppermute x7, waiting for transfers between devices, swap(): return lax.ppermute(array, 'core', [(0, 1), (1, 0)])  5.27 us
  transfers between devices with their start and end apart: 12, of which 8 were waited for; matrix products, arithmetic and copies ran while one was open for 5% of the time, Pallas kernels for 7%

profile of v8, /device:TPU:1, one launch (start us, length us, event | category | flops | bytes accessed | tf_op | source)
XLA Modules:
  0.0 196.3 jit_solution(11161791997187334640)
XLA Ops:
  8.1 8.8 %collective-permute-start = (bf16[128,224]{1,0:T(8,128)(2,1)S(1)}, bf16[128,224]{1,0:T(8,128)(2,1)S(1)}, u32[]{:S(2)}, u32[]{:S(2)}) collective-permute-start(bf16[128,224]{1,0:T(8,128)(2,1)S(1)} %pad_maximum_fusion.6), channel_id=1, source_target_pairs={{0,32},{32,0},{1,33},{33,1},{2,34},{34,2},{3,35},{35,3},{4,36},{36... | collective-permute-start | bytes 172040 | tf_op jit(solution)/shard_map/ppermute | solution.py:287
  17.8 2.6 %send_kernel.1 = bf16[32,4,4,896]{3,2,1,0:T(4,128)(2,1)} custom-call(s32[1]{0:T(128)} %bitcast.core_ref, bf16[128,224]{1,0:T(8,128)(2,1)S(1)} %collective-permute-done.others_ref, s32[8,64]{1,0:T(8,128)} %bitcast.22, f32[8,64]{1,0:T(8,128)} %bitcast.24, bf16[64,224]{1,0:T(8,128)(2,1)} %tokens_hbm.1, bf16[64,224]{1,0:T(8,128)(2,1)} %cotangent_hbm.1), custom_call_target="tpu_custom_call" | custom-call | tf_op jit(solution)/shard_map/send_kernel/pallas_call | solution.py:257
  20.4 7.6 %all-to-all-start = ((bf16[32,4,4,896]{3,2,1,0:T(4,128)(2,1)}), bf16[32,4,4,896]{3,2,1,0:T(4,128)(2,1)}, u32[]{:S(2)}, u32[]{:S(2)}) async-start(bf16[32,4,4,896]{3,2,1,0:T(4,128)(2,1)} %send_kernel.1), calls=%async_computation | async-start | bytes 1835008 | tf_op jit(solution)/shard_map/all_to_all | solution.py:283
  28.1 2.5 %collective-permute-start.1 = (bf16[224,1024]{1,0:T(8,128)(2,1)S(1)}, bf16[224,1024]{1,0:T(8,128)(2,1)S(1)}, u32[]{:S(2)}, u32[]{:S(2)}) collective-permute-start(bf16[224,1024]{1,0:T(8,128)(2,1)S(1)} %bitcast.37), channel_id=1, source_target_pairs={{0,32},{32,0},{1,33},{33,1},{2,34},{34,2},{3,35},{35,3},{4,36},{36... | collective-permute-start | bytes 1376264 | tf_op jit(solution)/shard_map/ppermute | solution.py:287
  30.6 1.9 collective-permute-start.2
  32.6 2.4 %collective-permute-start.3 = (bf16[224,1024]{1,0:T(8,128)(2,1)S(1)}, bf16[224,1024]{1,0:T(8,128)(2,1)S(1)}, u32[]{:S(2)}, u32[]{:S(2)}) collective-permute-start(bf16[224,1024]{1,0:T(8,128)(2,1)S(1)} %bitcast.31), channel_id=1, source_target_pairs={{0,32},{32,0},{1,33},{33,1},{2,34},{34,2},{3,35},{35,3},{4,36},{36... | collective-permute-start | bytes 1376264 | tf_op jit(solution)/shard_map/ppermute | solution.py:287
  36.4 1.7 pad_maximum_fusion.2
  38.1 13.9 %all-to-all-done.quads = bf16[32,4,4,896]{3,2,1,0:T(4,128)(2,1)} async-done(((bf16[32,4,4,896]{3,2,1,0:T(4,128)(2,1)}), bf16[32,4,4,896]{3,2,1,0:T(4,128)(2,1)}, u32[]{:S(2)}, u32[]{:S(2)}) %all-to-all-start) | async-done | bytes 917536 | tf_op jit(solution)/shard_map/all_to_all | solution.py:283
  52.0 4.1 %sums_kernel.1 = (bf16[512,896]{1,0:T(8,128)(2,1)}, bf16[512,3072]{1,0:T(8,128)(2,1)}) custom-call(bf16[32,4,4,896]{3,2,1,0:T(4,128)(2,1)} %all-to-all-done.quads, bf16[512,1024]{1,0:T(8,128)(2,1)S(1)} %get-tuple-element.67.gate, bf16[512,1024]{1,0:T(8,128)(2,1)S(1)} %get-tuple-element.66.up, bf16[512,1024]{1,0:T(8,128)(2,1)S(1)} %get-tuple-element.65.down), custom_call_target="tpu_custom_call" | custom-call | tf_op jit(solution)/shard_map/sums_kernel/pallas_call | solution.py:257
  56.2 2.3 %fusion = (bf16[512,224]{1,0:T(8,128)(2,1)S(1)}, bf16[512,224]{1,0:T(8,128)(2,1)S(1)}, bf16[512,224]{1,0:T(8,128)(2,1)S(1)}, bf16[512,224]{1,0:T(8,128)(2,1)}) fusion(bf16[512,896]{1,0:T(8,128)(2,1)} %get-tuple-element.37), kind=kLoop, calls=%fused_computation.9 | loop fusion | bytes 1835008 | tf_op jit(solution)/shard_map/slice | solution.py:295
  59.5 4.2 %collective-permute-start.4 = (bf16[512,448]{1,0:T(8,128)(2,1)}, bf16[512,448]{1,0:T(8,128)(2,1)}, u32[]{:S(2)}, u32[]{:S(2)}) collective-permute-start(bf16[512,448]{1,0:T(8,128)(2,1)} %pad_maximum_fusion.5), channel_id=1, source_target_pairs={{0,32},{32,0},{1,33},{33,1},{2,34},{34,2},{3,35},{35,3},{4,36},{36... | collective-permute-start | bytes 1376264 | tf_op jit(solution)/shard_map/ppermute | solution.py:287
  66.8 1.6 slice.37
  70.6 30.5 %reduce-scatter.2.cloned.1.call-done.sums_hbm = bf16[64,3072]{1,0:T(8,128)(2,1)} async-done(((bf16[512,3072]{1,0:T(8,128)(2,1)}), bf16[64,3072]{1,0:T(8,128)(2,1)}) %reduce-scatter.2.cloned.1.call-update) | async-done | bytes 393232 | tf_op jit(solution)/shard_map/reduce_scatter | solution.py:333
  101.1 1.8 shard_kernel.1
  103.0 20.8 %all_gather.7.full.refs_1_ = bf16[128,3072]{1,0:T(8,128)(2,1)S(1)} all-gather(bf16[16,3072]{1,0:T(8,128)(2,1)S(1)} %get-tuple-element.46), channel_id=1, replica_groups=mesh['y'=8,'core'=2,'expert'=32] {'y'}, dimensions={0}, use_global_device_ids=true | all-gather | bytes 884736 | tf_op jit(solution)/shard_map/all_gather | solution.py:366
  126.6 9.7 %all-to-all-start.2 = ((bf16[32,1,4,896]{3,2,1,0:T(4,128)(2,1)}), bf16[32,1,4,896]{3,2,1,0:T(4,128)(2,1)S(1)}, u32[]{:S(2)}, u32[]{:S(2)}) async-start(bf16[32,1,4,896]{3,2,1,0:T(4,128)(2,1)} %copy-done.4), calls=%async_computation.3 | async-start | bytes 458752 | tf_op jit(solution)/shard_map/all_to_all | solution.py:283
  136.3 17.1 %all-gather.2.cloned.1.call-done.full_hbm.refs_0_ = bf16[768,3072]{1,0:T(8,128)(2,1)} async-done(((bf16[48,3072]{1,0:T(8,128)(2,1)}), bf16[768,3072]{1,0:T(8,128)(2,1)}) %all-gather.2.cloned.1.call-update) | async-done | bytes 4718608 | tf_op jit(solution)/shard_map/all_gather | solution.py:364
  153.4 5.2 %back_kernel.1 = bf16[32,3,4,896]{3,2,1,0:T(4,128)(2,1)} custom-call(bf16[768,3072]{1,0:T(8,128)(2,1)} %all-gather.2.cloned.1.call-done.full_hbm.refs_0_, bf16[224,1024]{1,0:T(8,128)(2,1)} %bitcast.36, bf16[224,1024]{1,0:T(8,128)(2,1)} %bitcast.33, bf16[224,1024]{1,0:T(8,128)(2,1)} %bitcast.30), custom_call_target="tpu_custom_call" | custom-call | tf_op jit(solution)/shard_map/back_kernel/pallas_call | solution.py:257
  158.6 9.7 %all-to-all-start.1 = ((bf16[32,3,4,896]{3,2,1,0:T(4,128)(2,1)}), bf16[32,3,4,896]{3,2,1,0:T(4,128)(2,1)S(1)}, u32[]{:S(2)}, u32[]{:S(2)}) async-start(bf16[32,3,4,896]{3,2,1,0:T(4,128)(2,1)} %back_kernel.1), calls=%async_computation.2 | async-start | bytes 1376256 | tf_op jit(solution)/shard_map/all_to_all | solution.py:283
  168.3 2.6 %collective-permute-start.5 = (bf16[128,3072]{1,0:T(8,128)(2,1)S(1)}, bf16[128,3072]{1,0:T(8,128)(2,1)S(1)}, u32[]{:S(2)}, u32[]{:S(2)}) collective-permute-start(bf16[128,3072]{1,0:T(8,128)(2,1)S(1)} %copy-done.1), channel_id=1, source_target_pairs={{0,32},{32,0},{1,33},{33,1},{2,34},{34,2},{3,35},{35,3},{4,36},{36... | collective-permute-start | bytes 2359304 | tf_op jit(solution)/shard_map/ppermute | solution.py:287
  170.9 1.9 collective-permute-done.5.refs_2_
  173.6 5.8 %grads_kernel.1 = (bf16[224,1024]{1,0:T(8,128)(2,1)}, bf16[224,1024]{1,0:T(8,128)(2,1)}, bf16[224,1024]{1,0:T(8,128)(2,1)}) custom-call(bf16[768,3072]{1,0:T(8,128)(2,1)} %all-gather.2.cloned.1.call-done.full_hbm.refs_0_, bf16[128,3072]{1,0:T(8,128)(2,1)} %copy-done, bf16[128,3072]{1,0:T(8,128)(2,1)} %copy-done.10, bf16[768,448]{1,0:T(8,128)(2,1)} %bitcast.26, ...), custom_call_target="tpu_custom_call" | custom-call | tf_op jit(solution)/shard_map/grads_kernel/pallas_call | solution.py:257
  179.8 2.3 %collective-permute-start.6 = (f32[64,896]{1,0:T(8,128)S(1)}, f32[64,896]{1,0:T(8,128)S(1)}, u32[]{:S(2)}, u32[]{:S(2)}) collective-permute-start(f32[64,896]{1,0:T(8,128)S(1)} %mix_last_kernel.1.own_ref), channel_id=1, source_target_pairs={{0,32},{32,0},{1,33},{33,1},{2,34},{34,2},{3,35},{35,3},{4,36},{36... | collective-permute-start | bytes 688136 | tf_op jit(solution)/shard_map/ppermute | solution.py:287
  183.2 4.9 %all-to-all-done.1.main_ref = bf16[32,3,4,896]{3,2,1,0:T(4,128)(2,1)S(1)} async-done(((bf16[32,3,4,896]{3,2,1,0:T(4,128)(2,1)}), bf16[32,3,4,896]{3,2,1,0:T(4,128)(2,1)S(1)}, u32[]{:S(2)}, u32[]{:S(2)}) %all-to-all-start.1) | async-done | bytes 688160 | tf_op jit(solution)/shard_map/all_to_all | solution.py:283
  (45 shorter events, 16.1 us)
Async XLA Ops:
  7.2 25.4 %copy-start.7 = (bf16[1,1024,224]{1,2,0:T(8,128)(2,1)S(1)}, bf16[1,1024,224]{1,2,0:T(8,128)(2,1)}, u32[]{:S(2)}) copy-start(bf16[1,1024,224]{1,2,0:T(8,128)(2,1)} %param.12) | copy-start | bytes 1376260
  7.2 23.4 %copy-start.8 = (bf16[1,224,1024]{2,1,0:T(8,128)(2,1)S(1)}, bf16[1,224,1024]{2,1,0:T(8,128)(2,1)}, u32[]{:S(2)}) copy-start(bf16[1,224,1024]{2,1,0:T(8,128)(2,1)} %param.11) | copy-start | bytes 1376260
  7.2 20.9 %copy-start.9 = (bf16[1,224,1024]{2,1,0:T(8,128)(2,1)S(1)}, bf16[1,224,1024]{2,1,0:T(8,128)(2,1)}, u32[]{:S(2)}) copy-start(bf16[1,224,1024]{2,1,0:T(8,128)(2,1)} %param.10) | copy-start | bytes 1376260
  8.1 9.7 %collective-permute-start = (bf16[128,224]{1,0:T(8,128)(2,1)S(1)}, bf16[128,224]{1,0:T(8,128)(2,1)S(1)}, u32[]{:S(2)}, u32[]{:S(2)}) collective-permute-start(bf16[128,224]{1,0:T(8,128)(2,1)S(1)} %pad_maximum_fusion.6), channel_id=1, source_target_pairs={{0,32},{32,0},{1,33},{33,1},{2,34},{34,2},{3,35},{35,3},{4,36},{36... | collective-permute-start | bytes 172040 | tf_op jit(solution)/shard_map/ppermute | solution.py:287
  20.4 31.6 %all-to-all-start = ((bf16[32,4,4,896]{3,2,1,0:T(4,128)(2,1)}), bf16[32,4,4,896]{3,2,1,0:T(4,128)(2,1)}, u32[]{:S(2)}, u32[]{:S(2)}) async-start(bf16[32,4,4,896]{3,2,1,0:T(4,128)(2,1)} %send_kernel.1), calls=%async_computation | async-start | bytes 1835008 | tf_op jit(solution)/shard_map/all_to_all | solution.py:283
  28.0 73.1 %reduce-scatter.2.cloned.1.call-start = ((), (), s32[]{:S(2)}) async-start(), calls=%async_computation.4 | async-start | bytes 3538944 | tf_op jit(solution)/shard_map/reduce_scatter | solution.py:333
  28.1 6.9 %collective-permute-start.1 = (bf16[224,1024]{1,0:T(8,128)(2,1)S(1)}, bf16[224,1024]{1,0:T(8,128)(2,1)S(1)}, u32[]{:S(2)}, u32[]{:S(2)}) collective-permute-start(bf16[224,1024]{1,0:T(8,128)(2,1)S(1)} %bitcast.37), channel_id=1, source_target_pairs={{0,32},{32,0},{1,33},{33,1},{2,34},{34,2},{3,35},{35,3},{4,36},{36... | collective-permute-start | bytes 1376264 | tf_op jit(solution)/shard_map/ppermute | solution.py:287
  30.6 4.4 %collective-permute-start.2 = (bf16[224,1024]{1,0:T(8,128)(2,1)S(1)}, bf16[224,1024]{1,0:T(8,128)(2,1)S(1)}, u32[]{:S(2)}, u32[]{:S(2)}) collective-permute-start(bf16[224,1024]{1,0:T(8,128)(2,1)S(1)} %bitcast.34), channel_id=1, source_target_pairs={{0,32},{32,0},{1,33},{33,1},{2,34},{34,2},{3,35},{35,3},{4,36},{36... | collective-permute-start | bytes 1376264 | tf_op jit(solution)/shard_map/ppermute | solution.py:287
  32.6 3.8 %collective-permute-start.3 = (bf16[224,1024]{1,0:T(8,128)(2,1)S(1)}, bf16[224,1024]{1,0:T(8,128)(2,1)S(1)}, u32[]{:S(2)}, u32[]{:S(2)}) collective-permute-start(bf16[224,1024]{1,0:T(8,128)(2,1)S(1)} %bitcast.31), channel_id=1, source_target_pairs={{0,32},{32,0},{1,33},{33,1},{2,34},{34,2},{3,35},{35,3},{4,36},{36... | collective-permute-start | bytes 1376264 | tf_op jit(solution)/shard_map/ppermute | solution.py:287
  56.1 97.3 %all-gather.2.cloned.1.call-start = ((), (), s32[]{:S(2)}) async-start(), calls=%async_computation.5 | async-start | bytes 5013504 | tf_op jit(solution)/shard_map/all_gather | solution.py:364
  56.1 9.3 %copy-start.5 = (s32[64,8]{0,1:T(8,128)S(1)}, s32[64,8]{0,1:T(8,128)}, u32[]{:S(2)}) copy-start(s32[64,8]{0,1:T(8,128)} %param.8) | copy-start | bytes 6148
  56.2 9.3 %copy-start.6 = (f32[64,8]{0,1:T(8,128)S(1)}, f32[64,8]{0,1:T(8,128)}, u32[]{:S(2)}) copy-start(f32[64,8]{0,1:T(8,128)} %param.9) | copy-start | bytes 6148
  59.5 7.3 %collective-permute-start.4 = (bf16[512,448]{1,0:T(8,128)(2,1)}, bf16[512,448]{1,0:T(8,128)(2,1)}, u32[]{:S(2)}, u32[]{:S(2)}) collective-permute-start(bf16[512,448]{1,0:T(8,128)(2,1)} %pad_maximum_fusion.5), channel_id=1, source_target_pairs={{0,32},{32,0},{1,33},{33,1},{2,34},{34,2},{3,35},{35,3},{4,36},{36... | collective-permute-start | bytes 1376264 | tf_op jit(solution)/shard_map/ppermute | solution.py:287
  66.0 0.9 copy-start.2
  125.0 0.9 copy-start
  125.9 0.7 copy-start.4
  126.6 32.0 %all-to-all-start.2 = ((bf16[32,1,4,896]{3,2,1,0:T(4,128)(2,1)}), bf16[32,1,4,896]{3,2,1,0:T(4,128)(2,1)S(1)}, u32[]{:S(2)}, u32[]{:S(2)}) async-start(bf16[32,1,4,896]{3,2,1,0:T(4,128)(2,1)} %copy-done.4), calls=%async_computation.3 | async-start | bytes 458752 | tf_op jit(solution)/shard_map/all_to_all | solution.py:283
  136.3 32.0 %copy-start.1 = (bf16[128,3072]{1,0:T(8,128)(2,1)S(1)}, bf16[128,3072]{1,0:T(8,128)(2,1)}, u32[]{:S(2)}) copy-start(bf16[128,3072]{1,0:T(8,128)(2,1)} %copy-done) | copy-start | bytes 2359300
  158.6 29.5 %all-to-all-start.1 = ((bf16[32,3,4,896]{3,2,1,0:T(4,128)(2,1)}), bf16[32,3,4,896]{3,2,1,0:T(4,128)(2,1)S(1)}, u32[]{:S(2)}, u32[]{:S(2)}) async-start(bf16[32,3,4,896]{3,2,1,0:T(4,128)(2,1)} %back_kernel.1), calls=%async_computation.2 | async-start | bytes 1376256 | tf_op jit(solution)/shard_map/all_to_all | solution.py:283
  168.3 11.1 %copy-start.3 = (f32[2,512,1]{2,1,0:T(8,128)S(1)}, f32[2,512,1]{2,1,0:T(8,128)}, u32[]{:S(2)}) copy-start(f32[2,512,1]{2,1,0:T(8,128)} %copy-done.2) | copy-start | bytes 12292
  168.3 4.5 %collective-permute-start.5 = (bf16[128,3072]{1,0:T(8,128)(2,1)S(1)}, bf16[128,3072]{1,0:T(8,128)(2,1)S(1)}, u32[]{:S(2)}, u32[]{:S(2)}) collective-permute-start(bf16[128,3072]{1,0:T(8,128)(2,1)S(1)} %copy-done.1), channel_id=1, source_target_pairs={{0,32},{32,0},{1,33},{33,1},{2,34},{34,2},{3,35},{35,3},{4,36},{36... | collective-permute-start | bytes 2359304 | tf_op jit(solution)/shard_map/ppermute | solution.py:287
  172.8 0.9 copy-start.10
  179.8 3.4 %collective-permute-start.6 = (f32[64,896]{1,0:T(8,128)S(1)}, f32[64,896]{1,0:T(8,128)S(1)}, u32[]{:S(2)}, u32[]{:S(2)}) collective-permute-start(f32[64,896]{1,0:T(8,128)S(1)} %mix_last_kernel.1.own_ref), channel_id=1, source_target_pairs={{0,32},{32,0},{1,33},{33,1},{2,34},{34,2},{3,35},{35,3},{4,36},{36... | collective-permute-start | bytes 688136 | tf_op jit(solution)/shard_map/ppermute | solution.py:287
Sparse Core Ops, SparseCore 0:
  56.2 44.8 reduce-scatter.1
  103.8 49.5 all-gather.1

commit v9 on v8

--- a/solution.py
+++ b/solution.py
@@ -119,27 +119,29 @@
         out_ref[:, q] = rows.astype(BF)
 
 
-def table_kernel(ids_ref, gates_ref, pick_ref, gate_ref):
+def table_kernel(ids_ref, gates_ref, pick_ref, gated_ref):
     firsts = [QUAD * q for q in range(2 * QUADS)]
     for i, (pick, gate) in enumerate(slot_table(ids_ref, gates_ref, firsts)):
         half, q = i // QUADS, i % QUADS
         pick_ref[half, q * QROWS : (q + 1) * QROWS] = pick
-        gate_ref[half, q * QROWS : (q + 1) * QROWS] = gate
+        gated_ref[half, q * QROWS : (q + 1) * QROWS] = (pick.astype(F32) * gate).astype(BF)
 
 
 def sums_kernel(quads, gate, up, down, rows_hbm, out_hbm, rows, out, sems):
-    columns = [pl.ds(i * FFW, FFW) for i in range(3)]
+    wide = FFW // 2
+    columns = [pl.ds(i * wide, wide) for i in range(6)]
     stores = copies_of([(out.at[:, c], out_hbm.at[:, c]) for c in columns], sems)
     for q in range(QUADS):
         block = quads[:, q].astype(F32).reshape(QROWS, 2 * PAIR).astype(BF)
         for y in range(N_Y):
             at = y * SHARD + q * PIECE
             rows[at : at + PIECE] = block[y * PIECE : (y + 1) * PIECE]
-    rows_store = pltpu.make_async_copy(rows, rows_hbm, sems.at[3])
+    rows_store = pltpu.make_async_copy(rows, rows_hbm, sems.at[6])
     rows_store.start()
-    for i, weights in enumerate((gate, up, down)):
-        left = rows[:, :STACK] if i < 2 else rows[:, 2 * PAIR - STACK :]
-        out[:, i * FFW : (i + 1) * FFW] = dot(left, weights[...]).astype(BF)
+    for i, weights in enumerate((gate, gate, up, up, down, down)):
+        left = rows[:, :STACK] if i < 4 else rows[:, 2 * PAIR - STACK :]
+        right = weights[:, i % 2 * wide : (i % 2 + 1) * wide]
+        out[:, i * wide : (i + 1) * wide] = dot(left, right).astype(BF)
         stores[i].start()
     wait(stores + [rows_store])
 
@@ -216,30 +218,26 @@
         out[...] = total.astype(BF)
 
 
-def gated_sum(pick, scaled):
-    high = scaled.astype(BF)
-    low = (scaled - high.astype(F32)).astype(BF)
-    return t_dot(pick, high) + t_dot(pick, low)
-
-
-def mix_last_kernel(core_ref, pick_ref, gate_ref, last_ref, out_ref):
-    back = last_ref[:, 0].astype(F32).reshape(QROWS, 2 * PAIR)
+def mix_last_kernel(core_ref, pick_ref, gated_ref, last_ref, out_ref):
+    back = last_ref[:, 0].astype(F32).reshape(QROWS, 2 * PAIR).astype(BF)
     rows = pl.ds(MAIN * QROWS, QROWS)
-    scale = jnp.where(iota((1, 2 * PAIR), 1) < PAIR, 1.0, gate_ref[core_ref[0], rows])
-    out_ref[...] = gated_sum(pick_ref[core_ref[0], rows], back * scale)
-
-
-def mix_kernel(pick_ref, gate_ref, main_ref, own_ref, other_ref, grad_ref, mixed_ref):
+    plain = t_dot(pick_ref[core_ref[0], rows], back)
+    gated = t_dot(gated_ref[core_ref[0], rows], back)
+    out_ref[...] = jnp.where(iota((1, 2 * PAIR), 1) < PAIR, plain, gated)
+
+
+def mix_kernel(pick_ref, gated_ref, main_ref, own_ref, other_ref, grad_ref, mixed_ref):
     quads = [main_ref[:, q] for q in range(MAIN)]
-    back = jnp.concatenate([q.astype(F32).reshape(QROWS, 2 * PAIR) for q in quads], axis=0)
+    quads = [q.astype(F32).reshape(QROWS, 2 * PAIR).astype(BF) for q in quads]
+    back = jnp.concatenate(quads, axis=0)
     rows = slice(0, MAIN * QROWS)
     totals = []
     for half in range(2):
+        columns = back[:, half * JOIN : half * JOIN + STACK]
+        plain = t_dot(pick_ref[half, rows], columns)
+        gated = t_dot(gated_ref[half, rows], columns)
         skip = half * (PAIR - JOIN)
-        lane = iota((1, STACK), 1)
-        scale = jnp.where(lane < skip + WIDE, 1.0, gate_ref[half, rows])
-        scaled = back[:, half * JOIN : half * JOIN + STACK] * scale
-        totals.append(gated_sum(pick_ref[half, rows], scaled))
+        totals.append(jnp.where(iota((1, STACK), 1) < skip + WIDE, plain, gated))
     total = totals[0][:, :PAIR] + totals[1][:, STACK - PAIR :]
     own, other = own_ref[...], other_ref[...]
     grad = total[:, :WIDE] + own[:, :WIDE] + other[:, WIDE:PAIR]
@@ -328,14 +326,14 @@
         in_specs=[VMEM_SPEC] * 4,
         out_specs=[HBM_SPEC] * 2,
         scratch_shapes=[pltpu.VMEM((ROWS, 2 * PAIR), BF), pltpu.VMEM((ROWS, 3 * FFW), BF)]
-        + semaphores(4),
+        + semaphores(7),
     )
     sums = lax.psum_scatter(parts, "y", scatter_dimension=0, tiled=True)
 
     rows, ids, gates, _ = lax.optimization_barrier((rows, ids, gates, parts))
-    pick, slot_gate = call(
+    pick, gated = call(
         table_kernel,
-        [shape(2, ROWS, tokens.shape[0]), shape(2, ROWS, 1, dtype=F32)],
+        [shape(2, ROWS, tokens.shape[0])] * 2,
         ids,
         gates,
     )
@@ -348,8 +346,8 @@
     first = jnp.where(core == 0, own, other)[:, None, :cut]
     second = jnp.where(core == 0, other, own)[:, None, :cut]
     main = jnp.concatenate([first, second], axis=1).reshape(2 * MAIN * QROWS, PAIR)
-    sums, main, own_last, other_last, pick, slot_gate = lax.optimization_barrier(
-        (sums, main, own_last, other_last, pick, slot_gate)
+    sums, main, own_last, other_last, pick, gated = lax.optimization_barrier(
+        (sums, main, own_last, other_last, pick, gated)
     )
 
     shard_shape = shape(cut, 3 * FFW)
@@ -397,14 +395,14 @@
         shape(tokens.shape[0], 2 * PAIR, dtype=F32),
         core.reshape(1),
         pick,
-        slot_gate,
+        gated,
         back_last,
         in_specs=[SMEM_SPEC] + [VMEM_SPEC] * 3,
     )
     other_total = swap(total_last)
     back = after(back, other_total, *grads)
     token_grad, mixed = call(
-        mix_kernel, [shape(*tokens.shape)] * 2, pick, slot_gate, back, total_last, other_total
+        mix_kernel, [shape(*tokens.shape)] * 2, pick, gated, back, total_last, other_total
     )
     return mixed, token_grad, grads[0][None], grads[1][None], grads[2].T[None]
 

time: 197 us -> 197 us (level)
  no operation moved by 1% of the time
where the time goes in v9:
time: 197 us; the launch traced here: 196 us
  waiting for transfers between devices  71.7 us (36%)
  starting transfers between devices  52.2 us (26%)
  Pallas kernels  22.4 us (11%)
  blocking collectives  20.6 us (10%)
  between operations  14.4 us (7%)
  local copies, waits for them, and re-layouts  8.74 us (4%)
  other arithmetic  5.88 us (3%)
    reduce_scatter x1, waiting for transfers between devices, body(): sums = lax.psum_scatter(parts, 'y', scatter_dimension=0, tiled=True)  30.6 us
    all_to_all x3, starting transfers between devices, across(): return lax.all_to_all(quads, axis, split_axis=0, concat_axis=0, tiled=True)  27.5 us
    ppermute x7, starting transfers between devices, swap(): return lax.ppermute(array, 'core', [(0, 1), (1, 0)])  24.7 us
    pallas_call x9, Pallas kernels, call(): pl.pallas_call(kernel, out_shape=out_shape, compiler_params=pltpu.Compile...  22.4 us
    all_gather x1, blocking collectives, body(): full_last = lax.all_gather(shard_last, 'y', axis=0, tiled=True)  20.6 us
    all_to_all x3, waiting for transfers between devices, across(): return lax.all_to_all(quads, axis, split_axis=0, concat_axis=0, tiled=True)  18.9 us
    all_gather x1, waiting for transfers between devices, body(): full = lax.all_gather(shard, ('y', 'core'), axis=0, tiled=True)  16.9 us
    ppermute x7, waiting for transfers between devices, swap(): return lax.ppermute(array, 'core', [(0, 1), (1, 0)])  5.27 us
  transfers between devices with their start and end apart: 12, of which 8 were waited for; matrix products, arithmetic and copies ran while one was open for 5% of the time, Pallas kernels for 7%

profile of v9, /device:TPU:1, one launch (start us, length us, event | category | flops | bytes accessed | tf_op | source)
XLA Modules:
  0.0 195.9 jit_solution(14889298113769285525)
XLA Ops:
  8.1 8.8 %collective-permute-start = (bf16[128,224]{1,0:T(8,128)(2,1)S(1)}, bf16[128,224]{1,0:T(8,128)(2,1)S(1)}, u32[]{:S(2)}, u32[]{:S(2)}) collective-permute-start(bf16[128,224]{1,0:T(8,128)(2,1)S(1)} %pad_maximum_fusion.6), channel_id=1, source_target_pairs={{0,32},{32,0},{1,33},{33,1},{2,34},{34,2},{3,35},{35,3},{4,36},{36... | collective-permute-start | bytes 172040 | tf_op jit(solution)/shard_map/ppermute | solution.py:285
  17.8 2.6 %send_kernel.1 = bf16[32,4,4,896]{3,2,1,0:T(4,128)(2,1)} custom-call(s32[1]{0:T(128)} %bitcast.core_ref, bf16[128,224]{1,0:T(8,128)(2,1)S(1)} %collective-permute-done.others_ref, s32[8,64]{1,0:T(8,128)} %bitcast.22, f32[8,64]{1,0:T(8,128)} %bitcast.24, bf16[64,224]{1,0:T(8,128)(2,1)} %tokens_hbm.1, bf16[64,224]{1,0:T(8,128)(2,1)} %cotangent_hbm.1), custom_call_target="tpu_custom_call" | custom-call | tf_op jit(solution)/shard_map/send_kernel/pallas_call | solution.py:255
  20.4 7.6 %all-to-all-start = ((bf16[32,4,4,896]{3,2,1,0:T(4,128)(2,1)}), bf16[32,4,4,896]{3,2,1,0:T(4,128)(2,1)}, u32[]{:S(2)}, u32[]{:S(2)}) async-start(bf16[32,4,4,896]{3,2,1,0:T(4,128)(2,1)} %send_kernel.1), calls=%async_computation | async-start | bytes 1835008 | tf_op jit(solution)/shard_map/all_to_all | solution.py:281
  28.1 2.5 %collective-permute-start.1 = (bf16[224,1024]{1,0:T(8,128)(2,1)S(1)}, bf16[224,1024]{1,0:T(8,128)(2,1)S(1)}, u32[]{:S(2)}, u32[]{:S(2)}) collective-permute-start(bf16[224,1024]{1,0:T(8,128)(2,1)S(1)} %bitcast.37), channel_id=1, source_target_pairs={{0,32},{32,0},{1,33},{33,1},{2,34},{34,2},{3,35},{35,3},{4,36},{36... | collective-permute-start | bytes 1376264 | tf_op jit(solution)/shard_map/ppermute | solution.py:285
  30.6 1.9 collective-permute-start.2
  32.6 2.4 %collective-permute-start.3 = (bf16[224,1024]{1,0:T(8,128)(2,1)S(1)}, bf16[224,1024]{1,0:T(8,128)(2,1)S(1)}, u32[]{:S(2)}, u32[]{:S(2)}) collective-permute-start(bf16[224,1024]{1,0:T(8,128)(2,1)S(1)} %bitcast.31), channel_id=1, source_target_pairs={{0,32},{32,0},{1,33},{33,1},{2,34},{34,2},{3,35},{35,3},{4,36},{36... | collective-permute-start | bytes 1376264 | tf_op jit(solution)/shard_map/ppermute | solution.py:285
  36.4 1.7 pad_maximum_fusion.2
  38.1 13.9 %all-to-all-done.quads = bf16[32,4,4,896]{3,2,1,0:T(4,128)(2,1)} async-done(((bf16[32,4,4,896]{3,2,1,0:T(4,128)(2,1)}), bf16[32,4,4,896]{3,2,1,0:T(4,128)(2,1)}, u32[]{:S(2)}, u32[]{:S(2)}) %all-to-all-start) | async-done | bytes 917536 | tf_op jit(solution)/shard_map/all_to_all | solution.py:281
  52.0 3.9 %sums_kernel.1 = (bf16[512,896]{1,0:T(8,128)(2,1)}, bf16[512,3072]{1,0:T(8,128)(2,1)}) custom-call(bf16[32,4,4,896]{3,2,1,0:T(4,128)(2,1)} %all-to-all-done.quads, bf16[512,1024]{1,0:T(8,128)(2,1)S(1)} %get-tuple-element.67.gate, bf16[512,1024]{1,0:T(8,128)(2,1)S(1)} %get-tuple-element.66.up, bf16[512,1024]{1,0:T(8,128)(2,1)S(1)} %get-tuple-element.65.down), custom_call_target="tpu_custom_call" | custom-call | tf_op jit(solution)/shard_map/sums_kernel/pallas_call | solution.py:255
  56.0 2.3 %fusion = (bf16[512,224]{1,0:T(8,128)(2,1)S(1)}, bf16[512,224]{1,0:T(8,128)(2,1)S(1)}, bf16[512,224]{1,0:T(8,128)(2,1)S(1)}, bf16[512,224]{1,0:T(8,128)(2,1)}) fusion(bf16[512,896]{1,0:T(8,128)(2,1)} %get-tuple-element.37), kind=kLoop, calls=%fused_computation.9 | loop fusion | bytes 1835008 | tf_op jit(solution)/shard_map/slice | solution.py:293
  59.3 4.2 %collective-permute-start.4 = (bf16[512,448]{1,0:T(8,128)(2,1)}, bf16[512,448]{1,0:T(8,128)(2,1)}, u32[]{:S(2)}, u32[]{:S(2)}) collective-permute-start(bf16[512,448]{1,0:T(8,128)(2,1)} %pad_maximum_fusion.5), channel_id=1, source_target_pairs={{0,32},{32,0},{1,33},{33,1},{2,34},{34,2},{3,35},{35,3},{4,36},{36... | collective-permute-start | bytes 1376264 | tf_op jit(solution)/shard_map/ppermute | solution.py:285
  66.6 1.6 slice.37
  70.3 30.6 %reduce-scatter.2.cloned.1.call-done.sums_hbm = bf16[64,3072]{1,0:T(8,128)(2,1)} async-done(((bf16[512,3072]{1,0:T(8,128)(2,1)}), bf16[64,3072]{1,0:T(8,128)(2,1)}) %reduce-scatter.2.cloned.1.call-update) | async-done | bytes 393232 | tf_op jit(solution)/shard_map/reduce_scatter | solution.py:331
  101.0 1.8 shard_kernel.1
  102.8 20.6 %all_gather.7.full.refs_1_ = bf16[128,3072]{1,0:T(8,128)(2,1)S(1)} all-gather(bf16[16,3072]{1,0:T(8,128)(2,1)S(1)} %get-tuple-element.46), channel_id=1, replica_groups=mesh['y'=8,'core'=2,'expert'=32] {'y'}, dimensions={0}, use_global_device_ids=true | all-gather | bytes 884736 | tf_op jit(solution)/shard_map/all_gather | solution.py:364
  126.2 10.2 %all-to-all-start.2 = ((bf16[32,1,4,896]{3,2,1,0:T(4,128)(2,1)}), bf16[32,1,4,896]{3,2,1,0:T(4,128)(2,1)S(1)}, u32[]{:S(2)}, u32[]{:S(2)}) async-start(bf16[32,1,4,896]{3,2,1,0:T(4,128)(2,1)} %copy-done.4), calls=%async_computation.3 | async-start | bytes 458752 | tf_op jit(solution)/shard_map/all_to_all | solution.py:281
  136.4 16.9 %all-gather.2.cloned.1.call-done.full_hbm.refs_0_ = bf16[768,3072]{1,0:T(8,128)(2,1)} async-done(((bf16[48,3072]{1,0:T(8,128)(2,1)}), bf16[768,3072]{1,0:T(8,128)(2,1)}) %all-gather.2.cloned.1.call-update) | async-done | bytes 4718608 | tf_op jit(solution)/shard_map/all_gather | solution.py:362
  153.2 5.2 %back_kernel.1 = bf16[32,3,4,896]{3,2,1,0:T(4,128)(2,1)} custom-call(bf16[768,3072]{1,0:T(8,128)(2,1)} %all-gather.2.cloned.1.call-done.full_hbm.refs_0_, bf16[224,1024]{1,0:T(8,128)(2,1)} %bitcast.36, bf16[224,1024]{1,0:T(8,128)(2,1)} %bitcast.33, bf16[224,1024]{1,0:T(8,128)(2,1)} %bitcast.30), custom_call_target="tpu_custom_call" | custom-call | tf_op jit(solution)/shard_map/back_kernel/pallas_call | solution.py:255
  158.4 9.7 %all-to-all-start.1 = ((bf16[32,3,4,896]{3,2,1,0:T(4,128)(2,1)}), bf16[32,3,4,896]{3,2,1,0:T(4,128)(2,1)S(1)}, u32[]{:S(2)}, u32[]{:S(2)}) async-start(bf16[32,3,4,896]{3,2,1,0:T(4,128)(2,1)} %back_kernel.1), calls=%async_computation.2 | async-start | bytes 1376256 | tf_op jit(solution)/shard_map/all_to_all | solution.py:281
  168.1 2.6 %collective-permute-start.5 = (bf16[128,3072]{1,0:T(8,128)(2,1)S(1)}, bf16[128,3072]{1,0:T(8,128)(2,1)S(1)}, u32[]{:S(2)}, u32[]{:S(2)}) collective-permute-start(bf16[128,3072]{1,0:T(8,128)(2,1)S(1)} %copy-done.1), channel_id=1, source_target_pairs={{0,32},{32,0},{1,33},{33,1},{2,34},{34,2},{3,35},{35,3},{4,36},{36... | collective-permute-start | bytes 2359304 | tf_op jit(solution)/shard_map/ppermute | solution.py:285
  170.7 1.9 collective-permute-done.5.refs_2_
  173.5 5.8 %grads_kernel.1 = (bf16[224,1024]{1,0:T(8,128)(2,1)}, bf16[224,1024]{1,0:T(8,128)(2,1)}, bf16[224,1024]{1,0:T(8,128)(2,1)}) custom-call(bf16[768,3072]{1,0:T(8,128)(2,1)} %all-gather.2.cloned.1.call-done.full_hbm.refs_0_, bf16[128,3072]{1,0:T(8,128)(2,1)} %copy-done, bf16[128,3072]{1,0:T(8,128)(2,1)} %copy-done.10, bf16[768,448]{1,0:T(8,128)(2,1)} %bitcast.26, ...), custom_call_target="tpu_custom_call" | custom-call | tf_op jit(solution)/shard_map/grads_kernel/pallas_call | solution.py:255
  179.5 2.3 %collective-permute-start.6 = (f32[64,896]{1,0:T(8,128)S(1)}, f32[64,896]{1,0:T(8,128)S(1)}, u32[]{:S(2)}, u32[]{:S(2)}) collective-permute-start(f32[64,896]{1,0:T(8,128)S(1)} %mix_last_kernel.1.own_ref), channel_id=1, source_target_pairs={{0,32},{32,0},{1,33},{33,1},{2,34},{34,2},{3,35},{35,3},{4,36},{36... | collective-permute-start | bytes 688136 | tf_op jit(solution)/shard_map/ppermute | solution.py:285
  182.9 5.0 %all-to-all-done.1.main_ref = bf16[32,3,4,896]{3,2,1,0:T(4,128)(2,1)S(1)} async-done(((bf16[32,3,4,896]{3,2,1,0:T(4,128)(2,1)}), bf16[32,3,4,896]{3,2,1,0:T(4,128)(2,1)S(1)}, u32[]{:S(2)}, u32[]{:S(2)}) %all-to-all-start.1) | async-done | bytes 688160 | tf_op jit(solution)/shard_map/all_to_all | solution.py:281
  (45 shorter events, 15.7 us)
Async XLA Ops:
  7.2 25.4 %copy-start.7 = (bf16[1,1024,224]{1,2,0:T(8,128)(2,1)S(1)}, bf16[1,1024,224]{1,2,0:T(8,128)(2,1)}, u32[]{:S(2)}) copy-start(bf16[1,1024,224]{1,2,0:T(8,128)(2,1)} %param.12) | copy-start | bytes 1376260
  7.2 23.4 %copy-start.8 = (bf16[1,224,1024]{2,1,0:T(8,128)(2,1)S(1)}, bf16[1,224,1024]{2,1,0:T(8,128)(2,1)}, u32[]{:S(2)}) copy-start(bf16[1,224,1024]{2,1,0:T(8,128)(2,1)} %param.11) | copy-start | bytes 1376260
  7.2 20.9 %copy-start.9 = (bf16[1,224,1024]{2,1,0:T(8,128)(2,1)S(1)}, bf16[1,224,1024]{2,1,0:T(8,128)(2,1)}, u32[]{:S(2)}) copy-start(bf16[1,224,1024]{2,1,0:T(8,128)(2,1)} %param.10) | copy-start | bytes 1376260
  8.1 9.7 %collective-permute-start = (bf16[128,224]{1,0:T(8,128)(2,1)S(1)}, bf16[128,224]{1,0:T(8,128)(2,1)S(1)}, u32[]{:S(2)}, u32[]{:S(2)}) collective-permute-start(bf16[128,224]{1,0:T(8,128)(2,1)S(1)} %pad_maximum_fusion.6), channel_id=1, source_target_pairs={{0,32},{32,0},{1,33},{33,1},{2,34},{34,2},{3,35},{35,3},{4,36},{36... | collective-permute-start | bytes 172040 | tf_op jit(solution)/shard_map/ppermute | solution.py:285
  20.4 31.6 %all-to-all-start = ((bf16[32,4,4,896]{3,2,1,0:T(4,128)(2,1)}), bf16[32,4,4,896]{3,2,1,0:T(4,128)(2,1)}, u32[]{:S(2)}, u32[]{:S(2)}) async-start(bf16[32,4,4,896]{3,2,1,0:T(4,128)(2,1)} %send_kernel.1), calls=%async_computation | async-start | bytes 1835008 | tf_op jit(solution)/shard_map/all_to_all | solution.py:281
  28.0 72.9 %reduce-scatter.2.cloned.1.call-start = ((), (), s32[]{:S(2)}) async-start(), calls=%async_computation.4 | async-start | bytes 3538944 | tf_op jit(solution)/shard_map/reduce_scatter | solution.py:331
  28.1 6.9 %collective-permute-start.1 = (bf16[224,1024]{1,0:T(8,128)(2,1)S(1)}, bf16[224,1024]{1,0:T(8,128)(2,1)S(1)}, u32[]{:S(2)}, u32[]{:S(2)}) collective-permute-start(bf16[224,1024]{1,0:T(8,128)(2,1)S(1)} %bitcast.37), channel_id=1, source_target_pairs={{0,32},{32,0},{1,33},{33,1},{2,34},{34,2},{3,35},{35,3},{4,36},{36... | collective-permute-start | bytes 1376264 | tf_op jit(solution)/shard_map/ppermute | solution.py:285
  30.6 4.4 %collective-permute-start.2 = (bf16[224,1024]{1,0:T(8,128)(2,1)S(1)}, bf16[224,1024]{1,0:T(8,128)(2,1)S(1)}, u32[]{:S(2)}, u32[]{:S(2)}) collective-permute-start(bf16[224,1024]{1,0:T(8,128)(2,1)S(1)} %bitcast.34), channel_id=1, source_target_pairs={{0,32},{32,0},{1,33},{33,1},{2,34},{34,2},{3,35},{35,3},{4,36},{36... | collective-permute-start | bytes 1376264 | tf_op jit(solution)/shard_map/ppermute | solution.py:285
  32.6 3.8 %collective-permute-start.3 = (bf16[224,1024]{1,0:T(8,128)(2,1)S(1)}, bf16[224,1024]{1,0:T(8,128)(2,1)S(1)}, u32[]{:S(2)}, u32[]{:S(2)}) collective-permute-start(bf16[224,1024]{1,0:T(8,128)(2,1)S(1)} %bitcast.31), channel_id=1, source_target_pairs={{0,32},{32,0},{1,33},{33,1},{2,34},{34,2},{3,35},{35,3},{4,36},{36... | collective-permute-start | bytes 1376264 | tf_op jit(solution)/shard_map/ppermute | solution.py:285
  55.9 97.3 %all-gather.2.cloned.1.call-start = ((), (), s32[]{:S(2)}) async-start(), calls=%async_computation.5 | async-start | bytes 5013504 | tf_op jit(solution)/shard_map/all_gather | solution.py:362
  56.0 9.3 %copy-start.5 = (s32[64,8]{0,1:T(8,128)S(1)}, s32[64,8]{0,1:T(8,128)}, u32[]{:S(2)}) copy-start(s32[64,8]{0,1:T(8,128)} %param.8) | copy-start | bytes 6148
  56.0 9.3 %copy-start.6 = (f32[64,8]{0,1:T(8,128)S(1)}, f32[64,8]{0,1:T(8,128)}, u32[]{:S(2)}) copy-start(f32[64,8]{0,1:T(8,128)} %param.9) | copy-start | bytes 6148
  59.3 7.2 %collective-permute-start.4 = (bf16[512,448]{1,0:T(8,128)(2,1)}, bf16[512,448]{1,0:T(8,128)(2,1)}, u32[]{:S(2)}, u32[]{:S(2)}) collective-permute-start(bf16[512,448]{1,0:T(8,128)(2,1)} %pad_maximum_fusion.5), channel_id=1, source_target_pairs={{0,32},{32,0},{1,33},{33,1},{2,34},{34,2},{3,35},{35,3},{4,36},{36... | collective-permute-start | bytes 1376264 | tf_op jit(solution)/shard_map/ppermute | solution.py:285
  65.8 0.7 copy-start.2
  124.6 0.9 copy-start
  125.5 0.7 copy-start.4
  126.2 32.2 %all-to-all-start.2 = ((bf16[32,1,4,896]{3,2,1,0:T(4,128)(2,1)}), bf16[32,1,4,896]{3,2,1,0:T(4,128)(2,1)S(1)}, u32[]{:S(2)}, u32[]{:S(2)}) async-start(bf16[32,1,4,896]{3,2,1,0:T(4,128)(2,1)} %copy-done.4), calls=%async_computation.3 | async-start | bytes 458752 | tf_op jit(solution)/shard_map/all_to_all | solution.py:281
  136.3 31.7 %copy-start.1 = (bf16[128,3072]{1,0:T(8,128)(2,1)S(1)}, bf16[128,3072]{1,0:T(8,128)(2,1)}, u32[]{:S(2)}) copy-start(bf16[128,3072]{1,0:T(8,128)(2,1)} %copy-done) | copy-start | bytes 2359300
  158.4 29.5 %all-to-all-start.1 = ((bf16[32,3,4,896]{3,2,1,0:T(4,128)(2,1)}), bf16[32,3,4,896]{3,2,1,0:T(4,128)(2,1)S(1)}, u32[]{:S(2)}, u32[]{:S(2)}) async-start(bf16[32,3,4,896]{3,2,1,0:T(4,128)(2,1)} %back_kernel.1), calls=%async_computation.2 | async-start | bytes 1376256 | tf_op jit(solution)/shard_map/all_to_all | solution.py:281
  168.1 11.1 %copy-start.3 = (bf16[2,512,64]{2,1,0:T(8,128)(2,1)S(1)}, bf16[2,512,64]{2,1,0:T(8,128)(2,1)}, u32[]{:S(2)}) copy-start(bf16[2,512,64]{2,1,0:T(8,128)(2,1)} %copy-done.2) | copy-start | bytes 393220
  168.1 4.5 %collective-permute-start.5 = (bf16[128,3072]{1,0:T(8,128)(2,1)S(1)}, bf16[128,3072]{1,0:T(8,128)(2,1)S(1)}, u32[]{:S(2)}, u32[]{:S(2)}) collective-permute-start(bf16[128,3072]{1,0:T(8,128)(2,1)S(1)} %copy-done.1), channel_id=1, source_target_pairs={{0,32},{32,0},{1,33},{33,1},{2,34},{34,2},{3,35},{35,3},{4,36},{36... | collective-permute-start | bytes 2359304 | tf_op jit(solution)/shard_map/ppermute | solution.py:285
  172.6 0.9 copy-start.10
  179.5 3.4 %collective-permute-start.6 = (f32[64,896]{1,0:T(8,128)S(1)}, f32[64,896]{1,0:T(8,128)S(1)}, u32[]{:S(2)}, u32[]{:S(2)}) collective-permute-start(f32[64,896]{1,0:T(8,128)S(1)} %mix_last_kernel.1.own_ref), channel_id=1, source_target_pairs={{0,32},{32,0},{1,33},{33,1},{2,34},{34,2},{3,35},{35,3},{4,36},{36... | collective-permute-start | bytes 688136 | tf_op jit(solution)/shard_map/ppermute | solution.py:285
Sparse Core Ops, SparseCore 0:
  56.0 44.8 reduce-scatter.1
  103.6 49.5 all-gather.1

commit v10 on v9

--- a/solution.py
+++ b/solution.py
@@ -82,8 +82,6 @@
 
 
 def send_kernel(
-    core_ref,
-    others_ref,
     ids_hbm,
     gates_hbm,
     tokens_hbm,
@@ -106,17 +104,17 @@
     )
     start(loads)
     wait(loads[:2])
-    firsts = [core_ref[0] * HALF + QUAD * q for q in range(QUADS)]
-    tables = slot_table(ids_ref, gates_ref, firsts)
+    tables = slot_table(ids_ref, gates_ref, [QUAD * q for q in range(2 * QUADS)])
     wait(loads[2:])
-    count = tokens_ref.shape[0]
-    features = jnp.concatenate(
-        [tokens_ref[...], others_ref[:count], cotangent_ref[...], others_ref[count:]], axis=1
-    )
-    for q, (pick, gate) in enumerate(tables):
-        scale = jnp.where(iota((1, 2 * PAIR), 1) < PAIR, 1.0, gate)
-        rows = (dot(pick, features) * scale).reshape(EXPERTS, QUAD, 2 * PAIR)
-        out_ref[:, q] = rows.astype(BF)
+    features = jnp.concatenate([tokens_ref[...], cotangent_ref[...]], axis=1)
+    for pair in range(QUADS):
+        rows = []
+        for pick, gate in tables[2 * pair : 2 * pair + 2]:
+            scale = jnp.where(iota((1, PAIR), 1) < WIDE, 1.0, gate)
+            rows.append(dot(pick, features) * scale)
+        rows = jnp.concatenate(rows, axis=1).reshape(EXPERTS, QUAD, 2 * PAIR)
+        half, place = pair // (QUADS // 2), pair % (QUADS // 2)
+        out_ref[half * EXPERTS : (half + 1) * EXPERTS, place] = rows.astype(BF)
 
 
 def table_kernel(ids_ref, gates_ref, pick_ref, gated_ref):
@@ -132,7 +130,13 @@
     columns = [pl.ds(i * wide, wide) for i in range(6)]
     stores = copies_of([(out.at[:, c], out_hbm.at[:, c]) for c in columns], sems)
     for q in range(QUADS):
-        block = quads[:, q].astype(F32).reshape(QROWS, 2 * PAIR).astype(BF)
+        pieces = []
+        for core in range(2):
+            block = quads[core * EXPERTS : (core + 1) * EXPERTS, q // 2].astype(F32)
+            block = block.reshape(QROWS, 2 * PAIR)[:, q % 2 * PAIR : (q % 2 + 1) * PAIR]
+            pieces.append((block[:, :WIDE], block[:, WIDE:]))
+        (in_0, dy_0), (in_1, dy_1) = pieces
+        block = jnp.concatenate([in_0, in_1, dy_0, dy_1], axis=1).astype(BF)
         for y in range(N_Y):
             at = y * SHARD + q * PIECE
             rows[at : at + PIECE] = block[y * PIECE : (y + 1) * PIECE]
@@ -226,7 +230,7 @@
     out_ref[...] = jnp.where(iota((1, 2 * PAIR), 1) < PAIR, plain, gated)
 
 
-def mix_kernel(pick_ref, gated_ref, main_ref, own_ref, other_ref, grad_ref, mixed_ref):
+def mix_kernel(core_ref, pick_ref, gated_ref, main_ref, own_ref, other_ref, grad_ref, mixed_ref):
     quads = [main_ref[:, q] for q in range(MAIN)]
     quads = [q.astype(F32).reshape(QROWS, 2 * PAIR).astype(BF) for q in quads]
     back = jnp.concatenate(quads, axis=0)
@@ -239,11 +243,12 @@
         skip = half * (PAIR - JOIN)
         totals.append(jnp.where(iota((1, STACK), 1) < skip + WIDE, plain, gated))
     total = totals[0][:, :PAIR] + totals[1][:, STACK - PAIR :]
-    own, other = own_ref[...], other_ref[...]
-    grad = total[:, :WIDE] + own[:, :WIDE] + other[:, WIDE:PAIR]
-    mixed = total[:, WIDE:] + own[:, PAIR : PAIR + WIDE] + other[:, PAIR + WIDE :]
+    last = own_ref[...] + other_ref[...]
+    is_first = core_ref[0] == 0
+    grad = total[:, :WIDE] + jnp.where(is_first, last[:, :WIDE], last[:, WIDE:PAIR])
+    last = jnp.where(is_first, last[:, PAIR : PAIR + WIDE], last[:, PAIR + WIDE :])
     grad_ref[...] = grad.astype(BF)
-    mixed_ref[...] = mixed.astype(BF)
+    mixed_ref[...] = (total[:, WIDE:] + last).astype(BF)
 
 
 HBM_SPEC = pl.BlockSpec(memory_space=pltpu.HBM)
@@ -289,34 +294,35 @@
     return lax.optimization_barrier((array,) + others)[0]
 
 
-def split_features(rows):
-    own = jnp.concatenate([rows[:, :WIDE], rows[:, PAIR : PAIR + WIDE]], axis=1)
-    other = jnp.concatenate([rows[:, WIDE:PAIR], rows[:, PAIR + WIDE :]], axis=1)
-    return own, other
+def by_core(core, own, other):
+    return jnp.where(core == 0, own, other), jnp.where(core == 0, other, own)
+
+
+def split_features(core, rows):
+    first = jnp.concatenate([rows[:, :WIDE], rows[:, PAIR : PAIR + WIDE]], axis=1)
+    second = jnp.concatenate([rows[:, WIDE:PAIR], rows[:, PAIR + WIDE :]], axis=1)
+    return by_core(core, first, second)
 
 
 def body(tokens, expert_ids, gate_weights, w_gate, w_up, w_down, cotangent):
     gate_own, up_own, down_own = w_gate[0], w_up[0], w_down[0].T
     core = lax.axis_index("core")
-    others = swap(jnp.concatenate([tokens, cotangent], axis=0))
     ids, gates = expert_ids.T, gate_weights.T
     inputs = (ids, gates, tokens, cotangent)
     send = call(
         send_kernel,
-        shape(EXPERTS, QUADS, QUAD, 2 * PAIR),
-        core.reshape(1),
-        others,
+        shape(2 * EXPERTS, QUADS // 2, QUAD, 2 * PAIR),
         *in_hbm(*inputs),
-        in_specs=[SMEM_SPEC, VMEM_SPEC] + [HBM_SPEC] * 4,
+        in_specs=[HBM_SPEC] * 4,
         scratch_shapes=buffers(*inputs) + semaphores(4),
     )
-    quads = across(send, "expert")
+    quads = across(send, ("core", "expert"))
     gate_sent, up_sent, down_sent, _ = lax.optimization_barrier((gate_own, up_own, down_own, send))
     zeros = jnp.zeros((STACK - PAIR, FFW), BF)
     stacks = (
-        jnp.concatenate([gate_sent, swap(gate_sent), zeros], axis=0),
-        jnp.concatenate([up_sent, swap(up_sent), zeros], axis=0),
-        jnp.concatenate([zeros, down_sent, swap(down_sent)], axis=0),
+        jnp.concatenate([*by_core(core, gate_sent, swap(gate_sent)), zeros], axis=0),
+        jnp.concatenate([*by_core(core, up_sent, swap(up_sent)), zeros], axis=0),
+        jnp.concatenate([zeros, *by_core(core, down_sent, swap(down_sent))], axis=0),
     )
     rows, parts = call(
         sums_kernel,
@@ -337,7 +343,7 @@
         ids,
         gates,
     )
-    own, other = split_features(rows)
+    own, other = split_features(core, rows)
     other = swap(other)
     own, other = own.reshape(N_Y, SHARD, PAIR), other.reshape(N_Y, SHARD, PAIR)
     cut = SHARD - PIECE
@@ -402,7 +408,15 @@
     other_total = swap(total_last)
     back = after(back, other_total, *grads)
     token_grad, mixed = call(
-        mix_kernel, [shape(*tokens.shape)] * 2, pick, gated, back, total_last, other_total
+        mix_kernel,
+        [shape(*tokens.shape)] * 2,
+        core.reshape(1),
+        pick,
+        gated,
+        back,
+        total_last,
+        other_total,
+        in_specs=[SMEM_SPEC] + [VMEM_SPEC] * 5,
     )
     return mixed, token_grad, grads[0][None], grads[1][None], grads[2].T[None]
 

time: 197 us -> 194 us (0.985)
  waiting for transfers between devices: 71.7 us -> 76.8 us
  other arithmetic: 5.88 us -> 1.45 us
  starting transfers between devices: 52.2 us -> 49.5 us
    ppermute x7 -> x6, starting transfers between devices: 24.7 us -> 13.6 us  [swap(): return lax.ppermute(array, 'core', [(0, 1), (1, 0)])]
    all_to_all x3, starting transfers between devices: 27.5 us -> 35.8 us  [across(): return lax.all_to_all(quads, axis, split_axis=0, concat_axis=0, tiled=True)]
    reduce_scatter x1, waiting for transfers between devices: 30.6 us -> 35.1 us  [body(): sums = lax.psum_scatter(parts, 'y', scatter_dimension=0, tiled=True)]
    concatenate x4 -> x1, other arithmetic: 4.69 us -> 0.31 us  [body(): jnp.concatenate([zeros, *by_core(core, down_sent, swap(down_sent))], axis=0)]
    all_to_all x3, waiting for transfers between devices: 18.9 us -> 21.8 us  [across(): return lax.all_to_all(quads, axis, split_axis=0, concat_axis=0, tiled=True)]
    ppermute x7 -> x6, waiting for transfers between devices: 5.27 us -> 4.06 us  [swap(): return lax.ppermute(array, 'core', [(0, 1), (1, 0)])]
  transfers between devices with their start and end apart: 12 -> 11, of which waited for: 8 -> 7; matrix products, arithmetic and copies ran while one was open for 5% -> 3% of each run, Pallas kernels for 7% -> 7%
where the time goes in v10:
time: 194 us; the launch traced here: 193 us
  waiting for transfers between devices  76.8 us (40%)
  starting transfers between devices  49.5 us (26%)
  Pallas kernels  22.9 us (12%)
  blocking collectives  20.6 us (11%)
  between operations  14.4 us (7%)
  local copies, waits for them, and re-layouts  7.14 us (4%)
    all_to_all x3, starting transfers between devices, across(): return lax.all_to_all(quads, axis, split_axis=0, concat_axis=0, tiled=True)  35.8 us
    reduce_scatter x1, waiting for transfers between devices, body(): sums = lax.psum_scatter(parts, 'y', scatter_dimension=0, tiled=True)  35.1 us
    pallas_call x9, Pallas kernels, call(): pl.pallas_call(kernel, out_shape=out_shape, compiler_params=pltpu.Compile...  22.9 us
    all_to_all x3, waiting for transfers between devices, across(): return lax.all_to_all(quads, axis, split_axis=0, concat_axis=0, tiled=True)  21.8 us
    all_gather x1, blocking collectives, body(): full_last = lax.all_gather(shard_last, 'y', axis=0, tiled=True)  20.6 us
    all_gather x1, waiting for transfers between devices, body(): full = lax.all_gather(shard, ('y', 'core'), axis=0, tiled=True)  15.8 us
    ppermute x6, starting transfers between devices, swap(): return lax.ppermute(array, 'core', [(0, 1), (1, 0)])  13.6 us
    ppermute x6, waiting for transfers between devices, swap(): return lax.ppermute(array, 'core', [(0, 1), (1, 0)])  4.06 us
  transfers between devices with their start and end apart: 11, of which 7 were waited for; matrix products, arithmetic and copies ran while one was open for 3% of the time, Pallas kernels for 7%

profile of v10, /device:TPU:1, one launch (start us, length us, event | category | flops | bytes accessed | tf_op | source)
XLA Modules:
  0.0 192.9 jit_solution(85358494850695609)
XLA Ops:
  7.2 2.9 %send_kernel.1 = bf16[64,2,4,896]{3,2,1,0:T(4,128)(2,1)} custom-call(s32[8,64]{1,0:T(8,128)} %bitcast.25, f32[8,64]{1,0:T(8,128)} %bitcast.27, bf16[64,224]{1,0:T(8,128)(2,1)} %tokens_hbm.1, bf16[64,224]{1,0:T(8,128)(2,1)} %cotangent_hbm.1), custom_call_target="tpu_custom_call" | custom-call | tf_op jit(solution)/shard_map/send_kernel/pallas_call | solution.py:260
  10.1 15.1 %all-to-all-start = ((bf16[64,2,4,896]{3,2,1,0:T(4,128)(2,1)}), bf16[64,2,4,896]{3,2,1,0:T(4,128)(2,1)}, u32[]{:S(2)}, u32[]{:S(2)}) async-start(bf16[64,2,4,896]{3,2,1,0:T(4,128)(2,1)} %send_kernel.1), calls=%async_computation | async-start | bytes 1835008 | tf_op jit(solution)/shard_map/all_to_all | solution.py:286
  25.3 2.3 %collective-permute-start = (bf16[224,1024]{1,0:T(8,128)(2,1)S(1)}, bf16[224,1024]{1,0:T(8,128)(2,1)S(1)}, u32[]{:S(2)}, u32[]{:S(2)}) collective-permute-start(bf16[224,1024]{1,0:T(8,128)(2,1)S(1)} %bitcast.41), channel_id=1, source_target_pairs={{0,32},{32,0},{1,33},{33,1},{2,34},{34,2},{3,35},{35,3},{4,36},{36... | collective-permute-start | bytes 1376264 | tf_op jit(solution)/shard_map/ppermute | solution.py:290
  27.7 2.0 %collective-permute-start.1 = (bf16[224,1024]{1,0:T(8,128)(2,1)S(1)}, bf16[224,1024]{1,0:T(8,128)(2,1)S(1)}, u32[]{:S(2)}, u32[]{:S(2)}) collective-permute-start(bf16[224,1024]{1,0:T(8,128)(2,1)S(1)} %bitcast.38), channel_id=1, source_target_pairs={{0,32},{32,0},{1,33},{33,1},{2,34},{34,2},{3,35},{35,3},{4,36},{36... | collective-permute-start | bytes 1376264 | tf_op jit(solution)/shard_map/ppermute | solution.py:290
  29.7 2.3 %collective-permute-start.2 = (bf16[224,1024]{1,0:T(8,128)(2,1)S(1)}, bf16[224,1024]{1,0:T(8,128)(2,1)S(1)}, u32[]{:S(2)}, u32[]{:S(2)}) collective-permute-start(bf16[224,1024]{1,0:T(8,128)(2,1)S(1)} %bitcast.35), channel_id=1, source_target_pairs={{0,32},{32,0},{1,33},{33,1},{2,34},{34,2},{3,35},{35,3},{4,36},{36... | collective-permute-start | bytes 1376264 | tf_op jit(solution)/shard_map/ppermute | solution.py:290
  32.2 1.2 collective-permute-done.2
  33.8 16.8 %all-to-all-done.quads = bf16[64,2,4,896]{3,2,1,0:T(4,128)(2,1)} async-done(((bf16[64,2,4,896]{3,2,1,0:T(4,128)(2,1)}), bf16[64,2,4,896]{3,2,1,0:T(4,128)(2,1)}, u32[]{:S(2)}, u32[]{:S(2)}) %all-to-all-start) | async-done | bytes 917536 | tf_op jit(solution)/shard_map/all_to_all | solution.py:286
  50.6 4.1 %sums_kernel.1 = (bf16[512,896]{1,0:T(8,128)(2,1)}, bf16[512,3072]{1,0:T(8,128)(2,1)}) custom-call(bf16[64,2,4,896]{3,2,1,0:T(4,128)(2,1)} %all-to-all-done.quads, bf16[512,1024]{1,0:T(8,128)(2,1)S(1)} %get-tuple-element.73.gate, bf16[512,1024]{1,0:T(8,128)(2,1)S(1)} %get-tuple-element.72.up, bf16[512,1024]{1,0:T(8,128)(2,1)S(1)} %get-tuple-element.71.down), custom_call_target="tpu_custom_call" | custom-call | tf_op jit(solution)/shard_map/sums_kernel/pallas_call | solution.py:260
  54.8 1.6 fusion
  56.9 1.9 collective-permute-start.3
  62.9 35.1 %reduce-scatter.2.cloned.1.call-done.sums_hbm = bf16[64,3072]{1,0:T(8,128)(2,1)} async-done(((bf16[512,3072]{1,0:T(8,128)(2,1)}), bf16[64,3072]{1,0:T(8,128)(2,1)}) %reduce-scatter.2.cloned.1.call-update) | async-done | bytes 393232 | tf_op jit(solution)/shard_map/reduce_scatter | solution.py:337
  98.1 1.8 shard_kernel.1
  99.9 20.6 %all_gather.7.full.refs_1_ = bf16[128,3072]{1,0:T(8,128)(2,1)S(1)} all-gather(bf16[16,3072]{1,0:T(8,128)(2,1)S(1)} %get-tuple-element.46), channel_id=1, replica_groups=mesh['y'=8,'core'=2,'expert'=32] {'y'}, dimensions={0}, use_global_device_ids=true | all-gather | bytes 884736 | tf_op jit(solution)/shard_map/all_gather | solution.py:370
  120.5 1.2 back_last_kernel.1
  123.3 10.8 %all-to-all-start.2 = ((bf16[32,1,4,896]{3,2,1,0:T(4,128)(2,1)}), bf16[32,1,4,896]{3,2,1,0:T(4,128)(2,1)S(1)}, u32[]{:S(2)}, u32[]{:S(2)}) async-start(bf16[32,1,4,896]{3,2,1,0:T(4,128)(2,1)} %copy-done.4), calls=%async_computation.3 | async-start | bytes 458752 | tf_op jit(solution)/shard_map/all_to_all | solution.py:286
  134.1 15.8 %all-gather.2.cloned.1.call-done.full_hbm.refs_0_ = bf16[768,3072]{1,0:T(8,128)(2,1)} async-done(((bf16[48,3072]{1,0:T(8,128)(2,1)}), bf16[768,3072]{1,0:T(8,128)(2,1)}) %all-gather.2.cloned.1.call-update) | async-done | bytes 4718608 | tf_op jit(solution)/shard_map/all_gather | solution.py:368
  149.9 5.2 %back_kernel.1 = bf16[32,3,4,896]{3,2,1,0:T(4,128)(2,1)} custom-call(bf16[768,3072]{1,0:T(8,128)(2,1)} %all-gather.2.cloned.1.call-done.full_hbm.refs_0_, bf16[224,1024]{1,0:T(8,128)(2,1)} %bitcast.40, bf16[224,1024]{1,0:T(8,128)(2,1)} %bitcast.37, bf16[224,1024]{1,0:T(8,128)(2,1)} %bitcast.34), custom_call_target="tpu_custom_call" | custom-call | tf_op jit(solution)/shard_map/back_kernel/pallas_call | solution.py:260
  155.1 9.9 %all-to-all-start.1 = ((bf16[32,3,4,896]{3,2,1,0:T(4,128)(2,1)}), bf16[32,3,4,896]{3,2,1,0:T(4,128)(2,1)S(1)}, u32[]{:S(2)}, u32[]{:S(2)}) async-start(bf16[32,3,4,896]{3,2,1,0:T(4,128)(2,1)} %back_kernel.1), calls=%async_computation.2 | async-start | bytes 1376256 | tf_op jit(solution)/shard_map/all_to_all | solution.py:286
  165.1 2.8 %collective-permute-start.4 = (bf16[128,3072]{1,0:T(8,128)(2,1)S(1)}, bf16[128,3072]{1,0:T(8,128)(2,1)S(1)}, u32[]{:S(2)}, u32[]{:S(2)}) collective-permute-start(bf16[128,3072]{1,0:T(8,128)(2,1)S(1)} %copy-done.1), channel_id=1, source_target_pairs={{0,32},{32,0},{1,33},{33,1},{2,34},{34,2},{3,35},{35,3},{4,36},{36... | collective-permute-start | bytes 2359304 | tf_op jit(solution)/shard_map/ppermute | solution.py:290
  167.8 1.7 collective-permute-done.4.refs_2_
  170.4 5.8 %grads_kernel.1 = (bf16[224,1024]{1,0:T(8,128)(2,1)}, bf16[224,1024]{1,0:T(8,128)(2,1)}, bf16[224,1024]{1,0:T(8,128)(2,1)}) custom-call(bf16[768,3072]{1,0:T(8,128)(2,1)} %all-gather.2.cloned.1.call-done.full_hbm.refs_0_, bf16[128,3072]{1,0:T(8,128)(2,1)} %copy-done, bf16[128,3072]{1,0:T(8,128)(2,1)} %copy-done.10, bf16[768,448]{1,0:T(8,128)(2,1)} %bitcast.29, ...), custom_call_target="tpu_custom_call" | custom-call | tf_op jit(solution)/shard_map/grads_kernel/pallas_call | solution.py:260
  176.5 2.3 %collective-permute-start.5 = (f32[64,896]{1,0:T(8,128)S(1)}, f32[64,896]{1,0:T(8,128)S(1)}, u32[]{:S(2)}, u32[]{:S(2)}) collective-permute-start(f32[64,896]{1,0:T(8,128)S(1)} %mix_last_kernel.1.own_ref), channel_id=1, source_target_pairs={{0,32},{32,0},{1,33},{33,1},{2,34},{34,2},{3,35},{35,3},{4,36},{36... | collective-permute-start | bytes 688136 | tf_op jit(solution)/shard_map/ppermute | solution.py:290
  179.8 5.0 %all-to-all-done.1.main_ref = bf16[32,3,4,896]{3,2,1,0:T(4,128)(2,1)S(1)} async-done(((bf16[32,3,4,896]{3,2,1,0:T(4,128)(2,1)}), bf16[32,3,4,896]{3,2,1,0:T(4,128)(2,1)S(1)}, u32[]{:S(2)}, u32[]{:S(2)}) %all-to-all-start.1) | async-done | bytes 688160 | tf_op jit(solution)/shard_map/all_to_all | solution.py:286
  184.9 1.2 mix_kernel.1
  (45 shorter events, 8.9 us)
Async XLA Ops:
  7.2 22.5 %copy-start.7 = (bf16[1,1024,224]{1,2,0:T(8,128)(2,1)S(1)}, bf16[1,1024,224]{1,2,0:T(8,128)(2,1)}, u32[]{:S(2)}) copy-start(bf16[1,1024,224]{1,2,0:T(8,128)(2,1)} %param.12) | copy-start | bytes 1376260
  7.2 20.5 %copy-start.8 = (bf16[1,224,1024]{2,1,0:T(8,128)(2,1)S(1)}, bf16[1,224,1024]{2,1,0:T(8,128)(2,1)}, u32[]{:S(2)}) copy-start(bf16[1,224,1024]{2,1,0:T(8,128)(2,1)} %param.11) | copy-start | bytes 1376260
  7.2 18.1 %copy-start.9 = (bf16[1,224,1024]{2,1,0:T(8,128)(2,1)S(1)}, bf16[1,224,1024]{2,1,0:T(8,128)(2,1)}, u32[]{:S(2)}) copy-start(bf16[1,224,1024]{2,1,0:T(8,128)(2,1)} %param.10) | copy-start | bytes 1376260
  10.1 40.5 %all-to-all-start = ((bf16[64,2,4,896]{3,2,1,0:T(4,128)(2,1)}), bf16[64,2,4,896]{3,2,1,0:T(4,128)(2,1)}, u32[]{:S(2)}, u32[]{:S(2)}) async-start(bf16[64,2,4,896]{3,2,1,0:T(4,128)(2,1)} %send_kernel.1), calls=%async_computation | async-start | bytes 1835008 | tf_op jit(solution)/shard_map/all_to_all | solution.py:286
  25.3 72.8 %reduce-scatter.2.cloned.1.call-start = ((), (), s32[]{:S(2)}) async-start(), calls=%async_computation.4 | async-start | bytes 3538944 | tf_op jit(solution)/shard_map/reduce_scatter | solution.py:337
  25.3 6.7 %collective-permute-start = (bf16[224,1024]{1,0:T(8,128)(2,1)S(1)}, bf16[224,1024]{1,0:T(8,128)(2,1)S(1)}, u32[]{:S(2)}, u32[]{:S(2)}) collective-permute-start(bf16[224,1024]{1,0:T(8,128)(2,1)S(1)} %bitcast.41), channel_id=1, source_target_pairs={{0,32},{32,0},{1,33},{33,1},{2,34},{34,2},{3,35},{35,3},{4,36},{36... | collective-permute-start | bytes 1376264 | tf_op jit(solution)/shard_map/ppermute | solution.py:290
  27.7 4.4 %collective-permute-start.1 = (bf16[224,1024]{1,0:T(8,128)(2,1)S(1)}, bf16[224,1024]{1,0:T(8,128)(2,1)S(1)}, u32[]{:S(2)}, u32[]{:S(2)}) collective-permute-start(bf16[224,1024]{1,0:T(8,128)(2,1)S(1)} %bitcast.38), channel_id=1, source_target_pairs={{0,32},{32,0},{1,33},{33,1},{2,34},{34,2},{3,35},{35,3},{4,36},{36... | collective-permute-start | bytes 1376264 | tf_op jit(solution)/shard_map/ppermute | solution.py:290
  29.7 3.8 %collective-permute-start.2 = (bf16[224,1024]{1,0:T(8,128)(2,1)S(1)}, bf16[224,1024]{1,0:T(8,128)(2,1)S(1)}, u32[]{:S(2)}, u32[]{:S(2)}) collective-permute-start(bf16[224,1024]{1,0:T(8,128)(2,1)S(1)} %bitcast.35), channel_id=1, source_target_pairs={{0,32},{32,0},{1,33},{33,1},{2,34},{34,2},{3,35},{35,3},{4,36},{36... | collective-permute-start | bytes 1376264 | tf_op jit(solution)/shard_map/ppermute | solution.py:290
  54.8 95.1 %all-gather.2.cloned.1.call-start = ((), (), s32[]{:S(2)}) async-start(), calls=%async_computation.5 | async-start | bytes 5013504 | tf_op jit(solution)/shard_map/all_gather | solution.py:368
  56.5 3.4 %copy-start.5 = (s32[64,8]{0,1:T(8,128)S(1)}, s32[64,8]{0,1:T(8,128)}, u32[]{:S(2)}) copy-start(s32[64,8]{0,1:T(8,128)} %param.8) | copy-start | bytes 6148
  56.5 3.4 %copy-start.6 = (f32[64,8]{0,1:T(8,128)S(1)}, f32[64,8]{0,1:T(8,128)}, u32[]{:S(2)}) copy-start(f32[64,8]{0,1:T(8,128)} %param.9) | copy-start | bytes 6148
  56.9 4.2 %collective-permute-start.3 = (bf16[512,448]{1,0:T(8,128)(2,1)S(1)}, bf16[512,448]{1,0:T(8,128)(2,1)S(1)}, u32[]{:S(2)}, u32[]{:S(2)}) collective-permute-start(bf16[512,448]{1,0:T(8,128)(2,1)S(1)} %maximum_select_fusion.1), channel_id=1, source_target_pairs={{0,32},{32,0},{1,33},{33,1},{2,34},{34,2},{3,35},{35,3},{4,36},{36... | collective-permute-start | bytes 1376264 | tf_op jit(solution)/shard_map/ppermute | solution.py:290
  60.4 0.7 copy-start.2
  121.7 0.9 copy-start
  122.6 0.7 copy-start.4
  123.3 31.8 %all-to-all-start.2 = ((bf16[32,1,4,896]{3,2,1,0:T(4,128)(2,1)}), bf16[32,1,4,896]{3,2,1,0:T(4,128)(2,1)S(1)}, u32[]{:S(2)}, u32[]{:S(2)}) async-start(bf16[32,1,4,896]{3,2,1,0:T(4,128)(2,1)} %copy-done.4), calls=%async_computation.3 | async-start | bytes 458752 | tf_op jit(solution)/shard_map/all_to_all | solution.py:286
  134.1 30.9 %copy-start.1 = (bf16[128,3072]{1,0:T(8,128)(2,1)S(1)}, bf16[128,3072]{1,0:T(8,128)(2,1)}, u32[]{:S(2)}) copy-start(bf16[128,3072]{1,0:T(8,128)(2,1)} %copy-done) | copy-start | bytes 2359300
  155.1 29.8 %all-to-all-start.1 = ((bf16[32,3,4,896]{3,2,1,0:T(4,128)(2,1)}), bf16[32,3,4,896]{3,2,1,0:T(4,128)(2,1)S(1)}, u32[]{:S(2)}, u32[]{:S(2)}) async-start(bf16[32,3,4,896]{3,2,1,0:T(4,128)(2,1)} %back_kernel.1), calls=%async_computation.2 | async-start | bytes 1376256 | tf_op jit(solution)/shard_map/all_to_all | solution.py:286
  165.0 11.2 %copy-start.3 = (bf16[2,512,64]{2,1,0:T(8,128)(2,1)S(1)}, bf16[2,512,64]{2,1,0:T(8,128)(2,1)}, u32[]{:S(2)}) copy-start(bf16[2,512,64]{2,1,0:T(8,128)(2,1)} %copy-done.2) | copy-start | bytes 393220
  165.1 4.5 %collective-permute-start.4 = (bf16[128,3072]{1,0:T(8,128)(2,1)S(1)}, bf16[128,3072]{1,0:T(8,128)(2,1)S(1)}, u32[]{:S(2)}, u32[]{:S(2)}) collective-permute-start(bf16[128,3072]{1,0:T(8,128)(2,1)S(1)} %copy-done.1), channel_id=1, source_target_pairs={{0,32},{32,0},{1,33},{33,1},{2,34},{34,2},{3,35},{35,3},{4,36},{36... | collective-permute-start | bytes 2359304 | tf_op jit(solution)/shard_map/ppermute | solution.py:290
  169.5 0.9 copy-start.10
  176.5 3.4 %collective-permute-start.5 = (f32[64,896]{1,0:T(8,128)S(1)}, f32[64,896]{1,0:T(8,128)S(1)}, u32[]{:S(2)}, u32[]{:S(2)}) collective-permute-start(f32[64,896]{1,0:T(8,128)S(1)} %mix_last_kernel.1.own_ref), channel_id=1, source_target_pairs={{0,32},{32,0},{1,33},{33,1},{2,34},{34,2},{3,35},{35,3},{4,36},{36... | collective-permute-start | bytes 688136 | tf_op jit(solution)/shard_map/ppermute | solution.py:290
Sparse Core Ops, SparseCore 0:
  54.9 43.0 reduce-scatter.1
  100.7 49.1 all-gather.1

commit v11 on v10

--- a/solution.py
+++ b/solution.py
@@ -373,6 +373,7 @@
     )
     back_last = across(send_last, "expert")
     full_other = swap(after(full_last, send_last))
+    full, full_other = lax.optimization_barrier((full, full_other))
 
     back = call(
         back_kernel,

time: 194 us -> 195 us (level)
  waiting for transfers between devices: 76.8 us -> 70.3 us
  starting transfers between devices: 49.5 us -> 54.9 us
  blocking collectives: 20.6 us -> 23.1 us
    all_gather x1, waiting for transfers between devices: 15.8 us -> 3.38 us  [body(): full = lax.all_gather(shard, ('y', 'core'), axis=0, tiled=True)]
    ppermute x6, starting transfers between devices: 13.6 us -> 22.3 us  [swap(): return lax.ppermute(array, 'core', [(0, 1), (1, 0)])]
    all_to_all x3, waiting for transfers between devices: 21.8 us -> 29.5 us  [across(): return lax.all_to_all(quads, axis, split_axis=0, concat_axis=0, tiled=True)]
    all_to_all x3, starting transfers between devices: 35.8 us -> 32.5 us  [across(): return lax.all_to_all(quads, axis, split_axis=0, concat_axis=0, tiled=True)]
    all_gather x1, blocking collectives: 20.6 us -> 23.1 us  [body(): full_last = lax.all_gather(shard_last, 'y', axis=0, tiled=True)]
where the time goes in v11:
time: 195 us; the launch traced here: 194 us
  waiting for transfers between devices  70.3 us (36%)
  starting transfers between devices  54.9 us (28%)
  Pallas kernels  24.1 us (12%)
  blocking collectives  23.1 us (12%)
  between operations  14.4 us (7%)
  local copies, waits for them, and re-layouts  5.38 us (3%)
    reduce_scatter x1, waiting for transfers between devices, body(): sums = lax.psum_scatter(parts, 'y', scatter_dimension=0, tiled=True)  35.1 us
    all_to_all x3, starting transfers between devices, across(): return lax.all_to_all(quads, axis, split_axis=0, concat_axis=0, tiled=True)  32.5 us
    all_to_all x3, waiting for transfers between devices, across(): return lax.all_to_all(quads, axis, split_axis=0, concat_axis=0, tiled=True)  29.5 us
    pallas_call x9, Pallas kernels, call(): pl.pallas_call(kernel, out_shape=out_shape, compiler_params=pltpu.Compile...  24.1 us
    all_gather x1, blocking collectives, body(): full_last = lax.all_gather(shard_last, 'y', axis=0, tiled=True)  23.1 us
    ppermute x6, starting transfers between devices, swap(): return lax.ppermute(array, 'core', [(0, 1), (1, 0)])  22.3 us
  transfers between devices with their start and end apart: 11, of which 7 were waited for; matrix products, arithmetic and copies ran while one was open for 3% of the time, Pallas kernels for 7%

profile of v11, /device:TPU:1, one launch (start us, length us, event | category | flops | bytes accessed | tf_op | source)
XLA Modules:
  0.0 193.6 jit_solution(13448293651377212942)
XLA Ops:
  7.2 2.9 %send_kernel.1 = bf16[64,2,4,896]{3,2,1,0:T(4,128)(2,1)} custom-call(s32[8,64]{1,0:T(8,128)} %bitcast.25, f32[8,64]{1,0:T(8,128)} %bitcast.27, bf16[64,224]{1,0:T(8,128)(2,1)} %tokens_hbm.1, bf16[64,224]{1,0:T(8,128)(2,1)} %cotangent_hbm.1), custom_call_target="tpu_custom_call" | custom-call | tf_op jit(solution)/shard_map/send_kernel/pallas_call | solution.py:260
  10.1 15.1 %all-to-all-start = ((bf16[64,2,4,896]{3,2,1,0:T(4,128)(2,1)}), bf16[64,2,4,896]{3,2,1,0:T(4,128)(2,1)}, u32[]{:S(2)}, u32[]{:S(2)}) async-start(bf16[64,2,4,896]{3,2,1,0:T(4,128)(2,1)} %send_kernel.1), calls=%async_computation | async-start | bytes 1835008 | tf_op jit(solution)/shard_map/all_to_all | solution.py:286
  25.3 2.3 %collective-permute-start.1 = (bf16[224,1024]{1,0:T(8,128)(2,1)S(1)}, bf16[224,1024]{1,0:T(8,128)(2,1)S(1)}, u32[]{:S(2)}, u32[]{:S(2)}) collective-permute-start(bf16[224,1024]{1,0:T(8,128)(2,1)S(1)} %bitcast.38), channel_id=1, source_target_pairs={{0,32},{32,0},{1,33},{33,1},{2,34},{34,2},{3,35},{35,3},{4,36},{36... | collective-permute-start | bytes 1376264 | tf_op jit(solution)/shard_map/ppermute | solution.py:290
  27.7 2.0 %collective-permute-start = (bf16[224,1024]{1,0:T(8,128)(2,1)S(1)}, bf16[224,1024]{1,0:T(8,128)(2,1)S(1)}, u32[]{:S(2)}, u32[]{:S(2)}) collective-permute-start(bf16[224,1024]{1,0:T(8,128)(2,1)S(1)} %bitcast.41), channel_id=1, source_target_pairs={{0,32},{32,0},{1,33},{33,1},{2,34},{34,2},{3,35},{35,3},{4,36},{36... | collective-permute-start | bytes 1376264 | tf_op jit(solution)/shard_map/ppermute | solution.py:290
  29.7 2.3 %collective-permute-start.2 = (bf16[224,1024]{1,0:T(8,128)(2,1)S(1)}, bf16[224,1024]{1,0:T(8,128)(2,1)S(1)}, u32[]{:S(2)}, u32[]{:S(2)}) collective-permute-start(bf16[224,1024]{1,0:T(8,128)(2,1)S(1)} %bitcast.35), channel_id=1, source_target_pairs={{0,32},{32,0},{1,33},{33,1},{2,34},{34,2},{3,35},{35,3},{4,36},{36... | collective-permute-start | bytes 1376264 | tf_op jit(solution)/shard_map/ppermute | solution.py:290
  32.2 1.2 collective-permute-done.2
  33.8 16.8 %all-to-all-done.quads = bf16[64,2,4,896]{3,2,1,0:T(4,128)(2,1)} async-done(((bf16[64,2,4,896]{3,2,1,0:T(4,128)(2,1)}), bf16[64,2,4,896]{3,2,1,0:T(4,128)(2,1)}, u32[]{:S(2)}, u32[]{:S(2)}) %all-to-all-start) | async-done | bytes 917536 | tf_op jit(solution)/shard_map/all_to_all | solution.py:286
  50.6 4.0 %sums_kernel.1 = (bf16[512,896]{1,0:T(8,128)(2,1)}, bf16[512,3072]{1,0:T(8,128)(2,1)}) custom-call(bf16[64,2,4,896]{3,2,1,0:T(4,128)(2,1)} %all-to-all-done.quads, bf16[512,1024]{1,0:T(8,128)(2,1)S(1)} %get-tuple-element.77.gate, bf16[512,1024]{1,0:T(8,128)(2,1)S(1)} %get-tuple-element.76.up, bf16[512,1024]{1,0:T(8,128)(2,1)S(1)} %get-tuple-element.75.down), custom_call_target="tpu_custom_call" | custom-call | tf_op jit(solution)/shard_map/sums_kernel/pallas_call | solution.py:260
  54.8 1.6 fusion
  56.8 1.9 collective-permute-start.3
  62.9 35.1 %reduce-scatter.2.cloned.1.call-done.sums_hbm = bf16[64,3072]{1,0:T(8,128)(2,1)} async-done(((bf16[512,3072]{1,0:T(8,128)(2,1)}), bf16[64,3072]{1,0:T(8,128)(2,1)}) %reduce-scatter.2.cloned.1.call-update) | async-done | bytes 393232 | tf_op jit(solution)/shard_map/reduce_scatter | solution.py:337
  98.0 1.8 shard_kernel.1
  99.9 23.1 %all_gather.7.full.refs_1_ = bf16[128,3072]{1,0:T(8,128)(2,1)} all-gather(bf16[16,3072]{1,0:T(8,128)(2,1)S(1)} %get-tuple-element.48), channel_id=1, replica_groups=mesh['y'=8,'core'=2,'expert'=32] {'y'}, dimensions={0}, use_global_device_ids=true | all-gather | bytes 884736 | tf_op jit(solution)/shard_map/all_gather | solution.py:370
  122.9 2.3 %back_last_kernel.1 = bf16[32,1,4,896]{3,2,1,0:T(4,128)(2,1)S(1)} custom-call(bf16[128,3072]{1,0:T(8,128)(2,1)} %all_gather.7.full.refs_1_, bf16[512,1024]{1,0:T(8,128)(2,1)S(1)} %get-tuple-element.77.gate, bf16[512,1024]{1,0:T(8,128)(2,1)S(1)} %get-tuple-element.76.up, bf16[512,1024]{1,0:T(8,128)(2,1)S(1)} %get-tuple-element.75.down), custom_call_target="tpu_custom_call" | custom-call | tf_op jit(solution)/shard_map/back_last_kernel/pallas_call | solution.py:260
  126.0 11.3 %collective-permute-start.4 = (bf16[128,3072]{1,0:T(8,128)(2,1)}, bf16[128,3072]{1,0:T(8,128)(2,1)S(1)}, u32[]{:S(2)}, u32[]{:S(2)}) collective-permute-start(bf16[128,3072]{1,0:T(8,128)(2,1)} %all_gather.7.full.refs_1_), channel_id=1, source_target_pairs={{0,32},{32,0},{1,33},{33,1},{2,34},{34,2},{3,35},{35,3},{4,36},{36... | collective-permute-start | bytes 2359304 | tf_op jit(solution)/shard_map/ppermute | solution.py:290
  137.3 9.7 %all-to-all-start.2 = ((bf16[32,1,4,896]{3,2,1,0:T(4,128)(2,1)}), bf16[32,1,4,896]{3,2,1,0:T(4,128)(2,1)S(1)}, u32[]{:S(2)}, u32[]{:S(2)}) async-start(bf16[32,1,4,896]{3,2,1,0:T(4,128)(2,1)} %copy-done.2), calls=%async_computation.3 | async-start | bytes 458752 | tf_op jit(solution)/shard_map/all_to_all | solution.py:286
  147.1 3.4 %all-gather.2.cloned.1.call-done.full_hbm.refs_0_ = bf16[768,3072]{1,0:T(8,128)(2,1)} async-done(((bf16[48,3072]{1,0:T(8,128)(2,1)}), bf16[768,3072]{1,0:T(8,128)(2,1)}) %all-gather.2.cloned.1.call-update) | async-done | bytes 4718608 | tf_op jit(solution)/shard_map/all_gather | solution.py:368
  150.4 5.2 %back_kernel.1 = bf16[32,3,4,896]{3,2,1,0:T(4,128)(2,1)} custom-call(bf16[768,3072]{1,0:T(8,128)(2,1)} %all-gather.2.cloned.1.call-done.full_hbm.refs_0_, bf16[224,1024]{1,0:T(8,128)(2,1)} %bitcast.40, bf16[224,1024]{1,0:T(8,128)(2,1)} %bitcast.37, bf16[224,1024]{1,0:T(8,128)(2,1)} %bitcast.34), custom_call_target="tpu_custom_call" | custom-call | tf_op jit(solution)/shard_map/back_kernel/pallas_call | solution.py:260
  155.6 2.7 %all-to-all-done.2.last_ref = bf16[32,1,4,896]{3,2,1,0:T(4,128)(2,1)S(1)} async-done(((bf16[32,1,4,896]{3,2,1,0:T(4,128)(2,1)}), bf16[32,1,4,896]{3,2,1,0:T(4,128)(2,1)S(1)}, u32[]{:S(2)}, u32[]{:S(2)}) %all-to-all-start.2) | async-done | bytes 229408 | tf_op jit(solution)/shard_map/all_to_all | solution.py:286
  158.3 7.7 %all-to-all-start.1 = ((bf16[32,3,4,896]{3,2,1,0:T(4,128)(2,1)}), bf16[32,3,4,896]{3,2,1,0:T(4,128)(2,1)S(1)}, u32[]{:S(2)}, u32[]{:S(2)}) async-start(bf16[32,3,4,896]{3,2,1,0:T(4,128)(2,1)} %back_kernel.1), calls=%async_computation.2 | async-start | bytes 1376256 | tf_op jit(solution)/shard_map/all_to_all | solution.py:286
  166.0 5.8 %grads_kernel.1 = (bf16[224,1024]{1,0:T(8,128)(2,1)}, bf16[224,1024]{1,0:T(8,128)(2,1)}, bf16[224,1024]{1,0:T(8,128)(2,1)}) custom-call(bf16[768,3072]{1,0:T(8,128)(2,1)} %all-gather.2.cloned.1.call-done.full_hbm.refs_0_, bf16[128,3072]{1,0:T(8,128)(2,1)} %all_gather.7.full.refs_1_, bf16[128,3072]{1,0:T(8,128)(2,1)} %copy-done.8, bf16[768,448]{1,0:T(8,128)(2,1)} %bitcast.29, ...), custom_call_target="tpu_custom_call" | custom-call | tf_op jit(solution)/shard_map/grads_kernel/pallas_call | solution.py:260
  172.0 2.4 %collective-permute-start.5 = (f32[64,896]{1,0:T(8,128)S(1)}, f32[64,896]{1,0:T(8,128)S(1)}, u32[]{:S(2)}, u32[]{:S(2)}) collective-permute-start(f32[64,896]{1,0:T(8,128)S(1)} %mix_last_kernel.1.own_ref), channel_id=1, source_target_pairs={{0,32},{32,0},{1,33},{33,1},{2,34},{34,2},{3,35},{35,3},{4,36},{36... | collective-permute-start | bytes 688136 | tf_op jit(solution)/shard_map/ppermute | solution.py:290
  175.6 10.0 %all-to-all-done.1.main_ref = bf16[32,3,4,896]{3,2,1,0:T(4,128)(2,1)S(1)} async-done(((bf16[32,3,4,896]{3,2,1,0:T(4,128)(2,1)}), bf16[32,3,4,896]{3,2,1,0:T(4,128)(2,1)S(1)}, u32[]{:S(2)}, u32[]{:S(2)}) %all-to-all-start.1) | async-done | bytes 688160 | tf_op jit(solution)/shard_map/all_to_all | solution.py:286
  185.6 1.2 mix_kernel.1
  (41 shorter events, 7.2 us)
Async XLA Ops:
  7.2 20.5 %copy-start.7 = (bf16[1,224,1024]{2,1,0:T(8,128)(2,1)S(1)}, bf16[1,224,1024]{2,1,0:T(8,128)(2,1)}, u32[]{:S(2)}) copy-start(bf16[1,224,1024]{2,1,0:T(8,128)(2,1)} %param.10) | copy-start | bytes 1376260
  7.2 18.1 %copy-start.6 = (bf16[1,224,1024]{2,1,0:T(8,128)(2,1)S(1)}, bf16[1,224,1024]{2,1,0:T(8,128)(2,1)}, u32[]{:S(2)}) copy-start(bf16[1,224,1024]{2,1,0:T(8,128)(2,1)} %param.11) | copy-start | bytes 1376260
  7.2 22.5 %copy-start.5 = (bf16[1,1024,224]{1,2,0:T(8,128)(2,1)S(1)}, bf16[1,1024,224]{1,2,0:T(8,128)(2,1)}, u32[]{:S(2)}) copy-start(bf16[1,1024,224]{1,2,0:T(8,128)(2,1)} %param.12) | copy-start | bytes 1376260
  10.1 40.5 %all-to-all-start = ((bf16[64,2,4,896]{3,2,1,0:T(4,128)(2,1)}), bf16[64,2,4,896]{3,2,1,0:T(4,128)(2,1)}, u32[]{:S(2)}, u32[]{:S(2)}) async-start(bf16[64,2,4,896]{3,2,1,0:T(4,128)(2,1)} %send_kernel.1), calls=%async_computation | async-start | bytes 1835008 | tf_op jit(solution)/shard_map/all_to_all | solution.py:286
  25.3 72.7 %reduce-scatter.2.cloned.1.call-start = ((), (), s32[]{:S(2)}) async-start(), calls=%async_computation.4 | async-start | bytes 3538944 | tf_op jit(solution)/shard_map/reduce_scatter | solution.py:337
  25.3 6.7 %collective-permute-start.1 = (bf16[224,1024]{1,0:T(8,128)(2,1)S(1)}, bf16[224,1024]{1,0:T(8,128)(2,1)S(1)}, u32[]{:S(2)}, u32[]{:S(2)}) collective-permute-start(bf16[224,1024]{1,0:T(8,128)(2,1)S(1)} %bitcast.38), channel_id=1, source_target_pairs={{0,32},{32,0},{1,33},{33,1},{2,34},{34,2},{3,35},{35,3},{4,36},{36... | collective-permute-start | bytes 1376264 | tf_op jit(solution)/shard_map/ppermute | solution.py:290
  27.7 4.4 %collective-permute-start = (bf16[224,1024]{1,0:T(8,128)(2,1)S(1)}, bf16[224,1024]{1,0:T(8,128)(2,1)S(1)}, u32[]{:S(2)}, u32[]{:S(2)}) collective-permute-start(bf16[224,1024]{1,0:T(8,128)(2,1)S(1)} %bitcast.41), channel_id=1, source_target_pairs={{0,32},{32,0},{1,33},{33,1},{2,34},{34,2},{3,35},{35,3},{4,36},{36... | collective-permute-start | bytes 1376264 | tf_op jit(solution)/shard_map/ppermute | solution.py:290
  29.7 3.8 %collective-permute-start.2 = (bf16[224,1024]{1,0:T(8,128)(2,1)S(1)}, bf16[224,1024]{1,0:T(8,128)(2,1)S(1)}, u32[]{:S(2)}, u32[]{:S(2)}) collective-permute-start(bf16[224,1024]{1,0:T(8,128)(2,1)S(1)} %bitcast.35), channel_id=1, source_target_pairs={{0,32},{32,0},{1,33},{33,1},{2,34},{34,2},{3,35},{35,3},{4,36},{36... | collective-permute-start | bytes 1376264 | tf_op jit(solution)/shard_map/ppermute | solution.py:290
  54.7 95.7 %all-gather.2.cloned.1.call-start = ((), (), s32[]{:S(2)}) async-start(), calls=%async_computation.5 | async-start | bytes 5013504 | tf_op jit(solution)/shard_map/all_gather | solution.py:368
  56.4 3.4 %copy-start.3 = (s32[64,8]{0,1:T(8,128)S(1)}, s32[64,8]{0,1:T(8,128)}, u32[]{:S(2)}) copy-start(s32[64,8]{0,1:T(8,128)} %param.8) | copy-start | bytes 6148
  56.4 3.4 %copy-start.4 = (f32[64,8]{0,1:T(8,128)S(1)}, f32[64,8]{0,1:T(8,128)}, u32[]{:S(2)}) copy-start(f32[64,8]{0,1:T(8,128)} %param.9) | copy-start | bytes 6148
  56.8 4.2 %collective-permute-start.3 = (bf16[512,448]{1,0:T(8,128)(2,1)S(1)}, bf16[512,448]{1,0:T(8,128)(2,1)S(1)}, u32[]{:S(2)}, u32[]{:S(2)}) collective-permute-start(bf16[512,448]{1,0:T(8,128)(2,1)S(1)} %maximum_select_fusion.1), channel_id=1, source_target_pairs={{0,32},{32,0},{1,33},{33,1},{2,34},{34,2},{3,35},{35,3},{4,36},{36... | collective-permute-start | bytes 1376264 | tf_op jit(solution)/shard_map/ppermute | solution.py:290
  60.3 0.7 copy-start
  125.3 0.7 copy-start.2
  126.0 21.0 %collective-permute-start.4 = (bf16[128,3072]{1,0:T(8,128)(2,1)}, bf16[128,3072]{1,0:T(8,128)(2,1)S(1)}, u32[]{:S(2)}, u32[]{:S(2)}) collective-permute-start(bf16[128,3072]{1,0:T(8,128)(2,1)} %all_gather.7.full.refs_1_), channel_id=1, source_target_pairs={{0,32},{32,0},{1,33},{33,1},{2,34},{34,2},{3,35},{35,3},{4,36},{36... | collective-permute-start | bytes 2359304 | tf_op jit(solution)/shard_map/ppermute | solution.py:290
  137.3 21.0 %all-to-all-start.2 = ((bf16[32,1,4,896]{3,2,1,0:T(4,128)(2,1)}), bf16[32,1,4,896]{3,2,1,0:T(4,128)(2,1)S(1)}, u32[]{:S(2)}, u32[]{:S(2)}) async-start(bf16[32,1,4,896]{3,2,1,0:T(4,128)(2,1)} %copy-done.2), calls=%async_computation.3 | async-start | bytes 458752 | tf_op jit(solution)/shard_map/all_to_all | solution.py:286
  147.0 8.6 %copy-start.8 = (bf16[128,3072]{1,0:T(8,128)(2,1)}, bf16[128,3072]{1,0:T(8,128)(2,1)S(1)}, u32[]{:S(2)}) copy-start(bf16[128,3072]{1,0:T(8,128)(2,1)S(1)} %collective-permute-done.4.refs_2_) | copy-start | bytes 2359300
  158.3 27.3 %all-to-all-start.1 = ((bf16[32,3,4,896]{3,2,1,0:T(4,128)(2,1)}), bf16[32,3,4,896]{3,2,1,0:T(4,128)(2,1)S(1)}, u32[]{:S(2)}, u32[]{:S(2)}) async-start(bf16[32,3,4,896]{3,2,1,0:T(4,128)(2,1)} %back_kernel.1), calls=%async_computation.2 | async-start | bytes 1376256 | tf_op jit(solution)/shard_map/all_to_all | solution.py:286
  166.0 5.8 %copy-start.1 = (bf16[2,512,64]{2,1,0:T(8,128)(2,1)S(1)}, bf16[2,512,64]{2,1,0:T(8,128)(2,1)}, u32[]{:S(2)}) copy-start(bf16[2,512,64]{2,1,0:T(8,128)(2,1)} %copy-done) | copy-start | bytes 393220
  172.0 3.5 %collective-permute-start.5 = (f32[64,896]{1,0:T(8,128)S(1)}, f32[64,896]{1,0:T(8,128)S(1)}, u32[]{:S(2)}, u32[]{:S(2)}) collective-permute-start(f32[64,896]{1,0:T(8,128)S(1)} %mix_last_kernel.1.own_ref), channel_id=1, source_target_pairs={{0,32},{32,0},{1,33},{33,1},{2,34},{34,2},{3,35},{35,3},{4,36},{36... | collective-permute-start | bytes 688136 | tf_op jit(solution)/shard_map/ppermute | solution.py:290
Sparse Core Ops, SparseCore 0:
  54.8 43.0 reduce-scatter.1
  100.7 49.7 all-gather.1

commit v12 on v10

--- a/solution.py
+++ b/solution.py
@@ -169,28 +169,27 @@
     store.wait()
 
 
-def back_parts(full, weights):
-    grad = dot_t(full[:, FFW : 2 * FFW], weights[1]) + dot_t(full[:, 2 * FFW :], weights[2])
-    return [grad, dot_t(full[:, :FFW], weights[0])]
-
-
 def back_kernel(full_hbm, gate_hbm, up_hbm, down_hbm, out_ref, full, weights, sems):
     size = full.shape[1] // N_Y
-    loads = copies_of(
-        [(w, weights.at[i]) for i, w in enumerate((down_hbm, gate_hbm, up_hbm))]
-        + [
-            (full_hbm.at[pl.ds((2 * y + half) * size, size)], full.at[half, pl.ds(y * size, size)])
-            for half in range(2)
-            for y in range(N_Y)
-        ],
-        sems,
-    )
+    pairs = [
+        (full_hbm.at[pl.ds((2 * y + half) * size, size)], full.at[half, pl.ds(y * size, size)])
+        for half in range(2)
+        for y in range(N_Y)
+    ]
+    inner = [(w, weights.at[i]) for i, w in enumerate((gate_hbm, up_hbm, down_hbm))]
+    loads = copies_of(pairs[:N_Y] + inner + pairs[N_Y:], sems)
     start(loads)
-    wait(loads[:3])
     parts = []
     for half in range(2):
-        wait(loads[3 + half * N_Y : 3 + (half + 1) * N_Y])
-        parts += back_parts(full.at[half], weights)
+        first = half * (N_Y + 3)
+        wait(loads[first : first + N_Y])
+        products = []
+        for i, column in enumerate((1, 2, 0)):
+            if half == 0:
+                loads[N_Y + i].wait()
+            rows = full[half, :, column * FFW : (column + 1) * FFW]
+            products.append(dot_t(rows, weights[i]))
+        parts += [products[0] + products[1], products[2]]
     result = jnp.concatenate(parts, axis=1)
     for q in range(MAIN):
         starts = [y * size + q * PIECE for y in range(N_Y)]

time: 194 us -> 194 us (level)
  no operation moved by 1% of the time
where the time goes in v12:
time: 194 us; the launch traced here: 193 us
  waiting for transfers between devices  76.8 us (40%)
  starting transfers between devices  49.5 us (26%)
  Pallas kernels  22.9 us (12%)
  blocking collectives  20.6 us (11%)
  between operations  14.4 us (7%)
  local copies, waits for them, and re-layouts  7.14 us (4%)
    all_to_all x3, starting transfers between devices, across(): return lax.all_to_all(quads, axis, split_axis=0, concat_axis=0, tiled=True)  35.8 us
    reduce_scatter x1, waiting for transfers between devices, body(): sums = lax.psum_scatter(parts, 'y', scatter_dimension=0, tiled=True)  35.1 us
    pallas_call x9, Pallas kernels, call(): pl.pallas_call(kernel, out_shape=out_shape, compiler_params=pltpu.Compile...  22.9 us
    all_to_all x3, waiting for transfers between devices, across(): return lax.all_to_all(quads, axis, split_axis=0, concat_axis=0, tiled=True)  21.8 us
    all_gather x1, blocking collectives, body(): full_last = lax.all_gather(shard_last, 'y', axis=0, tiled=True)  20.6 us
    all_gather x1, waiting for transfers between devices, body(): full = lax.all_gather(shard, ('y', 'core'), axis=0, tiled=True)  15.8 us
    ppermute x6, starting transfers between devices, swap(): return lax.ppermute(array, 'core', [(0, 1), (1, 0)])  13.6 us
    ppermute x6, waiting for transfers between devices, swap(): return lax.ppermute(array, 'core', [(0, 1), (1, 0)])  4.06 us
  transfers between devices with their start and end apart: 11, of which 7 were waited for; matrix products, arithmetic and copies ran while one was open for 3% of the time, Pallas kernels for 7%

profile of v12, /device:TPU:1, one launch (start us, length us, event | category | flops | bytes accessed | tf_op | source)
XLA Modules:
  0.0 192.8 jit_solution(4795623273105708516)
XLA Ops:
  7.2 2.9 %send_kernel.1 = bf16[64,2,4,896]{3,2,1,0:T(4,128)(2,1)} custom-call(s32[8,64]{1,0:T(8,128)} %bitcast.25, f32[8,64]{1,0:T(8,128)} %bitcast.27, bf16[64,224]{1,0:T(8,128)(2,1)} %tokens_hbm.1, bf16[64,224]{1,0:T(8,128)(2,1)} %cotangent_hbm.1), custom_call_target="tpu_custom_call" | custom-call | tf_op jit(solution)/shard_map/send_kernel/pallas_call | solution.py:259
  10.1 15.1 %all-to-all-start = ((bf16[64,2,4,896]{3,2,1,0:T(4,128)(2,1)}), bf16[64,2,4,896]{3,2,1,0:T(4,128)(2,1)}, u32[]{:S(2)}, u32[]{:S(2)}) async-start(bf16[64,2,4,896]{3,2,1,0:T(4,128)(2,1)} %send_kernel.1), calls=%async_computation | async-start | bytes 1835008 | tf_op jit(solution)/shard_map/all_to_all | solution.py:285
  25.3 2.3 %collective-permute-start = (bf16[224,1024]{1,0:T(8,128)(2,1)S(1)}, bf16[224,1024]{1,0:T(8,128)(2,1)S(1)}, u32[]{:S(2)}, u32[]{:S(2)}) collective-permute-start(bf16[224,1024]{1,0:T(8,128)(2,1)S(1)} %bitcast.41), channel_id=1, source_target_pairs={{0,32},{32,0},{1,33},{33,1},{2,34},{34,2},{3,35},{35,3},{4,36},{36... | collective-permute-start | bytes 1376264 | tf_op jit(solution)/shard_map/ppermute | solution.py:289
  27.7 2.0 %collective-permute-start.1 = (bf16[224,1024]{1,0:T(8,128)(2,1)S(1)}, bf16[224,1024]{1,0:T(8,128)(2,1)S(1)}, u32[]{:S(2)}, u32[]{:S(2)}) collective-permute-start(bf16[224,1024]{1,0:T(8,128)(2,1)S(1)} %bitcast.38), channel_id=1, source_target_pairs={{0,32},{32,0},{1,33},{33,1},{2,34},{34,2},{3,35},{35,3},{4,36},{36... | collective-permute-start | bytes 1376264 | tf_op jit(solution)/shard_map/ppermute | solution.py:289
  29.7 2.3 %collective-permute-start.2 = (bf16[224,1024]{1,0:T(8,128)(2,1)S(1)}, bf16[224,1024]{1,0:T(8,128)(2,1)S(1)}, u32[]{:S(2)}, u32[]{:S(2)}) collective-permute-start(bf16[224,1024]{1,0:T(8,128)(2,1)S(1)} %bitcast.35), channel_id=1, source_target_pairs={{0,32},{32,0},{1,33},{33,1},{2,34},{34,2},{3,35},{35,3},{4,36},{36... | collective-permute-start | bytes 1376264 | tf_op jit(solution)/shard_map/ppermute | solution.py:289
  32.2 1.2 collective-permute-done.2
  33.8 16.8 %all-to-all-done.quads = bf16[64,2,4,896]{3,2,1,0:T(4,128)(2,1)} async-done(((bf16[64,2,4,896]{3,2,1,0:T(4,128)(2,1)}), bf16[64,2,4,896]{3,2,1,0:T(4,128)(2,1)}, u32[]{:S(2)}, u32[]{:S(2)}) %all-to-all-start) | async-done | bytes 917536 | tf_op jit(solution)/shard_map/all_to_all | solution.py:285
  50.6 4.1 %sums_kernel.1 = (bf16[512,896]{1,0:T(8,128)(2,1)}, bf16[512,3072]{1,0:T(8,128)(2,1)}) custom-call(bf16[64,2,4,896]{3,2,1,0:T(4,128)(2,1)} %all-to-all-done.quads, bf16[512,1024]{1,0:T(8,128)(2,1)S(1)} %get-tuple-element.73.gate, bf16[512,1024]{1,0:T(8,128)(2,1)S(1)} %get-tuple-element.72.up, bf16[512,1024]{1,0:T(8,128)(2,1)S(1)} %get-tuple-element.71.down), custom_call_target="tpu_custom_call" | custom-call | tf_op jit(solution)/shard_map/sums_kernel/pallas_call | solution.py:259
  54.8 1.6 fusion
  56.9 1.9 collective-permute-start.3
  62.9 35.1 %reduce-scatter.2.cloned.1.call-done.sums_hbm = bf16[64,3072]{1,0:T(8,128)(2,1)} async-done(((bf16[512,3072]{1,0:T(8,128)(2,1)}), bf16[64,3072]{1,0:T(8,128)(2,1)}) %reduce-scatter.2.cloned.1.call-update) | async-done | bytes 393232 | tf_op jit(solution)/shard_map/reduce_scatter | solution.py:336
  98.1 1.8 shard_kernel.1
  99.9 20.6 %all_gather.7.full.refs_1_ = bf16[128,3072]{1,0:T(8,128)(2,1)S(1)} all-gather(bf16[16,3072]{1,0:T(8,128)(2,1)S(1)} %get-tuple-element.46), channel_id=1, replica_groups=mesh['y'=8,'core'=2,'expert'=32] {'y'}, dimensions={0}, use_global_device_ids=true | all-gather | bytes 884736 | tf_op jit(solution)/shard_map/all_gather | solution.py:369
  120.5 1.2 back_last_kernel.1
  123.3 10.8 %all-to-all-start.2 = ((bf16[32,1,4,896]{3,2,1,0:T(4,128)(2,1)}), bf16[32,1,4,896]{3,2,1,0:T(4,128)(2,1)S(1)}, u32[]{:S(2)}, u32[]{:S(2)}) async-start(bf16[32,1,4,896]{3,2,1,0:T(4,128)(2,1)} %copy-done.4), calls=%async_computation.3 | async-start | bytes 458752 | tf_op jit(solution)/shard_map/all_to_all | solution.py:285
  134.1 15.8 %all-gather.2.cloned.1.call-done.full_hbm.refs_0_ = bf16[768,3072]{1,0:T(8,128)(2,1)} async-done(((bf16[48,3072]{1,0:T(8,128)(2,1)}), bf16[768,3072]{1,0:T(8,128)(2,1)}) %all-gather.2.cloned.1.call-update) | async-done | bytes 4718608 | tf_op jit(solution)/shard_map/all_gather | solution.py:367
  149.9 5.1 %back_kernel.1 = bf16[32,3,4,896]{3,2,1,0:T(4,128)(2,1)} custom-call(bf16[768,3072]{1,0:T(8,128)(2,1)} %all-gather.2.cloned.1.call-done.full_hbm.refs_0_, bf16[224,1024]{1,0:T(8,128)(2,1)} %bitcast.40, bf16[224,1024]{1,0:T(8,128)(2,1)} %bitcast.37, bf16[224,1024]{1,0:T(8,128)(2,1)} %bitcast.34), custom_call_target="tpu_custom_call" | custom-call | tf_op jit(solution)/shard_map/back_kernel/pallas_call | solution.py:259
  155.1 9.9 %all-to-all-start.1 = ((bf16[32,3,4,896]{3,2,1,0:T(4,128)(2,1)}), bf16[32,3,4,896]{3,2,1,0:T(4,128)(2,1)S(1)}, u32[]{:S(2)}, u32[]{:S(2)}) async-start(bf16[32,3,4,896]{3,2,1,0:T(4,128)(2,1)} %back_kernel.1), calls=%async_computation.2 | async-start | bytes 1376256 | tf_op jit(solution)/shard_map/all_to_all | solution.py:285
  165.0 2.8 %collective-permute-start.4 = (bf16[128,3072]{1,0:T(8,128)(2,1)S(1)}, bf16[128,3072]{1,0:T(8,128)(2,1)S(1)}, u32[]{:S(2)}, u32[]{:S(2)}) collective-permute-start(bf16[128,3072]{1,0:T(8,128)(2,1)S(1)} %copy-done.1), channel_id=1, source_target_pairs={{0,32},{32,0},{1,33},{33,1},{2,34},{34,2},{3,35},{35,3},{4,36},{36... | collective-permute-start | bytes 2359304 | tf_op jit(solution)/shard_map/ppermute | solution.py:289
  167.8 1.7 collective-permute-done.4.refs_2_
  170.4 5.8 %grads_kernel.1 = (bf16[224,1024]{1,0:T(8,128)(2,1)}, bf16[224,1024]{1,0:T(8,128)(2,1)}, bf16[224,1024]{1,0:T(8,128)(2,1)}) custom-call(bf16[768,3072]{1,0:T(8,128)(2,1)} %all-gather.2.cloned.1.call-done.full_hbm.refs_0_, bf16[128,3072]{1,0:T(8,128)(2,1)} %copy-done, bf16[128,3072]{1,0:T(8,128)(2,1)} %copy-done.10, bf16[768,448]{1,0:T(8,128)(2,1)} %bitcast.29, ...), custom_call_target="tpu_custom_call" | custom-call | tf_op jit(solution)/shard_map/grads_kernel/pallas_call | solution.py:259
  176.4 2.3 %collective-permute-start.5 = (f32[64,896]{1,0:T(8,128)S(1)}, f32[64,896]{1,0:T(8,128)S(1)}, u32[]{:S(2)}, u32[]{:S(2)}) collective-permute-start(f32[64,896]{1,0:T(8,128)S(1)} %mix_last_kernel.1.own_ref), channel_id=1, source_target_pairs={{0,32},{32,0},{1,33},{33,1},{2,34},{34,2},{3,35},{35,3},{4,36},{36... | collective-permute-start | bytes 688136 | tf_op jit(solution)/shard_map/ppermute | solution.py:289
  179.8 5.0 %all-to-all-done.1.main_ref = bf16[32,3,4,896]{3,2,1,0:T(4,128)(2,1)S(1)} async-done(((bf16[32,3,4,896]{3,2,1,0:T(4,128)(2,1)}), bf16[32,3,4,896]{3,2,1,0:T(4,128)(2,1)S(1)}, u32[]{:S(2)}, u32[]{:S(2)}) %all-to-all-start.1) | async-done | bytes 688160 | tf_op jit(solution)/shard_map/all_to_all | solution.py:285
  184.8 1.2 mix_kernel.1
  (45 shorter events, 8.9 us)
Async XLA Ops:
  7.2 22.5 %copy-start.7 = (bf16[1,1024,224]{1,2,0:T(8,128)(2,1)S(1)}, bf16[1,1024,224]{1,2,0:T(8,128)(2,1)}, u32[]{:S(2)}) copy-start(bf16[1,1024,224]{1,2,0:T(8,128)(2,1)} %param.12) | copy-start | bytes 1376260
  7.2 20.5 %copy-start.8 = (bf16[1,224,1024]{2,1,0:T(8,128)(2,1)S(1)}, bf16[1,224,1024]{2,1,0:T(8,128)(2,1)}, u32[]{:S(2)}) copy-start(bf16[1,224,1024]{2,1,0:T(8,128)(2,1)} %param.11) | copy-start | bytes 1376260
  7.2 18.1 %copy-start.9 = (bf16[1,224,1024]{2,1,0:T(8,128)(2,1)S(1)}, bf16[1,224,1024]{2,1,0:T(8,128)(2,1)}, u32[]{:S(2)}) copy-start(bf16[1,224,1024]{2,1,0:T(8,128)(2,1)} %param.10) | copy-start | bytes 1376260
  10.1 40.5 %all-to-all-start = ((bf16[64,2,4,896]{3,2,1,0:T(4,128)(2,1)}), bf16[64,2,4,896]{3,2,1,0:T(4,128)(2,1)}, u32[]{:S(2)}, u32[]{:S(2)}) async-start(bf16[64,2,4,896]{3,2,1,0:T(4,128)(2,1)} %send_kernel.1), calls=%async_computation | async-start | bytes 1835008 | tf_op jit(solution)/shard_map/all_to_all | solution.py:285
  25.3 72.8 %reduce-scatter.2.cloned.1.call-start = ((), (), s32[]{:S(2)}) async-start(), calls=%async_computation.4 | async-start | bytes 3538944 | tf_op jit(solution)/shard_map/reduce_scatter | solution.py:336
  25.3 6.7 %collective-permute-start = (bf16[224,1024]{1,0:T(8,128)(2,1)S(1)}, bf16[224,1024]{1,0:T(8,128)(2,1)S(1)}, u32[]{:S(2)}, u32[]{:S(2)}) collective-permute-start(bf16[224,1024]{1,0:T(8,128)(2,1)S(1)} %bitcast.41), channel_id=1, source_target_pairs={{0,32},{32,0},{1,33},{33,1},{2,34},{34,2},{3,35},{35,3},{4,36},{36... | collective-permute-start | bytes 1376264 | tf_op jit(solution)/shard_map/ppermute | solution.py:289
  27.7 4.4 %collective-permute-start.1 = (bf16[224,1024]{1,0:T(8,128)(2,1)S(1)}, bf16[224,1024]{1,0:T(8,128)(2,1)S(1)}, u32[]{:S(2)}, u32[]{:S(2)}) collective-permute-start(bf16[224,1024]{1,0:T(8,128)(2,1)S(1)} %bitcast.38), channel_id=1, source_target_pairs={{0,32},{32,0},{1,33},{33,1},{2,34},{34,2},{3,35},{35,3},{4,36},{36... | collective-permute-start | bytes 1376264 | tf_op jit(solution)/shard_map/ppermute | solution.py:289
  29.7 3.8 %collective-permute-start.2 = (bf16[224,1024]{1,0:T(8,128)(2,1)S(1)}, bf16[224,1024]{1,0:T(8,128)(2,1)S(1)}, u32[]{:S(2)}, u32[]{:S(2)}) collective-permute-start(bf16[224,1024]{1,0:T(8,128)(2,1)S(1)} %bitcast.35), channel_id=1, source_target_pairs={{0,32},{32,0},{1,33},{33,1},{2,34},{34,2},{3,35},{35,3},{4,36},{36... | collective-permute-start | bytes 1376264 | tf_op jit(solution)/shard_map/ppermute | solution.py:289
  54.8 95.1 %all-gather.2.cloned.1.call-start = ((), (), s32[]{:S(2)}) async-start(), calls=%async_computation.5 | async-start | bytes 5013504 | tf_op jit(solution)/shard_map/all_gather | solution.py:367
  56.5 3.4 %copy-start.5 = (s32[64,8]{0,1:T(8,128)S(1)}, s32[64,8]{0,1:T(8,128)}, u32[]{:S(2)}) copy-start(s32[64,8]{0,1:T(8,128)} %param.8) | copy-start | bytes 6148
  56.5 3.4 %copy-start.6 = (f32[64,8]{0,1:T(8,128)S(1)}, f32[64,8]{0,1:T(8,128)}, u32[]{:S(2)}) copy-start(f32[64,8]{0,1:T(8,128)} %param.9) | copy-start | bytes 6148
  56.9 4.2 %collective-permute-start.3 = (bf16[512,448]{1,0:T(8,128)(2,1)S(1)}, bf16[512,448]{1,0:T(8,128)(2,1)S(1)}, u32[]{:S(2)}, u32[]{:S(2)}) collective-permute-start(bf16[512,448]{1,0:T(8,128)(2,1)S(1)} %maximum_select_fusion.1), channel_id=1, source_target_pairs={{0,32},{32,0},{1,33},{33,1},{2,34},{34,2},{3,35},{35,3},{4,36},{36... | collective-permute-start | bytes 1376264 | tf_op jit(solution)/shard_map/ppermute | solution.py:289
  60.4 0.7 copy-start.2
  121.7 0.9 copy-start
  122.6 0.7 copy-start.4
  123.3 31.7 %all-to-all-start.2 = ((bf16[32,1,4,896]{3,2,1,0:T(4,128)(2,1)}), bf16[32,1,4,896]{3,2,1,0:T(4,128)(2,1)S(1)}, u32[]{:S(2)}, u32[]{:S(2)}) async-start(bf16[32,1,4,896]{3,2,1,0:T(4,128)(2,1)} %copy-done.4), calls=%async_computation.3 | async-start | bytes 458752 | tf_op jit(solution)/shard_map/all_to_all | solution.py:285
  134.1 30.9 %copy-start.1 = (bf16[128,3072]{1,0:T(8,128)(2,1)S(1)}, bf16[128,3072]{1,0:T(8,128)(2,1)}, u32[]{:S(2)}) copy-start(bf16[128,3072]{1,0:T(8,128)(2,1)} %copy-done) | copy-start | bytes 2359300
  155.1 29.8 %all-to-all-start.1 = ((bf16[32,3,4,896]{3,2,1,0:T(4,128)(2,1)}), bf16[32,3,4,896]{3,2,1,0:T(4,128)(2,1)S(1)}, u32[]{:S(2)}, u32[]{:S(2)}) async-start(bf16[32,3,4,896]{3,2,1,0:T(4,128)(2,1)} %back_kernel.1), calls=%async_computation.2 | async-start | bytes 1376256 | tf_op jit(solution)/shard_map/all_to_all | solution.py:285
  165.0 11.2 %copy-start.3 = (bf16[2,512,64]{2,1,0:T(8,128)(2,1)S(1)}, bf16[2,512,64]{2,1,0:T(8,128)(2,1)}, u32[]{:S(2)}) copy-start(bf16[2,512,64]{2,1,0:T(8,128)(2,1)} %copy-done.2) | copy-start | bytes 393220
  165.0 4.5 %collective-permute-start.4 = (bf16[128,3072]{1,0:T(8,128)(2,1)S(1)}, bf16[128,3072]{1,0:T(8,128)(2,1)S(1)}, u32[]{:S(2)}, u32[]{:S(2)}) collective-permute-start(bf16[128,3072]{1,0:T(8,128)(2,1)S(1)} %copy-done.1), channel_id=1, source_target_pairs={{0,32},{32,0},{1,33},{33,1},{2,34},{34,2},{3,35},{35,3},{4,36},{36... | collective-permute-start | bytes 2359304 | tf_op jit(solution)/shard_map/ppermute | solution.py:289
  169.5 0.9 copy-start.10
  176.4 3.4 %collective-permute-start.5 = (f32[64,896]{1,0:T(8,128)S(1)}, f32[64,896]{1,0:T(8,128)S(1)}, u32[]{:S(2)}, u32[]{:S(2)}) collective-permute-start(f32[64,896]{1,0:T(8,128)S(1)} %mix_last_kernel.1.own_ref), channel_id=1, source_target_pairs={{0,32},{32,0},{1,33},{33,1},{2,34},{34,2},{3,35},{35,3},{4,36},{36... | collective-permute-start | bytes 688136 | tf_op jit(solution)/shard_map/ppermute | solution.py:289
Sparse Core Ops, SparseCore 0:
  54.9 43.0 reduce-scatter.1
  100.7 49.1 all-gather.1
